TPU v7x, 32 devices: a whole 2x2x4 slice. The times are simulated.
32 devices in a mesh: wide: 4 (over y, core), narrow: 8 (over z, x).
Axes of the slice: x: 2, y: 2, z: 4, core: 2. Of those that a mesh axis runs over, the one named last changes fastest.
Arguments:
- tokens_in: bfloat16 [4096, 2048], P(('wide', 'narrow')), may hold values from -9 to 9
- query_weight: bfloat16 [2048, 2048], P(None, 'narrow'), may hold values from -0.125 to 0.125
- key_weight: bfloat16 [2048, 2048], P(None, 'narrow'), may hold values from -0.125 to 0.125
- value_weight: bfloat16 [2048, 2048], P(None, 'narrow'), may hold values from -0.125 to 0.125
- gate_weight: bfloat16 [2048, 2048], P(None, 'narrow'), may hold values from -0.125 to 0.125
- mixer_weight: bfloat16 [2048, 2048], P('narrow'), may hold values from -0.125 to 0.125
- first_weight: bfloat16 [2048, 5632], P(None, 'narrow'), may hold values from -0.125 to 0.125
- second_weight: bfloat16 [2048, 5632], P(None, 'narrow'), may hold values from -0.125 to 0.125
- down_weight: bfloat16 [5632, 2048], P('narrow'), may hold values from -0.078125 to 0.078125
- doc_lengths: int32 [4, 4], P('wide'), may hold values from 1 to 512, 1024 in all within a row
- head_decay: float32 [16], P('narrow'), may hold values from 0.00024414062 to 0.04
- out_grad: bfloat16 [4096, 2048], P(('wide', 'narrow')), may hold values from -6 to 6
Outputs:
- output: bfloat16 [4096, 2048], P(('wide', 'narrow'))
- input_grad: float32 [4096, 2048], P(('wide', 'narrow'))
- query_grad: float32 [2048, 2048], P(None, 'narrow')
- key_grad: float32 [2048, 2048], P(None, 'narrow')
- value_grad: float32 [2048, 2048], P(None, 'narrow')
- gate_grad: float32 [2048, 2048], P(None, 'narrow')
- mixer_grad: float32 [2048, 2048], P('narrow')
- first_grad: float32 [2048, 5632], P(None, 'narrow')
- second_grad: float32 [2048, 5632], P(None, 'narrow')
- down_grad: float32 [5632, 2048], P('narrow')
- stream_rms: float32 [3], replicated
All inputs are finite; a program needn't handle non-finite values.
Results may differ from a plain program's by a relative error of at most 0.014.
Values may be sent and summed in bfloat16 or wider, within the bound.
No kernel may reach another device: no remote copies, remote signals or barrier semaphores. Data moves between devices by JAX's collectives and lax.ppermute only.
A program may use at most 256 MiB of HBM per device.

v0:
```python
import jax
import jax.numpy as jnp
from jax import lax
from jax.sharding import PartitionSpec as P

D = 2048
HEAD_DIM = 128
NDOC = 4


EPS = 1e-06
HIGH = lax.Precision.HIGHEST
FIRST_AXIS = (((0,), (0,)), ((), ()))
SECOND_AXIS = (((1,), (1,)), ((), ()))


def normalize(values):
    return values * lax.rsqrt(jnp.mean(values * values, axis=-1, keepdims=True) + EPS)


def norm_grad(values, grad_in):
    inverse = lax.rsqrt(jnp.mean(values * values, axis=-1, keepdims=True) + EPS)
    normed = values * inverse
    return inverse * (grad_in - normed * jnp.mean(grad_in * normed, axis=-1, keepdims=True))


def silu_grad(before):
    sigmoid = jax.nn.sigmoid(before)
    return sigmoid * (1.0 + before * (1.0 - sigmoid))


def segment_ids(lengths_row, total):
    ends = jnp.cumsum(lengths_row)[:-1]
    positions = jnp.arange(total, dtype=jnp.int32)
    return jnp.sum((positions[:, None] >= ends[None, :]).astype(jnp.int32), axis=1)


def block_factors(segment_block, earlier_segment, rate):
    size = segment_block.shape[0]
    places = jnp.arange(size, dtype=jnp.float32)
    offset = places[:, None] - places[None, :]
    same = jnp.logical_and(segment_block[:, None] == segment_block[None, :], offset >= 0)
    decay = jnp.exp(-rate[:, None, None] * jnp.maximum(offset, 0.0)[None]) * same[None].astype(
        jnp.float32
    )
    inner = jnp.exp(-rate[None, :] * (places[:, None] + 1.0)) * (segment_block == earlier_segment)[
        :, None
    ].astype(jnp.float32)
    carried = jnp.exp(-rate[None, :] * (size - 1.0 - places)[:, None]) * (
        segment_block == segment_block[-1]
    )[:, None].astype(jnp.float32)
    keeping = jnp.exp(-rate * size) * (segment_block[-1] == earlier_segment).astype(jnp.float32)
    return (decay, inner, carried, keeping)


def block_layout(segments, total):
    size = min(512, total)
    count = total // size
    segment_blocks = segments.reshape(count, size)
    earlier = jnp.concatenate([jnp.full((1,), -1, dtype=jnp.int32), segment_blocks[:-1, -1]])
    return (size, count, segment_blocks, earlier)


def attention_forward(query_act, key_act, value_act, segments, rate):
    total = query_act.shape[0]
    heads = rate.shape[0]
    size, count, segment_blocks, earlier = block_layout(segments, total)
    shaped = (count, size, heads, HEAD_DIM)

    def advance(state, inputs):
        query_block, key_block, value_block, segment_block, earlier_segment = inputs
        decay, inner, carried, keeping = block_factors(segment_block, earlier_segment, rate)
        scores = jnp.einsum(
            "ihd,jhd->hij", query_block, key_block, preferred_element_type=jnp.float32
        )
        weights = (scores * decay).astype(jnp.bfloat16)
        intra = jnp.einsum("hij,jhd->ihd", weights, value_block, preferred_element_type=jnp.float32)
        inter = inner[:, :, None] * jnp.einsum(
            "ihd,hde->ihe", query_block.astype(jnp.float32), state, precision=HIGH
        )
        state_next = keeping[:, None, None] * state + jnp.einsum(
            "jhd,jhe->hde",
            key_block.astype(jnp.float32) * carried[:, :, None],
            value_block.astype(jnp.float32),
            precision=HIGH,
        )
        return (state_next, (intra + inter, state))

    start_state = jnp.zeros((heads, HEAD_DIM, HEAD_DIM), jnp.float32)
    final_state, (outputs, states) = lax.scan(
        advance,
        start_state,
        (
            query_act.reshape(shaped),
            key_act.reshape(shaped),
            value_act.reshape(shaped),
            segment_blocks,
            earlier,
        ),
    )
    return (outputs.reshape(total, heads * HEAD_DIM), states)


def attention_backward(query_act, key_act, value_act, segments, rate, mixed_g, states):
    total = query_act.shape[0]
    heads = rate.shape[0]
    size, count, segment_blocks, earlier = block_layout(segments, total)
    shaped = (count, size, heads, HEAD_DIM)

    def retreat(later, inputs):
        query_block, key_block, value_block, segment_block, earlier_segment, grad_block, state = (
            inputs
        )
        decay, inner, carried, keeping = block_factors(segment_block, earlier_segment, rate)
        scores = jnp.einsum(
            "ihd,jhd->hij", query_block, key_block, preferred_element_type=jnp.float32
        )
        weights = (scores * decay).astype(jnp.bfloat16)
        value_part = jnp.einsum(
            "hij,ihd->jhd", weights, grad_block, preferred_element_type=jnp.float32
        )
        weight_part = jnp.einsum(
            "ihd,jhd->hij", grad_block, value_block, preferred_element_type=jnp.float32
        )
        score_part = (weight_part * decay).astype(jnp.bfloat16)
        grad_wide = grad_block.astype(jnp.float32)
        query_part = jnp.einsum(
            "hij,jhd->ihd", score_part, key_block, preferred_element_type=jnp.float32
        ) + inner[:, :, None] * jnp.einsum("ihe,hde->ihd", grad_wide, state, precision=HIGH)
        key_part = jnp.einsum(
            "hij,ihd->jhd", score_part, query_block, preferred_element_type=jnp.float32
        ) + carried[:, :, None] * jnp.einsum(
            "jhe,hde->jhd", value_block.astype(jnp.float32), later, precision=HIGH
        )
        value_part = value_part + carried[:, :, None] * jnp.einsum(
            "jhd,hde->jhe", key_block.astype(jnp.float32), later, precision=HIGH
        )
        sooner = (
            jnp.einsum(
                "ihd,ihe->hde",
                query_block.astype(jnp.float32) * inner[:, :, None],
                grad_wide,
                precision=HIGH,
            )
            + keeping[:, None, None] * later
        )
        return (sooner, (query_part, key_part, value_part))

    start_state = jnp.zeros((heads, HEAD_DIM, HEAD_DIM), jnp.float32)
    first_state, (query_parts, key_parts, value_parts) = lax.scan(
        retreat,
        start_state,
        (
            query_act.reshape(shaped),
            key_act.reshape(shaped),
            value_act.reshape(shaped),
            segment_blocks,
            earlier,
            mixed_g.reshape(shaped),
            states,
        ),
        reverse=True,
    )
    flat = (total, heads * HEAD_DIM)
    return (query_parts.reshape(flat), key_parts.reshape(flat), value_parts.reshape(flat))


def local(
    tokens_in,
    query_weight,
    key_weight,
    value_weight,
    gate_weight,
    mixer_weight,
    first_weight,
    second_weight,
    down_weight,
    doc_lengths,
    head_decay,
    out_grad,
):
    own_rows = tokens_in.shape[0]
    total = own_rows * lax.axis_size("narrow")
    start_row = lax.axis_index("narrow") * own_rows
    segments = segment_ids(doc_lengths[0], total)
    own_segments = lax.dynamic_slice_in_dim(segments, start_row, own_rows)
    valid = (own_segments < NDOC - 1).astype(jnp.float32)
    tokens_wide = tokens_in.astype(jnp.float32)
    head_width = query_weight.shape[1]
    entry_weight = jnp.concatenate([query_weight, key_weight, value_weight, gate_weight], axis=1)
    normed_all = lax.all_gather(
        normalize(tokens_wide).astype(jnp.bfloat16), "narrow", axis=0, tiled=True
    )
    projected = jnp.dot(normed_all, entry_weight, preferred_element_type=jnp.float32)
    query_pre = projected[:, :head_width]
    key_pre = projected[:, head_width : 2 * head_width]
    value_act = projected[:, 2 * head_width : 3 * head_width].astype(jnp.bfloat16)
    gate_act = projected[:, 3 * head_width :]
    query_act = jax.nn.silu(query_pre).astype(jnp.bfloat16)
    key_act = jax.nn.silu(key_pre).astype(jnp.bfloat16)
    mixed, states = attention_forward(query_act, key_act, value_act, segments, head_decay)
    square_sums = lax.psum(jnp.sum(mixed * mixed, axis=1), "narrow")
    inverse = lax.rsqrt(square_sums / D + EPS)[:, None]
    unit = mixed * inverse
    scaled = (unit * gate_act).astype(jnp.bfloat16)
    attn_own = lax.psum_scatter(
        jnp.dot(scaled, mixer_weight, preferred_element_type=jnp.float32),
        "narrow",
        scatter_dimension=0,
        tiled=True,
    )
    hidden_own = tokens_wide + attn_own
    normed2_all = lax.all_gather(
        normalize(hidden_own).astype(jnp.bfloat16), "narrow", axis=0, tiled=True
    )
    inner_weight = jnp.concatenate([first_weight, second_weight], axis=1)
    unit_width = first_weight.shape[1]
    ffn_hidden = jnp.dot(normed2_all, inner_weight, preferred_element_type=jnp.float32)
    first_act = ffn_hidden[:, :unit_width]
    second_act = ffn_hidden[:, unit_width:]
    product = (first_act * second_act).astype(jnp.bfloat16)
    ffn_own = lax.psum_scatter(
        jnp.dot(product, down_weight, preferred_element_type=jnp.float32),
        "narrow",
        scatter_dimension=0,
        tiled=True,
    )
    output = (hidden_own + ffn_own).astype(jnp.bfloat16)
    totals = lax.psum(
        (
            jnp.sum(valid * jnp.sum(tokens_wide * tokens_wide, axis=1)),
            jnp.sum(valid * jnp.sum(attn_own * attn_own, axis=1)),
            jnp.sum(valid * jnp.sum(ffn_own * ffn_own, axis=1)),
            jnp.sum(valid),
        ),
        ("wide", "narrow"),
    )
    stream_rms = jnp.sqrt(jnp.stack([totals[0], totals[1], totals[2]]) / (totals[3] * D))
    grad_all = lax.all_gather(out_grad, "narrow", axis=0, tiled=True)
    product_g = lax.dot_general(
        grad_all, down_weight, SECOND_AXIS, preferred_element_type=jnp.float32
    )
    inner_g = jnp.concatenate(
        [
            (product_g * second_act).astype(jnp.bfloat16),
            (product_g * first_act).astype(jnp.bfloat16),
        ],
        axis=1,
    )
    down_wgrad = lax.dot_general(product, grad_all, FIRST_AXIS, preferred_element_type=jnp.float32)
    inner_wgrad = lax.dot_general(
        normed2_all, inner_g, FIRST_AXIS, preferred_element_type=jnp.float32
    )
    normed2_g = lax.psum_scatter(
        lax.dot_general(inner_g, inner_weight, SECOND_AXIS, preferred_element_type=jnp.float32),
        "narrow",
        scatter_dimension=0,
        tiled=True,
    )
    hidden_g = out_grad.astype(jnp.float32) + norm_grad(hidden_own, normed2_g)
    resid_all = lax.all_gather(hidden_g.astype(jnp.bfloat16), "narrow", axis=0, tiled=True)
    mixer_wgrad = lax.dot_general(scaled, resid_all, FIRST_AXIS, preferred_element_type=jnp.float32)
    scaled_g = lax.dot_general(
        resid_all, mixer_weight, SECOND_AXIS, preferred_element_type=jnp.float32
    )
    unit_g = scaled_g * gate_act
    gate_g = (scaled_g * unit).astype(jnp.bfloat16)
    inner_sums = lax.psum(jnp.sum(unit_g * unit, axis=1), "narrow")
    mixed_g = (inverse * (unit_g - unit * (inner_sums / D)[:, None])).astype(jnp.bfloat16)
    query_g, key_g, value_g = attention_backward(
        query_act, key_act, value_act, segments, head_decay, mixed_g, states
    )
    entry_g = jnp.concatenate(
        [
            (query_g * silu_grad(query_pre)).astype(jnp.bfloat16),
            (key_g * silu_grad(key_pre)).astype(jnp.bfloat16),
            value_g.astype(jnp.bfloat16),
            gate_g,
        ],
        axis=1,
    )
    entry_wgrad = lax.dot_general(
        normed_all, entry_g, FIRST_AXIS, preferred_element_type=jnp.float32
    )
    normed_g = lax.psum_scatter(
        lax.dot_general(entry_g, entry_weight, SECOND_AXIS, preferred_element_type=jnp.float32),
        "narrow",
        scatter_dimension=0,
        tiled=True,
    )
    input_grad = hidden_g + norm_grad(tokens_wide, normed_g)
    summed = lax.psum((entry_wgrad, mixer_wgrad, inner_wgrad, down_wgrad), "wide")
    entry_sum = summed[0]
    inner_sum = summed[2]
    return (
        output,
        input_grad,
        entry_sum[:, :head_width],
        entry_sum[:, head_width : 2 * head_width],
        entry_sum[:, 2 * head_width : 3 * head_width],
        entry_sum[:, 3 * head_width :],
        summed[1],
        inner_sum[:, :unit_width],
        inner_sum[:, unit_width:],
        summed[3],
        stream_rms,
    )


def solution(mesh):
    return jax.shard_map(
        local,
        mesh=mesh,
        in_specs=(
            P(("wide", "narrow"), None),
            P(None, "narrow"),
            P(None, "narrow"),
            P(None, "narrow"),
            P(None, "narrow"),
            P("narrow", None),
            P(None, "narrow"),
            P(None, "narrow"),
            P("narrow", None),
            P("wide", None),
            P("narrow"),
            P(("wide", "narrow"), None),
        ),
        out_specs=(
            P(("wide", "narrow"), None),
            P(("wide", "narrow"), None),
            P(None, "narrow"),
            P(None, "narrow"),
            P(None, "narrow"),
            P(None, "narrow"),
            P("narrow", None),
            P(None, "narrow"),
            P(None, "narrow"),
            P("narrow", None),
            P(),
        ),
        check_vma=False,
    )
```

profile of v0, /device:TPU:0, one launch (start us, length us, event | category | flops | bytes accessed | tf_op | source)
XLA Modules:
  0.0 1686.4 jit_solution(3060295013114730570)
XLA Ops:
  16.0 2.3 constant_dynamic-update-slice_fusion.3
  22.6 65.5 %all-gather.5.cloned.1.call-done = bf16[1024,2048]{1,0:T(8,128)(2,1)} async-done(((bf16[128,2048]{1,0:T(8,128)(2,1)}), bf16[1024,2048]{1,0:T(8,128)(2,1)}) %all-gather.5.cloned.1.call-update) | async-done | bytes 4194320 | tf_op jit(solution)/shard_map/all_gather | solution.py:191
  88.1 7.6 fusion.129
  109.4 30.3 %while.42 = (s32[]{:T(128)}, f32[2,128,128]{2,1,0:T(8,128)S(1)}, f32[2,512,2,128]{1,3,2,0:T(8,128)}, f32[2,2,128,128]{3,2,1,0:T(8,128)}, f32[2,1,1]{0,2,1:T(1,12...) while((s32[]{:T(128)}, f32[2,128,128]{2,1,0:T(8,128)S(1)}, ...), condition=%wide.region_4.5_spmd.clone.clone, body=%wide.region_3.4_spmd.clone.sunk.clone | while | flops 675716096 | bytes 8041743 | solution.py:90
  117.7 3.4 fusion.239
  132.9 3.4 fusion.239
  144.2 18.7 %psum.70 = f32[1024]{0:T(1024)S(1)} all-reduce(f32[1024]{0:T(1024)S(1)} %bitcast.344), channel_id=1, replica_groups=mesh['wide'=4,'narrow'=8] {'narrow'}, use_global_device_ids=true, to_apply=%region_6.7 | all-reduce | flops 1024 | bytes 8192 | tf_op jit(solution)/shard_map/psum | solution.py:202
  165.5 5.8 fusion.130
  171.3 146.3 %reduce-scatter.5.cloned.1.call-done = f32[128,2048]{1,0:T(8,128)} async-done(((f32[1024,2048]{1,0:T(8,128)}), f32[128,2048]{1,0:T(8,128)}) %reduce-scatter.5.cloned.1.call-update) | async-done | bytes 1048592 | tf_op jit(solution)/shard_map/reduce_scatter | solution.py:206
  319.3 2.3 multiply_convert_fusion.13
  322.5 3.9 constant_dynamic-update-slice_fusion.5
  328.2 65.9 %all-gather.7.cloned.1.call-done = bf16[1024,2048]{1,0:T(8,128)(2,1)} async-done(((bf16[128,2048]{1,0:T(8,128)(2,1)}), bf16[1024,2048]{1,0:T(8,128)(2,1)}) %all-gather.7.cloned.1.call-update) | async-done | bytes 4194320 | tf_op jit(solution)/shard_map/all_gather | solution.py:213
  394.1 11.8 fusion.131
  405.9 62.1 %all-gather.9.cloned.1.call-done = bf16[1024,2048]{1,0:T(8,128)(2,1)} async-done(((bf16[128,2048]{1,0:T(8,128)(2,1)}), bf16[1024,2048]{1,0:T(8,128)(2,1)}) %all-gather.9.cloned.1.call-update) | async-done | bytes 4194320 | tf_op jit(solution)/shard_map/all_gather | solution.py:239
  468.0 8.7 multiply_convert_fusion.4
  478.4 10.9 fusion.110
  489.3 147.4 %reduce-scatter.9.cloned.1.call-done = f32[128,2048]{1,0:T(8,128)} async-done(((f32[1024,2048]{1,0:T(8,128)}), f32[128,2048]{1,0:T(8,128)}) %reduce-scatter.9.cloned.1.call-update) | async-done | bytes 1048592 | tf_op jit(solution)/shard_map/reduce_scatter | solution.py:254
  636.7 2.5 multiply_reduce_fusion.1
  639.2 3.0 fusion.126
  645.6 8.6 fusion.134
  654.2 9.8 fusion.109
  664.0 50.8 %all-gather.11.cloned.1.call-done = bf16[1024,2048]{1,0:T(8,128)(2,1)} async-done(((bf16[128,2048]{1,0:T(8,128)(2,1)}), bf16[1024,2048]{1,0:T(8,128)(2,1)}) %all-gather.11.cloned.1.call-update) | async-done | bytes 4194320 | tf_op jit(solution)/shard_map/all_gather | solution.py:261
  714.8 5.4 multiply_reduce_fusion.2
  720.2 18.8 %psum.71 = f32[1024]{0:T(1024)S(1)} all-reduce(f32[1024]{0:T(1024)S(1)} %get-tuple-element.722), channel_id=1, replica_groups=mesh['wide'=4,'narrow'=8] {'narrow'}, use_global_device_ids=true, to_apply=%region_13.14 | all-reduce | flops 1024 | bytes 8192 | tf_op jit(solution)/shard_map/psum | solution.py:268
  739.0 3.2 multiply_convert_fusion.9
  749.0 85.8 %while.43 = (s32[]{:T(128)}, f32[2,128,128]{2,1,0:T(8,128)S(1)}, f32[2,512,2,128]{1,0,3,2:T(2,128)}, f32[2,512,2,128]{1,0,3,2:T(2,128)}, bf16[2,512,2,128]{1,3,2...) while((s32[]{:T(128)}, f32[2,128,128]{2,1,0:T(8,128)S(1)}, ...), condition=%wide.region_15.16_spmd.clone.clone, body=%wide.region_14.15_spmd.clone.sunk.clone | while | flops 1483643904 | bytes 36887488 | solution.py:150
  759.2 10.4 dynamic_update_slice.66
  774.1 10.4 dynamic_update_slice.65
  785.7 3.4 fusion.264
  802.2 10.4 dynamic_update_slice.66
  817.0 10.4 dynamic_update_slice.65
  828.6 3.4 fusion.264
  840.5 2.6 fusion.133
  843.7 8.9 fusion.119
  852.7 10.5 fusion.120
  863.4 7.4 fusion.132
  870.8 446.6 %all-reduce.4.cloned.1.call-done = (f32[2048,1024]{1,0:T(8,128)}, f32[256,2048]{1,0:T(8,128)}, f32[2048,1408]{1,0:T(8,128)}, f32[704,2048]{1,0:T(8,128)}) async-done(((f32[2048,1024]{1,0:T(8,128)}, f32[256,2048]{1,0:T(8,128)}, f32[2048,1408]{1,0:T(8,128)}, f32[704,2048]{1,0:T(8,128)}), (f32[2048,1024]{1,0:T(8,128)}, f32[256,2048]{1,0:T(8,128)}, f32[2048,1408]{1,0:T(8,128)}, ...) | async-done | bytes 27787280 | tf_op jit(solution)/shard_map/psum | solution.py:292
  1317.3 11.1 fusion.127
  1328.4 6.4 copy.63
  1334.8 6.4 copy.64
  1341.2 7.1 fusion.128
  1348.3 121.9 %reduce-scatter.11.cloned.1.call-done = f32[128,2048]{1,0:T(8,128)} async-done(((f32[1024,2048]{1,0:T(8,128)}), f32[128,2048]{1,0:T(8,128)}) %reduce-scatter.11.cloned.1.call-update) | async-done | bytes 1048592 | tf_op jit(solution)/shard_map/reduce_scatter | solution.py:285
  1471.8 150.6 %reduce-scatter.7.cloned.1.call-done = f32[128,2048]{1,0:T(8,128)} async-done(((f32[1024,2048]{1,0:T(8,128)}), f32[128,2048]{1,0:T(8,128)}) %reduce-scatter.7.cloned.1.call-update) | async-done | bytes 1048592 | tf_op jit(solution)/shard_map/reduce_scatter | solution.py:222
  1622.4 4.0 fusion.117
  1627.9 39.5 %all-reduce = (f32[1]{0:T(128)}, f32[1]{0:T(128)}, f32[1]{0:T(128)}, f32[]{:T(128)}) all-reduce(f32[1]{0:T(128)} %bitcast.7, f32[1]{0:T(128)} %bitcast.6, f32[1]{0:T(128)} %bitcast.5, f32[]{:T(128)} %get-tuple-element.628), channel_id=1, replica_groups=mesh['wide'=4,'narrow'=8] {'wide','narrow'}, use_global_device_ids=true, to_apply=%region_29.30 | all-reduce | flops 4 | bytes 32 | tf_op jit(solution)/shard_map/psum | solution.py:229
  1668.0 2.6 fusion.121
  1670.6 3.1 copy.139
  1673.7 5.9 copy.140
  (210 shorter events, 114.7 us)
Async XLA Ops:
  7.2 460.9 %copy-start = (bf16[704,2048]{1,0:T(8,128)(2,1)S(1)}, bf16[704,2048]{1,0:T(8,128)(2,1)}, u32[]{:S(2)}) copy-start(bf16[704,2048]{1,0:T(8,128)(2,1)} %param.24) | copy-start | bytes 8650756
  7.2 80.9 %all-gather.5.cloned.1.call-start = ((), (), s32[]{:S(2)}) async-start(), calls=%async_computation.4 | async-start | bytes 4718592 | tf_op jit(solution)/shard_map/all_gather | solution.py:191
  11.8 305.9 %reduce-scatter.5.cloned.1.call-start = ((), (), s32[]{:S(2)}) async-start(), calls=%async_computation.5 | async-start | bytes 9437184 | tf_op jit(solution)/shard_map/reduce_scatter | solution.py:206
  12.8 9.8 copy-start.18
  12.8 7.7 copy-start.11
  12.8 8.7 copy-start.12
  95.7 2.1 copy-start.6
  115.3 7.1 copy-start.16
  130.5 7.1 copy-start.16
  164.7 0.8 copy-start.9
  171.3 222.8 %all-gather.7.cloned.1.call-start = ((), (), s32[]{:S(2)}) async-start(), calls=%async_computation.6 | async-start | bytes 4718592 | tf_op jit(solution)/shard_map/all_gather | solution.py:213
  319.3 319.9 %copy-start.19 = (f32[128]{0:T(128)}, f32[128]{0:T(128)S(1)}, u32[]{:S(2)}) copy-start(f32[128]{0:T(128)S(1)} %add_rsqrt_fusion.1) | copy-start | bytes 1540
  321.6 146.4 %all-gather.9.cloned.1.call-start = ((), (), s32[]{:S(2)}) async-start(), calls=%async_computation.8 | async-start | bytes 4718592 | tf_op jit(solution)/shard_map/all_gather | solution.py:239
  322.2 314.5 %reduce-scatter.9.cloned.1.call-start = ((), (), s32[]{:S(2)}) async-start(), calls=%async_computation.9 | async-start | bytes 9437184 | tf_op jit(solution)/shard_map/reduce_scatter | solution.py:254
  322.5 3.9 copy-start.8
  476.7 1.1 copy-start.31
  476.7 1.7 copy-start.33
  489.3 225.5 %all-gather.11.cloned.1.call-start = ((), (), s32[]{:S(2)}) async-start(), calls=%async_computation.10 | async-start | bytes 4718592 | tf_op jit(solution)/shard_map/all_gather | solution.py:261
  639.2 14.9 copy-start.23
  642.3 675.1 %all-reduce.4.cloned.1.call-start = ((), (), s32[]{:S(2)}) async-start(), calls=%async_computation.12 | async-start | bytes 55574528 | tf_op jit(solution)/shard_map/psum | solution.py:292
  645.6 8.6 copy-start.30
  645.6 8.6 copy-start.32
  645.6 8.6 copy-start.34
  752.8 4.8 copy-start.4
  754.4 3.5 copy-start.2
  754.6 4.6 copy-start.3
  756.6 1.0 copy-start.1
  757.9 27.8 %copy-start.17 = (f32[2,1,1]{0,2,1:T(1,128)S(1)}, f32[2,1,1]{0,2,1:T(1,128)}, u32[]{:S(2)}) copy-start(f32[2,1,1]{0,2,1:T(1,128)} %get-tuple-element.1041) | copy-start | bytes 28 | tf_op jit(solution)/shard_map/while
  795.7 4.8 copy-start.4
  797.3 3.5 copy-start.2
  797.5 4.6 copy-start.3
  799.5 1.0 copy-start.1
  800.8 27.8 %copy-start.17 = (f32[2,1,1]{0,2,1:T(1,128)S(1)}, f32[2,1,1]{0,2,1:T(1,128)}, u32[]{:S(2)}) copy-start(f32[2,1,1]{0,2,1:T(1,128)} %get-tuple-element.1041) | copy-start | bytes 28 | tf_op jit(solution)/shard_map/while
  834.8 4.9 copy-start.7
  837.8 2.6 copy-start.10
  837.8 2.6 copy-start.29
  839.6 3.5 copy-start.14
  840.5 2.6 copy-start.13
  840.5 2.6 copy-start.15
  840.5 3.3 copy-start.28
  852.7 617.6 %reduce-scatter.11.cloned.1.call-start = ((), (), s32[]{:S(2)}) async-start(), calls=%async_computation.11 | async-start | bytes 9437184 | tf_op jit(solution)/shard_map/reduce_scatter | solution.py:285
  863.3 759.1 %reduce-scatter.7.cloned.1.call-start = ((), (), s32[]{:S(2)}) async-start(), calls=%async_computation.7 | async-start | bytes 9437184 | tf_op jit(solution)/shard_map/reduce_scatter | solution.py:222
  1341.2 129.0 %copy-start.5 = (bf16[128,2048]{1,0:T(8,128)(2,1)S(1)}, bf16[128,2048]{1,0:T(8,128)(2,1)}, u32[]{:S(2)}) copy-start(bf16[128,2048]{1,0:T(8,128)(2,1)} %param.16) | copy-start | bytes 1572868
  1341.2 129.0 %copy-start.22 = (f32[128]{0:T(128)S(1)}, f32[128]{0:T(128)}, u32[]{:S(2)}) copy-start(f32[128]{0:T(128)} %copy-done.21) | copy-start | bytes 1540
  1341.2 281.2 %copy-start.20 = (f32[128]{0:T(128)S(1)}, f32[128]{0:T(128)}, u32[]{:S(2)}) copy-start(f32[128]{0:T(128)} %copy-done.19) | copy-start | bytes 1540
  1341.2 281.2 %copy-start.24 = (f32[128]{0:T(128)S(1)}, f32[128]{0:T(128)}, u32[]{:S(2)}) copy-start(f32[128]{0:T(128)} %copy-done.23) | copy-start | bytes 1540
  1348.3 278.1 %copy-start.26 = (f32[128]{0:T(128)S(1)}, f32[128]{0:T(128)}, u32[]{:S(2)}) copy-start(f32[128]{0:T(128)} %copy-done.25) | copy-start | bytes 1540
  1348.3 278.1 %copy-start.27 = (f32[128]{0:T(128)S(1)}, f32[128]{0:T(128)}, u32[]{:S(2)}) copy-start(f32[128]{0:T(128)} %get-tuple-element.626) | copy-start | bytes 1540
  (2 other events, 1.2 us)
Sparse Core Ops, SparseCore 0:
  11.9 76.0 all-gather.4
  171.4 146.2 reduce-scatter.4
  321.7 72.3 all-gather.6
  396.3 71.6 all-gather.8
  489.4 147.2 reduce-scatter.8
  642.4 72.3 all-gather.10
  852.8 464.4 all-reduce.3
  1321.0 149.2 reduce-scatter.10
  1474.3 148.0 reduce-scatter.6
where the time goes:
time: 1700 us; the launch traced here: 1690 us
  waiting for transfers between devices  1260 us (74%)
  local copies, waits for them, and re-layouts  142 us (8%)
  matrix products  137 us (8%)
  blocking collectives  77 us (5%)
  other arithmetic  50.2 us (3%)
    psum x1, waiting for transfers between devices, local(): lax.psum((entry_wgrad, mixer_wgrad, inner_wgrad, down_wgrad), 'wide')  447 us
    reduce_scatter x1, waiting for transfers between devices, local(): lax.psum_scatter(jnp.dot(product, down_weight, preferred_element_type=jnp...  151 us
    reduce_scatter x1, waiting for transfers between devices, local(): lax.psum_scatter(lax.dot_general(inner_g, inner_weight, SECOND_AXIS, pref...  147 us
    reduce_scatter x1, waiting for transfers between devices, local(): lax.psum_scatter(jnp.dot(scaled, mixer_weight, preferred_element_type=jnp...  146 us
    reduce_scatter x1, waiting for transfers between devices, local(): lax.psum_scatter(lax.dot_general(entry_g, entry_weight, SECOND_AXIS, pref...  122 us
    all_gather x1, waiting for transfers between devices, local(): lax.all_gather(normalize(hidden_own).astype(jnp.bfloat16), 'narrow', axis...  65.9 us
    all_gather x1, waiting for transfers between devices, local(): lax.all_gather(normalize(tokens_wide).astype(jnp.bfloat16), 'narrow', axi...  65.5 us
    all_gather x1, waiting for transfers between devices, local(): grad_all = lax.all_gather(out_grad, 'narrow', axis=0, tiled=True)  62.1 us
  transfers between devices with their start and end apart: 9, of which 9 were waited for; matrix products, arithmetic and copies ran while one was open for 6% of the time, Pallas kernels for 0%

commit v1 on v0

v1 whole, which is shorter than its diff:
```python
import functools

import jax
import jax.numpy as jnp
import numpy as np
from jax import lax
from jax.experimental import pallas as pl
from jax.experimental.pallas import tpu as pltpu
from jax.sharding import PartitionSpec as P

D = 2048
HEAD_DIM = 128
NDOC = 4
EPS = 1e-06
BLOCK = 256
MIB = 1 << 20

F32 = jnp.float32
BF16 = jnp.bfloat16
NN = (((1,), (0,)), ((), ()))
NT = (((1,), (1,)), ((), ()))
TN = (((0,), (0,)), ((), ()))
VMEM = pl.BlockSpec(memory_space=pltpu.VMEM)
SMEM = pl.BlockSpec(memory_space=pltpu.SMEM)


def dot(a, b, dims=NN):
    return lax.dot_general(a, b, dims, preferred_element_type=F32)


def split(values):
    high = values.astype(BF16)
    return high, (values - high.astype(F32)).astype(BF16)


def normalize(values):
    return values * lax.rsqrt(jnp.mean(values * values, axis=-1, keepdims=True) + EPS)


def norm_grad(values, grad_in):
    inverse = lax.rsqrt(jnp.mean(values * values, axis=-1, keepdims=True) + EPS)
    normed = values * inverse
    return inverse * (grad_in - normed * jnp.mean(grad_in * normed, axis=-1, keepdims=True))


def ring_order(n):
    if n == 16:
        return [r * 4 + (c if r % 2 == 0 else 3 - c) for r in range(4) for c in range(4)]
    return list(range(0, n, 2)) + list(range(n - 1, 0, -2))


def distances(n):
    out = [0]
    for k in range(1, n // 2):
        out += [-k, k]
    return out + [n // 2]


def order_table(n):
    ring = ring_order(n)
    place = {device: i for i, device in enumerate(ring)}
    return np.array(
        [[ring[(place[me] + d) % n] for d in distances(n)] for me in range(n)], np.int32
    )


def onward(values, n):
    ring = ring_order(n)
    return lax.ppermute(values, "narrow", [(ring[i], ring[(i + 1) % n]) for i in range(n)])


def backward(values, n):
    ring = ring_order(n)
    return lax.ppermute(values, "narrow", [(ring[(i + 1) % n], ring[i]) for i in range(n)])


def ring_gather(own, n):
    left = right = own
    pieces = [own]
    for _ in range(n // 2 - 1):
        left, right = onward(left, n), backward(right, n)
        pieces += [left, right]
    half = own.shape[0] // 2
    return pieces + [onward(left[:half], n), backward(right[half:], n)]


def add16(a, b):
    return (a.astype(F32) + b.astype(F32)).astype(BF16)


def ring_scatter(parts, n):
    near = {d: parts[i] for i, d in enumerate(distances(n)[:-1])}
    half = parts[-1].shape[0]
    far = n // 2 - 1
    left, right = onward(parts[-2], n), backward(parts[-1], n)
    left = jnp.concatenate([add16(near[far][:half], left), near[far][half:]], 0)
    right = jnp.concatenate([near[-far][:half], add16(near[-far][half:], right)], 0)
    for k in range(far - 1, 0, -1):
        left, right = onward(left, n), backward(right, n)
        left, right = add16(near[k], left), add16(near[-k], right)
    left, right = onward(left, n), backward(right, n)
    return near[0].astype(F32) + left.astype(F32) + right.astype(F32)


def swap(values, axis, bit):
    size = lax.axis_size(axis)
    return lax.ppermute(values, axis, [(i, i ^ bit) for i in range(size)])


def butterfly(values, axis, first=1):
    bit = first
    while bit < lax.axis_size(axis):
        values = values + swap(values, axis, bit)
        bit *= 2
    return values


def wide_sum(send, keep):
    total = keep + swap(send, "wide", 1).astype(F32)
    bit = 2
    while bit < lax.axis_size("wide"):
        own = total.astype(BF16)
        total = own.astype(F32) + swap(own, "wide", bit).astype(F32)
        bit *= 2
    own = total.astype(BF16)
    return own, swap(own, "wide", 1)


def call(kernel, outs, in_specs, flops, limit, scratch=()):
    return pl.pallas_call(
        kernel,
        out_shape=[jax.ShapeDtypeStruct(s, d) for s, d in outs],
        in_specs=in_specs,
        out_specs=[VMEM] * len(outs),
        scratch_shapes=list(scratch),
        compiler_params=pltpu.CompilerParams(vmem_limit_bytes=limit),
        cost_estimate=pl.CostEstimate(
            flops=flops, bytes_accessed=2 * flops // 1000, transcendentals=0
        ),
    )


def part_shapes(n, rows):
    return [((rows, D), BF16)] * (n - 1) + [((rows // 2, D), BF16)] * 2


def store_part(parts, r, values):
    n = len(parts) - 1
    if r < n - 1:
        parts[r][...] = values
    else:
        half = values.shape[0] // 2
        parts[n - 1][...] = values[:half]
        parts[n][...] = values[half:]


def assemble(pieces, target, start_of):
    n = len(pieces) - 1
    rows = pieces[0].shape[0]
    half = rows // 2
    for r in range(n - 1):
        target[pl.ds(start_of(r), rows), :] = pieces[r][...]
    start = start_of(n - 1)
    target[pl.ds(start, half), :] = pieces[n - 1][...]
    target[pl.ds(start + half, half), :] = pieces[n][...]


def segment_of(positions, ends):
    return sum((positions >= e).astype(jnp.int32) for e in ends)


def row_ends(lengths):
    first = lengths[0, 0]
    second = first + lengths[0, 1]
    return (first, second, second + lengths[0, 2])


class Block:
    def __init__(self, b, ends):
        start = b * BLOCK
        rows = lax.broadcasted_iota(jnp.int32, (BLOCK, BLOCK), 0)
        columns = lax.broadcasted_iota(jnp.int32, (BLOCK, BLOCK), 1)
        seg_rows = segment_of(rows + start, ends)
        seg_columns = segment_of(columns + start, ends)
        self.mask = jnp.logical_and(seg_rows == seg_columns, rows >= columns)
        self.last = segment_of(start + BLOCK - 1, ends)
        self.earlier = segment_of(start - 1, ends) if b > 0 else -1
        wide_rows = lax.broadcasted_iota(jnp.int32, (BLOCK, HEAD_DIM), 0)
        segments = segment_of(wide_rows + start, ends)
        self.from_state = segments == self.earlier
        self.to_state = segments == self.last

    def decay(self, full):
        return jnp.where(self.mask, full, 0.0)

    def keeping(self, rate):
        factor = jnp.exp(jnp.full((HEAD_DIM, HEAD_DIM), -rate * BLOCK, F32))
        return jnp.where(self.last == self.earlier, factor, 0.0)


def full_decay(rate):
    rows = lax.broadcasted_iota(jnp.int32, (BLOCK, BLOCK), 0)
    columns = lax.broadcasted_iota(jnp.int32, (BLOCK, BLOCK), 1)
    return jnp.exp(-rate * jnp.maximum(rows - columns, 0).astype(F32))


def edge_factors(rate):
    rows = lax.broadcasted_iota(jnp.int32, (BLOCK, HEAD_DIM), 0).astype(F32)
    return jnp.exp(-rate * (rows + 1.0)), jnp.exp(-rate * (BLOCK - 1.0 - rows))


def silu16(values):
    return (values * jax.nn.sigmoid(values)).astype(BF16)


def silu_grad(before):
    sigmoid = jax.nn.sigmoid(before)
    return sigmoid * (1.0 + before * (1.0 - sigmoid))


def entry_kernel(n, heads, order, lengths, rates, *refs):
    pieces, refs = refs[: n + 1], refs[n + 1 :]
    weights, mixer, refs = refs[:4], refs[4], refs[5:]
    normed, proj, mixed, squares, states, refs = *refs[:5], refs[5:]
    parts, pre = refs[: n + 1], refs[n + 1]
    rows = pieces[0].shape[0]
    total = n * rows
    width = heads * HEAD_DIM
    assemble(pieces, normed, lambda r: pl.multiple_of(order[0, r] * rows, rows))
    for b in range(total // BLOCK):
        here = pl.ds(b * BLOCK, BLOCK)
        tokens = normed[here, :]
        for i, weight in enumerate(weights):
            proj[here, i * width : (i + 1) * width] = dot(tokens, weight[...])
    ends = row_ends(lengths)
    fulls = [full_decay(rates[h]) for h in range(heads)]
    edges = [edge_factors(rates[h]) for h in range(heads)]
    state = [jnp.zeros((HEAD_DIM, HEAD_DIM), F32) for _ in range(heads)]
    ones = jnp.ones((8, HEAD_DIM), BF16)
    for b in range(total // BLOCK):
        here = pl.ds(b * BLOCK, BLOCK)
        block = Block(b, ends)
        square = jnp.zeros((8, BLOCK), F32)
        for h in range(heads):
            at = [slice(i * width + h * HEAD_DIM, i * width + (h + 1) * HEAD_DIM) for i in range(4)]
            query, key = silu16(proj[here, at[0]]), silu16(proj[here, at[1]])
            value = proj[here, at[2]].astype(BF16)
            inner, carried = edges[h]
            inner = jnp.where(block.from_state, inner, 0.0)
            carried = jnp.where(block.to_state, carried, 0.0)
            states[b, h] = state[h]
            weight = (dot(query, key, NT) * block.decay(fulls[h])).astype(BF16)
            high, low = split(state[h])
            out = dot(weight, value) + inner * (dot(query, high) + dot(query, low))
            high, low = split(key.astype(F32) * carried)
            state[h] = block.keeping(rates[h]) * state[h] + (
                dot(high, value, TN) + dot(low, value, TN)
            )
            mixed[here, at[0]] = out
            pre[here, at[0]] = (out * proj[here, at[3]]).astype(BF16)
            high, low = split(out * out)
            square += dot(ones, high, NT) + dot(ones, low, NT)
        squares[:, here] = square[0:1]
    for r in range(0, n, 2):
        both = jnp.concatenate(
            [pre[pl.ds(pl.multiple_of(order[0, q] * rows, rows), rows), :] for q in (r, r + 1)], 0
        )
        result = dot(both, mixer[...]).astype(BF16)
        store_part(parts, r, result[:rows])
        store_part(parts, r + 1, result[rows:])


def column(row):
    return jnp.transpose(jnp.broadcast_to(row, (HEAD_DIM, row.shape[1])))


def exit_kernel(n, heads, order, lengths, rates, *refs):
    pieces, refs = refs[: n + 1], refs[n + 1 :]
    weights, mixer, refs = refs[:4], refs[4], refs[5:]
    proj, mixed, states, inverses, inners, refs = *refs[:5], refs[5:]
    resid, scaled, entry_g, refs = *refs[:3], refs[3:]
    parts, scaled_g = refs[: n + 1], refs[n + 1]
    rows = pieces[0].shape[0]
    total = n * rows
    width = heads * HEAD_DIM
    assemble(pieces, resid, lambda r: pl.multiple_of(order[0, r] * rows, rows))
    for b in range(total // BLOCK):
        here = pl.ds(b * BLOCK, BLOCK)
        scaled_g[here, :] = dot(resid[here, :], mixer[...], NT)
    ends = row_ends(lengths)
    fulls = [full_decay(rates[h]) for h in range(heads)]
    edges = [edge_factors(rates[h]) for h in range(heads)]
    later = [jnp.zeros((HEAD_DIM, HEAD_DIM), F32) for _ in range(heads)]
    for b in reversed(range(total // BLOCK)):
        here = pl.ds(b * BLOCK, BLOCK)
        block = Block(b, ends)
        inverse = column(inverses[:, here])
        mean = column(inners[:, here]) * (1.0 / D)
        for h in range(heads):
            at = [slice(i * width + h * HEAD_DIM, i * width + (h + 1) * HEAD_DIM) for i in range(4)]
            query_pre, key_pre = proj[here, at[0]], proj[here, at[1]]
            query, key = silu16(query_pre), silu16(key_pre)
            value = proj[here, at[2]].astype(BF16)
            gate = proj[here, at[3]]
            grad_s = scaled_g[here, at[0]]
            unit = mixed[here, at[0]] * inverse
            scaled[here, at[0]] = (unit * gate).astype(BF16)
            entry_g[here, at[3]] = (grad_s * unit).astype(BF16)
            grad = (inverse * (grad_s * gate - unit * mean)).astype(BF16)
            inner, carried = edges[h]
            inner = jnp.where(block.from_state, inner, 0.0)
            carried = jnp.where(block.to_state, carried, 0.0)
            decay = block.decay(fulls[h])
            weight = (dot(query, key, NT) * decay).astype(BF16)
            score = (dot(grad, value, NT) * decay).astype(BF16)
            high, low = split(states[b, h])
            query_g = dot(score, key) + inner * (dot(grad, high, NT) + dot(grad, low, NT))
            high, low = split(later[h])
            key_g = dot(score, query, TN) + carried * (dot(value, high, NT) + dot(value, low, NT))
            value_g = dot(weight, grad, TN) + carried * (dot(key, high) + dot(key, low))
            high, low = split(query.astype(F32) * inner)
            later[h] = (
                dot(high, grad, TN) + dot(low, grad, TN) + block.keeping(rates[h]) * later[h]
            )
            entry_g[here, at[0]] = (query_g * silu_grad(query_pre)).astype(BF16)
            entry_g[here, at[1]] = (key_g * silu_grad(key_pre)).astype(BF16)
            entry_g[here, at[2]] = value_g.astype(BF16)
    for r in range(0, n, 2):
        both = jnp.concatenate(
            [entry_g[pl.ds(pl.multiple_of(order[0, q] * rows, rows), rows), :] for q in (r, r + 1)],
            0,
        )
        result = sum(
            dot(both[:, i * width : (i + 1) * width], weight[...], NT)
            for i, weight in enumerate(weights)
        ).astype(BF16)
        store_part(parts, r, result[:rows])
        store_part(parts, r + 1, result[rows:])


def cotangent_kernel(n, *refs):
    pieces, down, grad, product_g = refs[: n + 1], *refs[n + 1 :]
    rows = pieces[0].shape[0]
    assemble(pieces, grad, lambda r: r * rows)
    for b in range(n * rows // BLOCK):
        here = pl.ds(b * BLOCK, BLOCK)
        product_g[here, :] = dot(grad[here, :], down[...], NT)


def hidden_kernel(n, *refs):
    pieces, refs = refs[: n + 1], refs[n + 1 :]
    first, second, product_g, refs = *refs[:3], refs[3:]
    normed, product, first_g, second_g, parts = *refs[:4], refs[4:]
    rows = pieces[0].shape[0]
    assemble(pieces, normed, lambda r: r * rows)
    for r in range(0, n, 2):
        here = pl.ds(r * rows, 2 * rows)
        tokens = normed[here, :]
        first_act, second_act = dot(tokens, first[...]), dot(tokens, second[...])
        product[here, :] = (first_act * second_act).astype(BF16)
        grad = product_g[here, :]
        one, two = (grad * second_act).astype(BF16), (grad * first_act).astype(BF16)
        first_g[here, :] = one
        second_g[here, :] = two
        result = (dot(one, first[...], NT) + dot(two, second[...], NT)).astype(BF16)
        store_part(parts, r, result[:rows])
        store_part(parts, r + 1, result[rows:])


def down_kernel(n, product, down, *parts):
    rows = parts[0].shape[0]
    for r in range(0, n, 2):
        result = dot(product[pl.ds(r * rows, 2 * rows), :], down[...]).astype(BF16)
        store_part(parts, r, result[:rows])
        store_part(parts, r + 1, result[rows:])


def local(
    tokens_in,
    query_weight,
    key_weight,
    value_weight,
    gate_weight,
    mixer_weight,
    first_weight,
    second_weight,
    down_weight,
    doc_lengths,
    head_decay,
    out_grad,
):
    n = lax.axis_size("narrow")
    rows = tokens_in.shape[0]
    total = rows * n
    heads = head_decay.shape[0]
    width = heads * HEAD_DIM
    units = first_weight.shape[1]
    me = lax.axis_index("narrow")
    core = lax.axis_index("wide") % 2
    start_row = me * rows
    order = lax.dynamic_slice(jnp.asarray(order_table(n)), (me, 0), (1, n))
    entry_weights = (query_weight, key_weight, value_weight, gate_weight)
    tokens_wide = tokens_in.astype(F32)
    rates = head_decay

    pieces = ring_gather(normalize(tokens_wide).astype(BF16), n)
    blocks = total // BLOCK
    normed, proj, mixed, squares, states, *parts = call(
        functools.partial(entry_kernel, n, heads),
        [
            ((total, D), BF16),
            ((total, 4 * width), F32),
            ((total, width), F32),
            ((1, total), F32),
            ((blocks, heads, HEAD_DIM, HEAD_DIM), F32),
        ]
        + part_shapes(n, rows),
        [SMEM] * 3 + [VMEM] * (n + 6),
        12 * total * D * width,
        50 * MIB,
        [pltpu.VMEM((total, width), BF16)],
    )(order, doc_lengths, rates, *pieces, *entry_weights, mixer_weight)

    grad_own, _ = lax.optimization_barrier((out_grad, pieces[-1]))
    grad_pieces = ring_gather(grad_own, n)
    grad_all, product_g = call(
        functools.partial(cotangent_kernel, n),
        [((total, D), BF16), ((total, units), F32)],
        [VMEM] * (n + 2),
        2 * total * D * units,
        32 * MIB,
    )(*grad_pieces, down_weight)

    inverses = lax.rsqrt(butterfly(squares, "narrow") / D + EPS)
    inverse_own = lax.dynamic_slice(inverses, (0, start_row), (1, rows)).reshape(rows, 1)
    attn_own = ring_scatter(parts, n) * inverse_own
    hidden_own = tokens_wide + attn_own

    pieces = ring_gather(normalize(hidden_own).astype(BF16), n)
    normed2, product, first_g, second_g, *parts = call(
        functools.partial(hidden_kernel, n),
        [((total, D), BF16)] + [((total, units), BF16)] * 3 + part_shapes(n, rows),
        [VMEM] * (n + 4),
        8 * total * D * units,
        56 * MIB,
    )(*pieces, first_weight, second_weight, product_g)
    normed2_g = ring_scatter(parts, n)
    hidden_g = out_grad.astype(F32) + norm_grad(hidden_own, normed2_g)
    resid_own = hidden_g.astype(BF16)
    inner_own = jnp.sum(resid_own.astype(F32) * attn_own, axis=1).reshape(1, rows)
    inners = butterfly(
        lax.dynamic_update_slice(jnp.zeros((1, total), F32), inner_own, (0, start_row)), "narrow"
    )
    resid_pieces = ring_gather(resid_own, n)

    product_late, _ = lax.optimization_barrier((product, resid_pieces[-1]))
    parts = call(
        functools.partial(down_kernel, n),
        part_shapes(n, rows),
        [VMEM] * 2,
        2 * total * D * units,
        24 * MIB,
    )(product_late, down_weight)
    ffn_own = ring_scatter(parts, n)
    output = (hidden_own + ffn_own).astype(BF16)
    counted = jnp.sum(doc_lengths[0, : NDOC - 1])
    valid = (start_row + jnp.arange(rows, dtype=jnp.int32) < counted).astype(F32)
    sums = jnp.stack(
        [
            jnp.sum(valid * jnp.sum(tokens_wide * tokens_wide, axis=1)),
            jnp.sum(valid * jnp.sum(attn_own * attn_own, axis=1)),
            jnp.sum(valid * jnp.sum(ffn_own * ffn_own, axis=1)),
            jnp.sum(valid),
        ]
    )
    sums = butterfly(butterfly(sums, "narrow"), "wide")
    stream_rms = jnp.sqrt(sums[:3] / (sums[3] * D))

    resid, scaled, entry_g, *parts = call(
        functools.partial(exit_kernel, n, heads),
        [((total, D), BF16), ((total, width), BF16), ((total, 4 * width), BF16)]
        + part_shapes(n, rows),
        [SMEM] * 3 + [VMEM] * (n + 11),
        12 * total * D * width,
        50 * MIB,
        [pltpu.VMEM((total, width), F32)],
    )(
        order,
        doc_lengths,
        rates,
        *resid_pieces,
        *entry_weights,
        mixer_weight,
        proj,
        mixed,
        states,
        inverses,
        inners,
    )
    normed_g = ring_scatter(parts, n)
    input_grad = hidden_g + norm_grad(tokens_wide, normed_g)

    def halves(values):
        return [
            lax.dynamic_slice_in_dim(values, place * (D // 2), D // 2, axis=1)
            for place in (1 - core, core)
        ]

    def by_rows(tokens, grads):
        send, keep = halves(tokens)
        own, other = wide_sum(dot(send, grads, TN).astype(BF16), dot(keep, grads, TN))
        return jnp.concatenate(
            [jnp.where(core == 0, own, other), jnp.where(core == 0, other, own)], 0
        )

    def by_columns(tokens, grads):
        send, keep = halves(grads)
        own, other = wide_sum(dot(tokens, send, TN).astype(BF16), dot(tokens, keep, TN))
        return jnp.concatenate(
            [jnp.where(core == 0, own, other), jnp.where(core == 0, other, own)], 1
        ).astype(F32)

    first_w = by_rows(normed2, first_g).astype(F32)
    second_w = by_rows(normed2, second_g).astype(F32)
    down_w = by_columns(product, grad_all)
    mixer_w = by_columns(scaled, resid)
    entry_w = by_rows(normed, entry_g)
    entry_ws = [entry_w[:, i * width : (i + 1) * width].astype(F32) for i in range(4)]
    return (output, input_grad, *entry_ws, mixer_w, first_w, second_w, down_w, stream_rms)


def solution(mesh):
    split_tokens = P(("wide", "narrow"), None)
    columns, rows = P(None, "narrow"), P("narrow", None)
    return jax.shard_map(
        local,
        mesh=mesh,
        in_specs=(split_tokens,)
        + (columns,) * 4
        + (rows, columns, columns, rows, P("wide", None), P("narrow"), split_tokens),
        out_specs=(split_tokens,) * 2 + (columns,) * 4 + (rows, columns, columns, rows, P()),
        check_vma=False,
    )
```

time: 1700 us -> 543 us (0.32)
  waiting for transfers between devices: 1260 us -> 266 us
  local copies, waits for them, and re-layouts: 142 us -> 27.5 us
  matrix products: 137 us -> 24.3 us
  starting transfers between devices: 1.19 us -> 97.6 us
  blocking collectives: 77 us -> 0 us
  Pallas kernels: 0 us -> 57.9 us
    reduce_scatter x4 -> x0, waiting for transfers between devices: 566 us -> none  [the longest x1 151 us: local(): lax.psum_scatter(jnp.dot(product, down_weight, preferred_element_type=jnp...]
    psum x1 -> x0, waiting for transfers between devices: 447 us -> none  [local(): lax.psum((entry_wgrad, mixer_wgrad, inner_wgrad, down_wgrad), 'wide')]
    ppermute x0 -> x90, waiting for transfers between devices: none -> 266 us  [the longest x32 103 us: onward(): lax.ppermute(values, 'narrow', [(ring[i], ring[(i + 1) % n]) for i in ran...]
    all_gather x4 -> x0, waiting for transfers between devices: 244 us -> none  [the longest x1 65.9 us: local(): lax.all_gather(normalize(hidden_own).astype(jnp.bfloat16), 'narrow', axis...]
    dot_general x34 -> x10, matrix products: 137 us -> 24.3 us  [dot(): return lax.dot_general(a, b, dims, preferred_element_type=F32)]
    ppermute x0 -> x90, starting transfers between devices: none -> 97.6 us  [the longest x32 45.4 us: onward(): lax.ppermute(values, 'narrow', [(ring[i], ring[(i + 1) % n]) for i in ran...]
    psum x3 -> x0, blocking collectives: 77 us -> none  [the longest x1 39.5 us: local(): lax.psum((jnp.sum(valid * jnp.sum(tokens_wide * tokens_wide, axis=1)), jn...]
    pallas_call x0 -> x5, Pallas kernels: none -> 57.9 us  [the longest x1 19.4 us: local(): call(functools.partial(hidden_kernel, n), [((total, D), BF16)] + [((total...]
  transfers between devices with their start and end apart: 9 -> 90, of which waited for: 9 -> 43; matrix products, arithmetic and copies ran while one was open for 6% -> 18% of each run, Pallas kernels for 0% -> 4%
where the time goes in v1:
time: 543 us; the launch traced here: 533 us
  waiting for transfers between devices  266 us (49%)
  starting transfers between devices  97.6 us (18%)
  Pallas kernels  57.9 us (11%)
  other arithmetic  56.8 us (10%)
  local copies, waits for them, and re-layouts  27.5 us (5%)
  matrix products  24.3 us (4%)
    ppermute x32, waiting for transfers between devices, onward(): lax.ppermute(values, 'narrow', [(ring[i], ring[(i + 1) % n]) for i in ran...  103 us
    ppermute x26, waiting for transfers between devices, swap(): return lax.ppermute(values, axis, [(i, i ^ bit) for i in range(size)])  96.5 us
    ppermute x32, waiting for transfers between devices, backward(): lax.ppermute(values, 'narrow', [(ring[(i + 1) % n], ring[i]) for i in ran...  67.2 us
    ppermute x32, starting transfers between devices, onward(): lax.ppermute(values, 'narrow', [(ring[i], ring[(i + 1) % n]) for i in ran...  45.4 us
    ppermute x32, starting transfers between devices, backward(): lax.ppermute(values, 'narrow', [(ring[(i + 1) % n], ring[i]) for i in ran...  26.5 us
    ppermute x26, starting transfers between devices, swap(): return lax.ppermute(values, axis, [(i, i ^ bit) for i in range(size)])  25.7 us
    dot_general x10, matrix products, dot(): return lax.dot_general(a, b, dims, preferred_element_type=F32)  24.3 us
    pallas_call x1, Pallas kernels, local(): call(functools.partial(hidden_kernel, n), [((total, D), BF16)] + [((total...  19.4 us
  transfers between devices with their start and end apart: 90, of which 43 were waited for; matrix products, arithmetic and copies ran while one was open for 18% of the time, Pallas kernels for 4%

profile of v1, /device:TPU:0, one launch (start us, length us, event | category | flops | bytes accessed | tf_op | source)
XLA Modules:
  0.0 532.6 jit_solution(14467230314749410709)
XLA Ops:
  3.1 3.0 collective-permute-start.1
  6.3 11.9 %collective-permute-done.1.refs_2_ = bf16[128,2048]{1,0:T(8,128)(2,1)S(1)} collective-permute-done((bf16[128,2048]{1,0:T(8,128)(2,1)S(1)}, bf16[128,2048]{1,0:T(8,128)(2,1)S(1)}, u32[]{:S(2)}, u32[]{:S(2)}) %collective-permute-start.1) | collective-permute-done | bytes 524320 | tf_op jit(solution)/shard_map/ppermute | solution.py:74
  20.2 11.1 %collective-permute-done.3.refs_4_ = bf16[128,2048]{1,0:T(8,128)(2,1)S(1)} collective-permute-done((bf16[128,2048]{1,0:T(8,128)(2,1)S(1)}, bf16[128,2048]{1,0:T(8,128)(2,1)S(1)}, u32[]{:S(2)}, u32[]{:S(2)}) %collective-permute-start.3) | collective-permute-done | bytes 524320 | tf_op jit(solution)/shard_map/ppermute | solution.py:74
  33.3 10.1 %collective-permute-done.5.refs_6_ = bf16[128,2048]{1,0:T(8,128)(2,1)S(1)} collective-permute-done((bf16[128,2048]{1,0:T(8,128)(2,1)S(1)}, bf16[128,2048]{1,0:T(8,128)(2,1)S(1)}, u32[]{:S(2)}, u32[]{:S(2)}) %collective-permute-start.5) | collective-permute-done | bytes 524320 | tf_op jit(solution)/shard_map/ppermute | solution.py:74
  46.3 3.6 collective-permute-done.7.refs_8_
  51.1 14.8 %shard_map.212 = (bf16[1024,2048]{1,0:T(8,128)(2,1)}, f32[1024,1024]{1,0:T(8,128)}, f32[1024,256]{1,0:T(8,128)}, f32[1,1024]{1,0:T(1,128)S(1)}, f32[4,2,128,128]...) custom-call(s32[1,8]{1,0:T(1,128)S(1)} %constant_dynamic-slice_fusio, ...), custom_call_target="tpu_custom_call" | custom-call | flops 6442450944 | bytes 12884901 | tf_op jit(solution)/shard_map/pallas_call | solution.py:408
  70.1 3.5 collective-permute-done.8
  78.1 9.1 %collective-permute-done.9 = bf16[128,2048]{1,0:T(8,128)(2,1)S(1)} collective-permute-done((bf16[128,2048]{1,0:T(8,128)(2,1)S(1)}, bf16[128,2048]{1,0:T(8,128)(2,1)S(1)}, u32[]{:S(2)}, u32[]{:S(2)}) %collective-permute-start.9) | collective-permute-done | bytes 524320 | tf_op jit(solution)/shard_map/ppermute | solution.py:69
  90.8 9.9 %collective-permute-done.10 = bf16[128,2048]{1,0:T(8,128)(2,1)S(1)} collective-permute-done((bf16[128,2048]{1,0:T(8,128)(2,1)S(1)}, bf16[128,2048]{1,0:T(8,128)(2,1)S(1)}, u32[]{:S(2)}, u32[]{:S(2)}) %collective-permute-start.10) | collective-permute-done | bytes 524320 | tf_op jit(solution)/shard_map/ppermute | solution.py:69
  106.0 5.0 collective-permute-done.16
  111.0 3.6 collective-permute-done.17
  114.6 6.3 %collective-permute-start.18 = (f32[1,1024]{1,0:T(1,128)S(1)}, f32[1,1024]{1,0:T(1,128)S(1)}, u32[]{:S(2)}, u32[]{:S(2)}) collective-permute-start(f32[1,1024]{1,0:T(1,128)S(1)} %add.238), channel_id=1, source_target_pairs={{0,4},{1,5},{2,6},{3,7},{4,0},{5,1},{6,2},{7,3},{8,12},{9,13},{10,... | collective-permute-start | bytes 12296 | tf_op jit(solution)/shard_map/ppermute | solution.py:107
  127.0 8.8 %collective-permute-done.27.refs_1_ = bf16[128,2048]{1,0:T(8,128)(2,1)S(1)} collective-permute-done((bf16[128,2048]{1,0:T(8,128)(2,1)S(1)}, bf16[128,2048]{1,0:T(8,128)(2,1)S(1)}, u32[]{:S(2)}, u32[]{:S(2)}) %collective-permute-start.27) | collective-permute-done | bytes 524320 | tf_op jit(solution)/shard_map/ppermute | solution.py:69
  137.9 9.2 %collective-permute-done.19.refs_1_ = bf16[128,2048]{1,0:T(8,128)(2,1)S(1)} collective-permute-done((bf16[128,2048]{1,0:T(8,128)(2,1)S(1)}, bf16[128,2048]{1,0:T(8,128)(2,1)S(1)}, u32[]{:S(2)}, u32[]{:S(2)}) %collective-permute-start.19) | collective-permute-done | bytes 524320 | tf_op jit(solution)/shard_map/ppermute | solution.py:69
  149.1 9.2 %collective-permute-done.29.refs_3_ = bf16[128,2048]{1,0:T(8,128)(2,1)S(1)} collective-permute-done((bf16[128,2048]{1,0:T(8,128)(2,1)S(1)}, bf16[128,2048]{1,0:T(8,128)(2,1)S(1)}, u32[]{:S(2)}, u32[]{:S(2)}) %collective-permute-start.29) | collective-permute-done | bytes 524320 | tf_op jit(solution)/shard_map/ppermute | solution.py:69
  160.3 9.3 %collective-permute-done.21.refs_3_ = bf16[128,2048]{1,0:T(8,128)(2,1)} collective-permute-done((bf16[128,2048]{1,0:T(8,128)(2,1)S(1)}, bf16[128,2048]{1,0:T(8,128)(2,1)}, u32[]{:S(2)}, u32[]{:S(2)}) %collective-permute-start.21) | collective-permute-done | bytes 524320 | tf_op jit(solution)/shard_map/ppermute | solution.py:69
  171.7 8.3 %collective-permute-done.31.refs_5_ = bf16[128,2048]{1,0:T(8,128)(2,1)S(1)} collective-permute-done((bf16[128,2048]{1,0:T(8,128)(2,1)S(1)}, bf16[128,2048]{1,0:T(8,128)(2,1)S(1)}, u32[]{:S(2)}, u32[]{:S(2)}) %collective-permute-start.31) | collective-permute-done | bytes 524320 | tf_op jit(solution)/shard_map/ppermute | solution.py:69
  183.5 4.7 copy.24.refs_9_
  188.2 4.6 copy.25.refs_10_
  200.2 4.4 shard_map.213
  209.1 19.4 %shard_map.214 = (bf16[1024,2048]{1,0:T(8,128)(2,1)}, bf16[1024,704]{1,0:T(8,128)(2,1)}, bf16[1024,704]{1,0:T(8,128)(2,1)}, bf16[1024,704]{1,0:T(8,128)(2,1)}, b...) custom-call(bf16[128,2048]{1,0:T(8,128)(2,1)} %copy-done.22, ...), custom_call_target="tpu_custom_call" | custom-call | flops 11811160064 | bytes 23622320 | tf_op jit(solution)/shard_map/pallas_call | solution.py:440
  239.9 6.5 %collective-permute-done.36 = bf16[128,2048]{1,0:T(8,128)(2,1)} collective-permute-done((bf16[128,2048]{1,0:T(8,128)(2,1)}, bf16[128,2048]{1,0:T(8,128)(2,1)}, u32[]{:S(2)}, u32[]{:S(2)}) %collective-permute-start.36) | collective-permute-done | bytes 524320 | tf_op jit(solution)/shard_map/ppermute | solution.py:69
  251.0 3.4 fusion.29
  264.7 4.3 collective-permute-done.38
  274.5 2.8 add_convert_fusion.3
  280.1 2.9 add_convert_fusion.5
  287.6 2.9 add_convert_fusion.7
  290.5 3.3 collective-permute-done.61
  296.3 3.3 collective-permute-start.44
  300.3 10.9 %collective-permute-done.44.refs_4_ = bf16[128,2048]{1,0:T(8,128)(2,1)} collective-permute-done((bf16[128,2048]{1,0:T(8,128)(2,1)S(1)}, bf16[128,2048]{1,0:T(8,128)(2,1)}, u32[]{:S(2)}, u32[]{:S(2)}) %collective-permute-start.44) | collective-permute-done | bytes 524320 | tf_op jit(solution)/shard_map/ppermute | solution.py:74
  317.2 25.9 %collective-permute-done.80 = bf16[1024,704]{0,1:T(8,128)(2,1)} collective-permute-done((bf16[1024,704]{0,1:T(8,128)(2,1)}, bf16[1024,704]{0,1:T(8,128)(2,1)}, u32[]{:S(2)}, u32[]{:S(2)}) %collective-permute-start.80) | collective-permute-done | bytes 1441824 | tf_op jit(solution)/shard_map/ppermute | solution.py:107
  348.0 20.9 %collective-permute-done.77 = bf16[1024,704]{0,1:T(8,128)(2,1)} collective-permute-done((bf16[1024,704]{0,1:T(8,128)(2,1)}, bf16[1024,704]{0,1:T(8,128)(2,1)}, u32[]{:S(2)}, u32[]{:S(2)}) %collective-permute-start.77) | collective-permute-done | bytes 1441824 | tf_op jit(solution)/shard_map/ppermute | solution.py:107
  371.5 15.9 %shard_map.216 = (bf16[1024,2048]{1,0:T(8,128)(2,1)}, bf16[1024,256]{1,0:T(8,128)(2,1)S(1)}, bf16[1024,1024]{1,0:T(8,128)(2,1)}, bf16[128,2048]{1,0:T(8,128)(2,1...) custom-call(s32[1,8]{1,0:T(1,128)S(1)} %constant_dynamic-slice_fusio, ...), custom_call_target="tpu_custom_call" | custom-call | flops 6442450944 | bytes 12884901 | tf_op jit(solution)/shard_map/pallas_call | solution.py:479
  390.8 4.8 fusion.12
  395.6 3.4 shard_map.215
  402.1 5.9 %collective-permute-done.47 = bf16[64,2048]{1,0:T(8,128)(2,1)S(1)} collective-permute-done((bf16[64,2048]{1,0:T(8,128)(2,1)S(1)}, bf16[64,2048]{1,0:T(8,128)(2,1)S(1)}, u32[]{:S(2)}, u32[]{:S(2)}) %collective-permute-start.47) | collective-permute-done | bytes 262176 | tf_op jit(solution)/shard_map/ppermute | solution.py:69
  414.3 3.3 maximum_convert_fusion.2
  420.6 3.3 maximum_convert_fusion.1
  426.1 3.3 maximum_convert_fusion
  432.7 3.2 collective-permute-done.48
  444.1 3.1 collective-permute-done.64
  447.3 3.5 collective-permute-done.68
  452.3 6.0 %collective-permute-done.49 = bf16[128,2048]{1,0:T(8,128)(2,1)S(1)} collective-permute-done((bf16[128,2048]{1,0:T(8,128)(2,1)S(1)}, bf16[128,2048]{1,0:T(8,128)(2,1)S(1)}, u32[]{:S(2)}, u32[]{:S(2)}) %collective-permute-start.49) | collective-permute-done | bytes 524320 | tf_op jit(solution)/shard_map/ppermute | solution.py:69
  461.7 26.4 %collective-permute-done.71 = bf16[1024,1024]{1,0:T(8,128)(2,1)S(1)} collective-permute-done((bf16[1024,1024]{1,0:T(8,128)(2,1)S(1)}, bf16[1024,1024]{1,0:T(8,128)(2,1)S(1)}, u32[]{:S(2)}, u32[]{:S(2)}) %collective-permute-start.71) | collective-permute-done | bytes 2097184 | tf_op jit(solution)/shard_map/ppermute | solution.py:107
  491.6 7.8 %collective-permute-done.54 = bf16[128,2048]{1,0:T(8,128)(2,1)S(1)} collective-permute-done((bf16[128,2048]{1,0:T(8,128)(2,1)S(1)}, bf16[128,2048]{1,0:T(8,128)(2,1)S(1)}, u32[]{:S(2)}, u32[]{:S(2)}) %collective-permute-start.54) | collective-permute-done | bytes 524320 | tf_op jit(solution)/shard_map/ppermute | solution.py:74
  505.4 3.5 collective-permute-done.85
  515.1 2.7 fusion.87
  528.9 3.5 fusion.63
  (346 shorter events, 173.7 us)
Async XLA Ops:
  3.1 15.0 %collective-permute-start.1 = (bf16[128,2048]{1,0:T(8,128)(2,1)S(1)}, bf16[128,2048]{1,0:T(8,128)(2,1)S(1)}, u32[]{:S(2)}, u32[]{:S(2)}) collective-permute-start(bf16[128,2048]{1,0:T(8,128)(2,1)S(1)} %fusion.42.refs_0_), channel_id=1, source_target_pairs={{2,0},{4,2},{6,4},{7,6},{5,7},{3,5},{1,3},{0,1},{10,8},{12,10},{14... | collective-permute-start | bytes 1572872 | tf_op jit(solution)/shard_map/ppermute | solution.py:74
  100.8 22.3 %collective-permute-start.11 = (bf16[128,2048]{1,0:T(8,128)(2,1)S(1)}, bf16[128,2048]{1,0:T(8,128)(2,1)}, u32[]{:S(2)}, u32[]{:S(2)}) collective-permute-start(bf16[128,2048]{1,0:T(8,128)(2,1)S(1)} %add_convert_fusion.24), channel_id=1, source_target_pairs={{0,2},{2,4},{4,6},{6,7},{7,5},{5,3},{3,1},{1,0},{8,10},{10,12},{12... | collective-permute-start | bytes 1572872 | tf_op jit(solution)/shard_map/ppermute | solution.py:69
  103.0 20.1 %collective-permute-start.15 = (bf16[128,2048]{1,0:T(8,128)(2,1)}, bf16[128,2048]{1,0:T(8,128)(2,1)}, u32[]{:S(2)}, u32[]{:S(2)}) collective-permute-start(bf16[128,2048]{1,0:T(8,128)(2,1)} %add_convert_fusion.22), channel_id=1, source_target_pairs={{2,0},{4,2},{6,4},{7,6},{5,7},{3,5},{1,3},{0,1},{10,8},{12,10},{14... | collective-permute-start | bytes 1572872 | tf_op jit(solution)/shard_map/ppermute | solution.py:74
  121.0 14.9 %collective-permute-start.27 = (bf16[128,2048]{1,0:T(8,128)(2,1)S(1)}, bf16[128,2048]{1,0:T(8,128)(2,1)S(1)}, u32[]{:S(2)}, u32[]{:S(2)}) collective-permute-start(bf16[128,2048]{1,0:T(8,128)(2,1)S(1)} %copy-done.3), channel_id=1, source_target_pairs={{0,2},{2,4},{4,6},{6,7},{7,5},{5,3},{3,1},{1,0},{8,10},{10,12},{12... | collective-permute-start | bytes 1572872 | tf_op jit(solution)/shard_map/ppermute | solution.py:69
  123.0 14.9 %collective-permute-start.28 = (bf16[128,2048]{1,0:T(8,128)(2,1)S(1)}, bf16[128,2048]{1,0:T(8,128)(2,1)S(1)}, u32[]{:S(2)}, u32[]{:S(2)}) collective-permute-start(bf16[128,2048]{1,0:T(8,128)(2,1)S(1)} %copy-done.3), channel_id=1, source_target_pairs={{2,0},{4,2},{6,4},{7,6},{5,7},{3,5},{1,3},{0,1},{10,8},{12,10},{14... | collective-permute-start | bytes 1572872 | tf_op jit(solution)/shard_map/ppermute | solution.py:74
  124.9 22.1 %collective-permute-start.19 = (bf16[128,2048]{1,0:T(8,128)(2,1)S(1)}, bf16[128,2048]{1,0:T(8,128)(2,1)S(1)}, u32[]{:S(2)}, u32[]{:S(2)}) collective-permute-start(bf16[128,2048]{1,0:T(8,128)(2,1)S(1)} %multiply_convert_fusion.refs_0_), channel_id=1, source_target_pairs={{0,2},{2,4},{4,6},{6,7},{7,5},{5,3},{3,1},{1,0},{8,10},{10,12},{12... | collective-permute-start | bytes 1572872 | tf_op jit(solution)/shard_map/ppermute | solution.py:69
  127.0 22.1 %collective-permute-start.20 = (bf16[128,2048]{1,0:T(8,128)(2,1)S(1)}, bf16[128,2048]{1,0:T(8,128)(2,1)S(1)}, u32[]{:S(2)}, u32[]{:S(2)}) collective-permute-start(bf16[128,2048]{1,0:T(8,128)(2,1)S(1)} %multiply_convert_fusion.refs_0_), channel_id=1, source_target_pairs={{2,0},{4,2},{6,4},{7,6},{5,7},{3,5},{1,3},{0,1},{10,8},{12,10},{14... | collective-permute-start | bytes 1572872 | tf_op jit(solution)/shard_map/ppermute | solution.py:74
  135.8 22.5 %collective-permute-start.29 = (bf16[128,2048]{1,0:T(8,128)(2,1)S(1)}, bf16[128,2048]{1,0:T(8,128)(2,1)S(1)}, u32[]{:S(2)}, u32[]{:S(2)}) collective-permute-start(bf16[128,2048]{1,0:T(8,128)(2,1)S(1)} %collective-permute-done.27.refs_1_), channel_id=1, source_target_pairs={{0,2},{2,4},{4,6},{6,7},{7,5},{5,3},{3,1},{1,0},{8,10},{10,12},{12... | collective-permute-start | bytes 1572872 | tf_op jit(solution)/shard_map/ppermute | solution.py:69
  137.9 22.5 %collective-permute-start.30 = (bf16[128,2048]{1,0:T(8,128)(2,1)S(1)}, bf16[128,2048]{1,0:T(8,128)(2,1)S(1)}, u32[]{:S(2)}, u32[]{:S(2)}) collective-permute-start(bf16[128,2048]{1,0:T(8,128)(2,1)S(1)} %collective-permute-done.28.refs_2_), channel_id=1, source_target_pairs={{2,0},{4,2},{6,4},{7,6},{5,7},{3,5},{1,3},{0,1},{10,8},{12,10},{14... | collective-permute-start | bytes 1572872 | tf_op jit(solution)/shard_map/ppermute | solution.py:74
  147.1 22.6 %collective-permute-start.21 = (bf16[128,2048]{1,0:T(8,128)(2,1)S(1)}, bf16[128,2048]{1,0:T(8,128)(2,1)}, u32[]{:S(2)}, u32[]{:S(2)}) collective-permute-start(bf16[128,2048]{1,0:T(8,128)(2,1)S(1)} %collective-permute-done.19.refs_1_), channel_id=1, source_target_pairs={{0,2},{2,4},{4,6},{6,7},{7,5},{5,3},{3,1},{1,0},{8,10},{10,12},{12... | collective-permute-start | bytes 1572872 | tf_op jit(solution)/shard_map/ppermute | solution.py:69
  149.1 22.6 %collective-permute-start.22 = (bf16[128,2048]{1,0:T(8,128)(2,1)S(1)}, bf16[128,2048]{1,0:T(8,128)(2,1)}, u32[]{:S(2)}, u32[]{:S(2)}) collective-permute-start(bf16[128,2048]{1,0:T(8,128)(2,1)S(1)} %collective-permute-done.20.refs_2_), channel_id=1, source_target_pairs={{2,0},{4,2},{6,4},{7,6},{5,7},{3,5},{1,3},{0,1},{10,8},{12,10},{14... | collective-permute-start | bytes 1572872 | tf_op jit(solution)/shard_map/ppermute | solution.py:74
  158.3 21.7 %collective-permute-start.31 = (bf16[128,2048]{1,0:T(8,128)(2,1)S(1)}, bf16[128,2048]{1,0:T(8,128)(2,1)S(1)}, u32[]{:S(2)}, u32[]{:S(2)}) collective-permute-start(bf16[128,2048]{1,0:T(8,128)(2,1)S(1)} %collective-permute-done.29.refs_3_), channel_id=1, source_target_pairs={{0,2},{2,4},{4,6},{6,7},{7,5},{5,3},{3,1},{1,0},{8,10},{10,12},{12... | collective-permute-start | bytes 1572872 | tf_op jit(solution)/shard_map/ppermute | solution.py:69
  160.3 22.3 %collective-permute-start.32 = (bf16[128,2048]{1,0:T(8,128)(2,1)S(1)}, bf16[128,2048]{1,0:T(8,128)(2,1)S(1)}, u32[]{:S(2)}, u32[]{:S(2)}) collective-permute-start(bf16[128,2048]{1,0:T(8,128)(2,1)S(1)} %collective-permute-done.30.refs_4_), channel_id=1, source_target_pairs={{2,0},{4,2},{6,4},{7,6},{5,7},{3,5},{1,3},{0,1},{10,8},{12,10},{14... | collective-permute-start | bytes 1572872 | tf_op jit(solution)/shard_map/ppermute | solution.py:74
  169.6 23.1 %collective-permute-start.23 = (bf16[128,2048]{1,0:T(8,128)(2,1)}, bf16[128,2048]{1,0:T(8,128)(2,1)}, u32[]{:S(2)}, u32[]{:S(2)}) collective-permute-start(bf16[128,2048]{1,0:T(8,128)(2,1)} %collective-permute-done.21.refs_3_), channel_id=1, source_target_pairs={{0,2},{2,4},{4,6},{6,7},{7,5},{5,3},{3,1},{1,0},{8,10},{10,12},{12... | collective-permute-start | bytes 1572872 | tf_op jit(solution)/shard_map/ppermute | solution.py:69
  171.7 24.0 %collective-permute-start.24 = (bf16[128,2048]{1,0:T(8,128)(2,1)}, bf16[128,2048]{1,0:T(8,128)(2,1)}, u32[]{:S(2)}, u32[]{:S(2)}) collective-permute-start(bf16[128,2048]{1,0:T(8,128)(2,1)} %collective-permute-done.22.refs_4_), channel_id=1, source_target_pairs={{2,0},{4,2},{6,4},{7,6},{5,7},{3,5},{1,3},{0,1},{10,8},{12,10},{14... | collective-permute-start | bytes 1572872 | tf_op jit(solution)/shard_map/ppermute | solution.py:74
  180.7 16.6 %collective-permute-start.33 = (bf16[64,2048]{1,0:T(8,128)(2,1)}, bf16[64,2048]{1,0:T(8,128)(2,1)S(1)}, u32[]{:S(2)}, u32[]{:S(2)}) collective-permute-start(bf16[64,2048]{1,0:T(8,128)(2,1)} %slice.128), channel_id=1, source_target_pairs={{0,2},{2,4},{4,6},{6,7},{7,5},{5,3},{3,1},{1,0},{8,10},{10,12},{12... | collective-permute-start | bytes 786440 | tf_op jit(solution)/shard_map/ppermute | solution.py:69
  183.4 14.0 %collective-permute-start.34 = (bf16[64,2048]{1,0:T(8,128)(2,1)}, bf16[64,2048]{1,0:T(8,128)(2,1)}, u32[]{:S(2)}, u32[]{:S(2)}) collective-permute-start(bf16[64,2048]{1,0:T(8,128)(2,1)} %slice.129), channel_id=1, source_target_pairs={{2,0},{4,2},{6,4},{7,6},{5,7},{3,5},{1,3},{0,1},{10,8},{12,10},{14... | collective-permute-start | bytes 786440 | tf_op jit(solution)/shard_map/ppermute | solution.py:74
  193.8 14.5 %collective-permute-start.25 = (bf16[64,2048]{1,0:T(8,128)(2,1)S(1)}, bf16[64,2048]{1,0:T(8,128)(2,1)S(1)}, u32[]{:S(2)}, u32[]{:S(2)}) collective-permute-start(bf16[64,2048]{1,0:T(8,128)(2,1)S(1)} %slice.126), channel_id=1, source_target_pairs={{0,2},{2,4},{4,6},{6,7},{7,5},{5,3},{3,1},{1,0},{8,10},{10,12},{12... | collective-permute-start | bytes 786440 | tf_op jit(solution)/shard_map/ppermute | solution.py:69
  254.4 19.1 %collective-permute-start.82 = (bf16[704,1024]{1,0:T(8,128)(2,1)S(1)}, bf16[704,1024]{1,0:T(8,128)(2,1)S(1)}, u32[]{:S(2)}, u32[]{:S(2)}) collective-permute-start(bf16[704,1024]{1,0:T(8,128)(2,1)S(1)} %fusion.29), channel_id=1, source_target_pairs={{0,8},{8,0},{16,24},{24,16},{1,9},{9,1},{17,25},{25,17},{2,10},{10... | collective-permute-start | bytes 4325384 | tf_op jit(solution)/shard_map/ppermute | solution.py:107
  262.3 17.7 %collective-permute-start.79 = (bf16[1024,704]{0,1:T(8,128)(2,1)S(1)}, bf16[1024,704]{0,1:T(8,128)(2,1)S(1)}, u32[]{:S(2)}, u32[]{:S(2)}) collective-permute-start(bf16[1024,704]{0,1:T(8,128)(2,1)S(1)} %fusion.26), channel_id=1, source_target_pairs={{0,8},{8,0},{16,24},{24,16},{1,9},{9,1},{17,25},{25,17},{2,10},{10... | collective-permute-start | bytes 4325384 | tf_op jit(solution)/shard_map/ppermute | solution.py:107
  264.2 21.3 %collective-permute-start.76 = (bf16[1024,704]{0,1:T(8,128)(2,1)S(1)}, bf16[1024,704]{0,1:T(8,128)(2,1)S(1)}, u32[]{:S(2)}, u32[]{:S(2)}) collective-permute-start(bf16[1024,704]{0,1:T(8,128)(2,1)S(1)} %fusion.23), channel_id=1, source_target_pairs={{0,8},{8,0},{16,24},{24,16},{1,9},{9,1},{17,25},{25,17},{2,10},{10... | collective-permute-start | bytes 4325384 | tf_op jit(solution)/shard_map/ppermute | solution.py:107
  277.4 37.3 %collective-permute-start.83 = (bf16[704,1024]{1,0:T(8,128)(2,1)}, bf16[704,1024]{1,0:T(8,128)(2,1)}, u32[]{:S(2)}, u32[]{:S(2)}) collective-permute-start(bf16[704,1024]{1,0:T(8,128)(2,1)} %add_convert_fusion.3), channel_id=1, source_target_pairs={{0,16},{8,24},{16,0},{24,8},{1,17},{9,25},{17,1},{25,9},{2,18},{10... | collective-permute-start | bytes 4325384 | tf_op jit(solution)/shard_map/ppermute | solution.py:107
  282.9 60.2 %collective-permute-start.80 = (bf16[1024,704]{0,1:T(8,128)(2,1)}, bf16[1024,704]{0,1:T(8,128)(2,1)}, u32[]{:S(2)}, u32[]{:S(2)}) collective-permute-start(bf16[1024,704]{0,1:T(8,128)(2,1)} %add_convert_fusion.5), channel_id=1, source_target_pairs={{0,16},{8,24},{16,0},{24,8},{1,17},{9,25},{17,1},{25,9},{2,18},{10... | collective-permute-start | bytes 4325384 | tf_op jit(solution)/shard_map/ppermute | solution.py:107
  284.3 15.3 %collective-permute-start.55 = (bf16[128,2048]{1,0:T(8,128)(2,1)S(1)}, bf16[128,2048]{1,0:T(8,128)(2,1)}, u32[]{:S(2)}, u32[]{:S(2)}) collective-permute-start(bf16[128,2048]{1,0:T(8,128)(2,1)S(1)} %get-tuple-element.122.refs_0_), channel_id=1, source_target_pairs={{0,2},{2,4},{4,6},{6,7},{7,5},{5,3},{3,1},{1,0},{8,10},{10,12},{12... | collective-permute-start | bytes 1572872 | tf_op jit(solution)/shard_map/ppermute | solution.py:69
  293.8 75.1 %collective-permute-start.77 = (bf16[1024,704]{0,1:T(8,128)(2,1)}, bf16[1024,704]{0,1:T(8,128)(2,1)}, u32[]{:S(2)}, u32[]{:S(2)}) collective-permute-start(bf16[1024,704]{0,1:T(8,128)(2,1)} %add_convert_fusion.7), channel_id=1, source_target_pairs={{0,16},{8,24},{16,0},{24,8},{1,17},{9,25},{17,1},{25,9},{2,18},{10... | collective-permute-start | bytes 4325384 | tf_op jit(solution)/shard_map/ppermute | solution.py:107
  296.3 14.9 %collective-permute-start.44 = (bf16[128,2048]{1,0:T(8,128)(2,1)S(1)}, bf16[128,2048]{1,0:T(8,128)(2,1)}, u32[]{:S(2)}, u32[]{:S(2)}) collective-permute-start(bf16[128,2048]{1,0:T(8,128)(2,1)S(1)} %collective-permute-done.43.refs_2_), channel_id=1, source_target_pairs={{2,0},{4,2},{6,4},{7,6},{5,7},{3,5},{1,3},{0,1},{10,8},{12,10},{14... | collective-permute-start | bytes 1572872 | tf_op jit(solution)/shard_map/ppermute | solution.py:74
  299.6 13.9 %collective-permute-start.56 = (bf16[128,2048]{1,0:T(8,128)(2,1)}, bf16[128,2048]{1,0:T(8,128)(2,1)}, u32[]{:S(2)}, u32[]{:S(2)}) collective-permute-start(bf16[128,2048]{1,0:T(8,128)(2,1)} %collective-permute-done.55.refs_1_), channel_id=1, source_target_pairs={{0,2},{2,4},{4,6},{6,7},{7,5},{5,3},{3,1},{1,0},{8,10},{10,12},{12... | collective-permute-start | bytes 1572872 | tf_op jit(solution)/shard_map/ppermute | solution.py:69
  311.2 34.4 %collective-permute-start.45 = (bf16[128,2048]{1,0:T(8,128)(2,1)}, bf16[128,2048]{1,0:T(8,128)(2,1)S(1)}, u32[]{:S(2)}, u32[]{:S(2)}) collective-permute-start(bf16[128,2048]{1,0:T(8,128)(2,1)} %collective-permute-done.44.refs_4_), channel_id=1, source_target_pairs={{2,0},{4,2},{6,4},{7,6},{5,7},{3,5},{1,3},{0,1},{10,8},{12,10},{14... | collective-permute-start | bytes 1572872 | tf_op jit(solution)/shard_map/ppermute | solution.py:74
  313.5 33.1 %collective-permute-start.57 = (bf16[128,2048]{1,0:T(8,128)(2,1)}, bf16[128,2048]{1,0:T(8,128)(2,1)S(1)}, u32[]{:S(2)}, u32[]{:S(2)}) collective-permute-start(bf16[128,2048]{1,0:T(8,128)(2,1)} %collective-permute-done.56.refs_3_), channel_id=1, source_target_pairs={{0,2},{2,4},{4,6},{6,7},{7,5},{5,3},{3,1},{1,0},{8,10},{10,12},{12... | collective-permute-start | bytes 1572872 | tf_op jit(solution)/shard_map/ppermute | solution.py:69
  317.1 95.0 %collective-permute-start.84 = (bf16[704,1024]{1,0:T(8,128)(2,1)S(1)}, bf16[704,1024]{1,0:T(8,128)(2,1)}, u32[]{:S(2)}, u32[]{:S(2)}) collective-permute-start(bf16[704,1024]{1,0:T(8,128)(2,1)S(1)} %add_convert_fusion.2), channel_id=1, source_target_pairs={{0,8},{8,0},{16,24},{24,16},{1,9},{9,1},{17,25},{25,17},{2,10},{10... | collective-permute-start | bytes 4325384 | tf_op jit(solution)/shard_map/ppermute | solution.py:107
  345.5 72.1 %collective-permute-start.81 = (bf16[1024,704]{0,1:T(8,128)(2,1)S(1)}, bf16[1024,704]{0,1:T(8,128)(2,1)}, u32[]{:S(2)}, u32[]{:S(2)}) collective-permute-start(bf16[1024,704]{0,1:T(8,128)(2,1)S(1)} %add_convert_fusion.4), channel_id=1, source_target_pairs={{0,8},{8,0},{16,24},{24,16},{1,9},{9,1},{17,25},{25,17},{2,10},{10... | collective-permute-start | bytes 4325384 | tf_op jit(solution)/shard_map/ppermute | solution.py:107
  345.6 25.8 %collective-permute-start.46 = (bf16[64,2048]{1,0:T(8,128)(2,1)S(1)}, bf16[64,2048]{1,0:T(8,128)(2,1)S(1)}, u32[]{:S(2)}, u32[]{:S(2)}) collective-permute-start(bf16[64,2048]{1,0:T(8,128)(2,1)S(1)} %slice.130), channel_id=1, source_target_pairs={{2,0},{4,2},{6,4},{7,6},{5,7},{3,5},{1,3},{0,1},{10,8},{12,10},{14... | collective-permute-start | bytes 786440 | tf_op jit(solution)/shard_map/ppermute | solution.py:74
  346.6 24.8 %collective-permute-start.58 = (bf16[64,2048]{1,0:T(8,128)(2,1)S(1)}, bf16[64,2048]{1,0:T(8,128)(2,1)S(1)}, u32[]{:S(2)}, u32[]{:S(2)}) collective-permute-start(bf16[64,2048]{1,0:T(8,128)(2,1)S(1)} %slice.131), channel_id=1, source_target_pairs={{0,2},{2,4},{4,6},{6,7},{7,5},{5,3},{3,1},{1,0},{8,10},{10,12},{12... | collective-permute-start | bytes 786440 | tf_op jit(solution)/shard_map/ppermute | solution.py:69
  371.4 52.6 %collective-permute-start.78 = (bf16[1024,704]{0,1:T(8,128)(2,1)S(1)}, bf16[1024,704]{0,1:T(8,128)(2,1)}, u32[]{:S(2)}, u32[]{:S(2)}) collective-permute-start(bf16[1024,704]{0,1:T(8,128)(2,1)S(1)} %add_convert_fusion.6), channel_id=1, source_target_pairs={{0,8},{8,0},{16,24},{24,16},{1,9},{9,1},{17,25},{25,17},{2,10},{10... | collective-permute-start | bytes 4325384 | tf_op jit(solution)/shard_map/ppermute | solution.py:107
  409.3 29.6 %collective-permute-start.70 = (bf16[1024,1024]{1,0:T(8,128)(2,1)S(1)}, bf16[1024,1024]{1,0:T(8,128)(2,1)S(1)}, u32[]{:S(2)}, u32[]{:S(2)}) collective-permute-start(bf16[1024,1024]{1,0:T(8,128)(2,1)S(1)} %fusion.12), channel_id=1, source_target_pairs={{0,8},{8,0},{16,24},{24,16},{1,9},{9,1},{17,25},{25,17},{2,10},{10... | collective-permute-start | bytes 6291464 | tf_op jit(solution)/shard_map/ppermute | solution.py:107
  409.9 19.5 %collective-permute-start.63 = (bf16[128,2048]{1,0:T(8,128)(2,1)S(1)}, bf16[128,2048]{1,0:T(8,128)(2,1)S(1)}, u32[]{:S(2)}, u32[]{:S(2)}) collective-permute-start(bf16[128,2048]{1,0:T(8,128)(2,1)S(1)} %pad_maximum_fusion.7), channel_id=1, source_target_pairs={{0,2},{2,4},{4,6},{6,7},{7,5},{5,3},{3,1},{1,0},{8,10},{10,12},{12... | collective-permute-start | bytes 1572872 | tf_op jit(solution)/shard_map/ppermute | solution.py:69
  412.1 18.9 %collective-permute-start.67 = (bf16[128,2048]{1,0:T(8,128)(2,1)S(1)}, bf16[128,2048]{1,0:T(8,128)(2,1)S(1)}, u32[]{:S(2)}, u32[]{:S(2)}) collective-permute-start(bf16[128,2048]{1,0:T(8,128)(2,1)S(1)} %pad_maximum_fusion.8), channel_id=1, source_target_pairs={{2,0},{4,2},{6,4},{7,6},{5,7},{3,5},{1,3},{0,1},{10,8},{12,10},{14... | collective-permute-start | bytes 1572872 | tf_op jit(solution)/shard_map/ppermute | solution.py:74
  417.6 18.3 %collective-permute-start.48 = (bf16[128,2048]{1,0:T(8,128)(2,1)S(1)}, bf16[128,2048]{1,0:T(8,128)(2,1)S(1)}, u32[]{:S(2)}, u32[]{:S(2)}) collective-permute-start(bf16[128,2048]{1,0:T(8,128)(2,1)S(1)} %pad_maximum_fusion.5), channel_id=1, source_target_pairs={{0,2},{2,4},{4,6},{6,7},{7,5},{5,3},{3,1},{1,0},{8,10},{10,12},{12... | collective-permute-start | bytes 1572872 | tf_op jit(solution)/shard_map/ppermute | solution.py:69
  431.0 16.1 %collective-permute-start.64 = (bf16[128,2048]{1,0:T(8,128)(2,1)S(1)}, bf16[128,2048]{1,0:T(8,128)(2,1)S(1)}, u32[]{:S(2)}, u32[]{:S(2)}) collective-permute-start(bf16[128,2048]{1,0:T(8,128)(2,1)S(1)} %add_convert_fusion.12), channel_id=1, source_target_pairs={{0,2},{2,4},{4,6},{6,7},{7,5},{5,3},{3,1},{1,0},{8,10},{10,12},{12... | collective-permute-start | bytes 1572872 | tf_op jit(solution)/shard_map/ppermute | solution.py:69
  435.9 14.9 %collective-permute-start.68 = (bf16[128,2048]{1,0:T(8,128)(2,1)S(1)}, bf16[128,2048]{1,0:T(8,128)(2,1)S(1)}, u32[]{:S(2)}, u32[]{:S(2)}) collective-permute-start(bf16[128,2048]{1,0:T(8,128)(2,1)S(1)} %add_convert_fusion.10), channel_id=1, source_target_pairs={{2,0},{4,2},{6,4},{7,6},{5,7},{3,5},{1,3},{0,1},{10,8},{12,10},{14... | collective-permute-start | bytes 1572872 | tf_op jit(solution)/shard_map/ppermute | solution.py:74
  437.4 21.0 %collective-permute-start.49 = (bf16[128,2048]{1,0:T(8,128)(2,1)S(1)}, bf16[128,2048]{1,0:T(8,128)(2,1)S(1)}, u32[]{:S(2)}, u32[]{:S(2)}) collective-permute-start(bf16[128,2048]{1,0:T(8,128)(2,1)S(1)} %add_convert_fusion.17), channel_id=1, source_target_pairs={{0,2},{2,4},{4,6},{6,7},{7,5},{5,3},{3,1},{1,0},{8,10},{10,12},{12... | collective-permute-start | bytes 1572872 | tf_op jit(solution)/shard_map/ppermute | solution.py:69
  438.9 20.9 %collective-permute-start.53 = (bf16[128,2048]{1,0:T(8,128)(2,1)S(1)}, bf16[128,2048]{1,0:T(8,128)(2,1)S(1)}, u32[]{:S(2)}, u32[]{:S(2)}) collective-permute-start(bf16[128,2048]{1,0:T(8,128)(2,1)S(1)} %add_convert_fusion.15), channel_id=1, source_target_pairs={{2,0},{4,2},{6,4},{7,6},{5,7},{3,5},{1,3},{0,1},{10,8},{12,10},{14... | collective-permute-start | bytes 1572872 | tf_op jit(solution)/shard_map/ppermute | solution.py:74
  442.3 45.8 %collective-permute-start.71 = (bf16[1024,1024]{1,0:T(8,128)(2,1)S(1)}, bf16[1024,1024]{1,0:T(8,128)(2,1)S(1)}, u32[]{:S(2)}, u32[]{:S(2)}) collective-permute-start(bf16[1024,1024]{1,0:T(8,128)(2,1)S(1)} %add_convert_fusion.1), channel_id=1, source_target_pairs={{0,16},{8,24},{16,0},{24,8},{1,17},{9,25},{17,1},{25,9},{2,18},{10... | collective-permute-start | bytes 6291464 | tf_op jit(solution)/shard_map/ppermute | solution.py:107
  447.1 42.3 %collective-permute-start.75 = (bf16[256,1024]{1,0:T(8,128)(2,1)S(1)}, bf16[256,1024]{1,0:T(8,128)(2,1)S(1)}, u32[]{:S(2)}, u32[]{:S(2)}) collective-permute-start(bf16[256,1024]{1,0:T(8,128)(2,1)S(1)} %add_convert_fusion.8), channel_id=1, source_target_pairs={{0,8},{8,0},{16,24},{24,16},{1,9},{9,1},{17,25},{25,17},{2,10},{10... | collective-permute-start | bytes 1572872 | tf_op jit(solution)/shard_map/ppermute | solution.py:107
  450.8 40.5 %collective-permute-start.65 = (bf16[128,2048]{1,0:T(8,128)(2,1)S(1)}, bf16[128,2048]{1,0:T(8,128)(2,1)S(1)}, u32[]{:S(2)}, u32[]{:S(2)}) collective-permute-start(bf16[128,2048]{1,0:T(8,128)(2,1)S(1)} %add_convert_fusion.11), channel_id=1, source_target_pairs={{0,2},{2,4},{4,6},{6,7},{7,5},{5,3},{3,1},{1,0},{8,10},{10,12},{12... | collective-permute-start | bytes 1572872 | tf_op jit(solution)/shard_map/ppermute | solution.py:69
  458.4 32.8 %collective-permute-start.69 = (bf16[128,2048]{1,0:T(8,128)(2,1)S(1)}, bf16[128,2048]{1,0:T(8,128)(2,1)S(1)}, u32[]{:S(2)}, u32[]{:S(2)}) collective-permute-start(bf16[128,2048]{1,0:T(8,128)(2,1)S(1)} %add_convert_fusion.9), channel_id=1, source_target_pairs={{2,0},{4,2},{6,4},{7,6},{5,7},{3,5},{1,3},{0,1},{10,8},{12,10},{14... | collective-permute-start | bytes 1572872 | tf_op jit(solution)/shard_map/ppermute | solution.py:74
  459.9 31.8 %collective-permute-start.50 = (bf16[128,2048]{1,0:T(8,128)(2,1)S(1)}, bf16[128,2048]{1,0:T(8,128)(2,1)S(1)}, u32[]{:S(2)}, u32[]{:S(2)}) collective-permute-start(bf16[128,2048]{1,0:T(8,128)(2,1)S(1)} %add_convert_fusion.16), channel_id=1, source_target_pairs={{0,2},{2,4},{4,6},{6,7},{7,5},{5,3},{3,1},{1,0},{8,10},{10,12},{12... | collective-permute-start | bytes 1572872 | tf_op jit(solution)/shard_map/ppermute | solution.py:69
  489.4 39.2 %collective-permute-start.72 = (bf16[1024,1024]{1,0:T(8,128)(2,1)S(1)}, bf16[1024,1024]{1,0:T(8,128)(2,1)S(1)}, u32[]{:S(2)}, u32[]{:S(2)}) collective-permute-start(bf16[1024,1024]{1,0:T(8,128)(2,1)S(1)} %add_convert_fusion), channel_id=1, source_target_pairs={{0,8},{8,0},{16,24},{24,16},{1,9},{9,1},{17,25},{25,17},{2,10},{10... | collective-permute-start | bytes 6291464 | tf_op jit(solution)/shard_map/ppermute | solution.py:107
  (93 other events, 1141.2 us)

commit v2 on v1

v2 whole, which is shorter than its diff:
```python
import functools

import jax
import jax.numpy as jnp
import numpy as np
from jax import lax
from jax.experimental import pallas as pl
from jax.experimental.pallas import tpu as pltpu
from jax.sharding import PartitionSpec as P

D = 2048
HEAD_DIM = 128
NDOC = 4
EPS = 1e-06
BLOCK = 256
MIB = 1 << 20

F32 = jnp.float32
BF16 = jnp.bfloat16
NN = (((1,), (0,)), ((), ()))
NT = (((1,), (1,)), ((), ()))
TN = (((0,), (0,)), ((), ()))
VMEM = pl.BlockSpec(memory_space=pltpu.VMEM)
SMEM = pl.BlockSpec(memory_space=pltpu.SMEM)
ANY = pl.BlockSpec(memory_space=pl.ANY)


def dot(a, b, dims=NN):
    return lax.dot_general(a, b, dims, preferred_element_type=F32)


def split(values):
    high = values.astype(BF16)
    return high, (values - high.astype(F32)).astype(BF16)


def normalize(values):
    return values * lax.rsqrt(jnp.mean(values * values, axis=-1, keepdims=True) + EPS)


def norm_grad(values, grad_in):
    inverse = lax.rsqrt(jnp.mean(values * values, axis=-1, keepdims=True) + EPS)
    normed = values * inverse
    return inverse * (grad_in - normed * jnp.mean(grad_in * normed, axis=-1, keepdims=True))


def ring_order(n):
    if n == 16:
        return [r * 4 + (c if r % 2 == 0 else 3 - c) for r in range(4) for c in range(4)]
    return list(range(0, n, 2)) + list(range(n - 1, 0, -2))


def distances(n):
    out = [0]
    for k in range(1, n // 2):
        out += [-k, k]
    return out + [n // 2]


def order_table(n):
    ring = ring_order(n)
    place = {device: i for i, device in enumerate(ring)}
    return np.array(
        [[ring[(place[me] + d) % n] for d in distances(n)] for me in range(n)], np.int32
    )


def onward(values, n):
    ring = ring_order(n)
    return lax.ppermute(values, "narrow", [(ring[i], ring[(i + 1) % n]) for i in range(n)])


def backward(values, n):
    ring = ring_order(n)
    return lax.ppermute(values, "narrow", [(ring[(i + 1) % n], ring[i]) for i in range(n)])


def barrier(*values):
    return lax.optimization_barrier(values)


def add16(a, b):
    return (a.astype(F32) + b.astype(F32)).astype(BF16)


class Gather:
    def __init__(self, own, n):
        self.n, self.left_steps = n, n // 2
        self.left = self.right = own
        self.pieces = [own]

    def outgoing(self):
        if self.left_steps == 1:
            half = self.left.shape[0] // 2
            return self.left[:half], self.right[half:]
        return self.left, self.right

    def incoming(self, left, right):
        self.left_steps -= 1
        self.left, self.right = left, right
        self.pieces += [left, right]

    def step(self, count=1):
        for _ in range(count):
            left, right = self.outgoing()
            self.incoming(onward(left, self.n), backward(right, self.n))
        return self

    def finish(self):
        return self.step(self.left_steps).pieces


def merge_kernel(layout, *refs):
    outs, refs = refs[-2:], list(refs[:-2])
    at = 0
    for rows, half, offset in layout:
        if offset is None:
            for out in outs:
                out[at : at + rows] = refs.pop(0)[...]
        else:
            nears, parts, refs = refs[:2], refs[2:4], refs[4:]
            for i in range(2):
                low = half * i if half < rows else 0
                outs[i][at : at + rows] = nears[i][...]
                outs[i][at + low : at + low + half] = add16(
                    nears[i][low : low + half], parts[i][offset : offset + half]
                )
        at += rows


def join_one(low, near, part, out):
    rows = part.shape[0]
    out[...] = near[...]
    out[low : low + rows] = add16(near[low : low + rows], part[...])


class Scatter:
    def __init__(self, parts, n):
        self.n, self.left_steps = n, n // 2
        self.near = {d: parts[i] for i, d in enumerate(distances(n)[:-1])}
        self.left, self.right = parts[-2], parts[-1]
        self.received = None

    def operands(self):
        if self.received is None:
            return [self.left, self.right], (self.left.shape[0], 0, None)
        left, right, offset, half = self.received
        near = [self.near[self.left_steps], self.near[-self.left_steps]]
        return near + [left, right], (near[0].shape[0], half, offset)

    def take(self, left, right, offset, rows):
        self.left_steps -= 1
        if self.left_steps == 0:
            at = slice(offset, offset + rows)
            self.result = self.near[0].astype(F32) + left[at].astype(F32) + right[at].astype(F32)
        self.received = (left, right, offset, rows)

    def step(self, count=1):
        for _ in range(count):
            self.left_steps -= 1
            left, right = onward(self.left, self.n), backward(self.right, self.n)
            k = self.left_steps
            shape = self.near[k].shape
            if k == 0:
                self.result = self.near[0].astype(F32) + left.astype(F32) + right.astype(F32)
            elif shape == left.shape:
                self.left, self.right = add16(self.near[k], left), add16(self.near[-k], right)
            else:
                half = shape[0] // 2
                self.left, self.right = [
                    call(
                        functools.partial(join_one, low),
                        [(shape, BF16)],
                        [VMEM] * 2,
                        shape[0] * shape[1],
                        4 * MIB,
                    )(near, part)[0]
                    for low, near, part in ((0, self.near[k], left), (half, self.near[-k], right))
                ]
        return self

    def finish(self):
        return self.step(self.left_steps).result


class Together:
    def __init__(self, *scatters):
        self.scatters, self.n = scatters, scatters[0].n

    def outgoing(self):
        operands, self.layout = [], []
        for s in self.scatters:
            values, layout = s.operands()
            operands += values
            self.layout.append(layout)
        if len(self.layout) == 1 and self.layout[0][2] is None:
            return operands
        rows = sum(entry[0] for entry in self.layout)
        return call(
            functools.partial(merge_kernel, tuple(self.layout)),
            [((rows, D), BF16)] * 2,
            [VMEM] * len(operands),
            2 * rows * D,
            10 * MIB,
        )(*operands)

    def incoming(self, left, right):
        offset = 0
        for s, (rows, _, _) in zip(self.scatters, self.layout):
            s.take(left, right, offset, rows)
            offset += rows


def region(streams=(), swaps=(), work=None, inputs=()):
    out = [v for s in streams for v in s.outgoing()]
    count = len(out)
    values, inputs = lax.optimization_barrier((out + [s[0] for s in swaps], list(inputs)))
    moved = [
        onward(v, streams[0].n) if i % 2 == 0 else backward(v, streams[0].n)
        for i, v in enumerate(values[:count])
    ]
    moved += [swap(v, s[1], s[2]) for v, s in zip(values[count:], swaps)]
    results = work(*inputs) if work else ()
    moved, results = lax.optimization_barrier((moved, results))
    for i, s in enumerate(streams):
        s.incoming(*moved[2 * i : 2 * i + 2])
    return moved[count:], results


def meet(*streams):
    values = barrier(*[v for s in streams for v in (s.left, s.right)])
    for i, s in enumerate(streams):
        s.left, s.right = values[2 * i : 2 * i + 2]


def swap(values, axis, bit):
    size = lax.axis_size(axis)
    return lax.ppermute(values, axis, [(i, i ^ bit) for i in range(size)])


class Butterfly:
    def __init__(self, values, axis):
        self.left, self.right, self.axis, self.bit = values, jnp.zeros((1, 128), F32), axis, 1

    def step(self):
        if self.bit < lax.axis_size(self.axis):
            self.left = self.left + swap(self.left, self.axis, self.bit)
            self.bit *= 2
        return self

    def finish(self):
        while self.bit < lax.axis_size(self.axis):
            self.step()
        return self.left


def ladder(values, bit=4):
    while bit < lax.axis_size("wide"):
        values = add16(values, swap(values, "wide", bit))
        bit *= 2
    return values


def own_half(core):
    return pl.ds(pl.multiple_of(core[0] * (D // 2), D // 2), D // 2)


def columns_kernel(cuts, width, right_low, core, left, left_other, right_hbm, right_other, *refs):
    outs, right, semaphores = refs[:-2], refs[-2], refs[-1]
    copies = Copies(semaphores)
    coming = copies.start(right_hbm.at[:, own_half(core)], right)
    other = right_other[:, right_low : right_low + D // 2]
    part = dot(left_other[:, :width], other, TN)
    coming.wait()
    part += dot(left[:, :width], right[...], TN)
    for out, (low, high) in zip(outs, cuts):
        out[...] = part[:, low:high].astype(BF16)


def own_columns(core, cuts, width, left, left_other, right, right_other):
    total = left.shape[0]
    return call(
        functools.partial(columns_kernel, cuts, width, right_other.shape[1] - D // 2),
        [((width, high - low), BF16) for low, high in cuts],
        [SMEM, VMEM, VMEM, ANY, VMEM],
        2 * total * D * width,
        40 * MIB,
        [pltpu.VMEM((total, D // 2), BF16), pltpu.SemaphoreType.DMA((1,))],
    )(core.reshape(1), left, left_other, right, right_other)


def entry_sums_kernel(
    core, bundle, bundle_other, resid_hbm, normed_hbm, normed_other, mixer_out, *refs
):
    outs, (resid, normed, semaphores) = refs[:4], refs[4:]
    width = mixer_out.shape[0]
    copies = Copies(semaphores)
    first = copies.start(normed_hbm.at[:, own_half(core)], normed)
    second = copies.start(resid_hbm.at[:, own_half(core)], resid)
    for i in (3, 2, 1, 0):
        at = slice(i * width, (i + 1) * width)
        part = dot(normed_other[...], bundle_other[:, at], TN)
        if i == 3:
            first.wait()
        outs[i][...] = (part + dot(normed[...], bundle[:, at], TN)).astype(BF16)
    at, half = slice(4 * width, 5 * width), slice(5 * width, 5 * width + D // 2)
    part = dot(bundle_other[:, at], bundle_other[:, half], TN)
    second.wait()
    mixer_out[...] = (part + dot(bundle[:, at], resid[...], TN)).astype(BF16)


def sum_kernel(*refs):
    out, low = refs[-1], 0
    for i in range(len(refs) // 2):
        width = refs[2 * i].shape[1]
        out[:, low : low + width] = add16(refs[2 * i][...], refs[2 * i + 1][...])
        low += width


def summed(*values):
    rows = values[0].shape[0]
    columns = sum(v.shape[1] for v in values[::2])
    return ladder(
        call(
            sum_kernel,
            [((rows, columns), BF16)],
            [VMEM] * len(values),
            rows * columns,
            12 * MIB,
        )(*values)[0]
    )


def place(core, own, other, row_halves):
    rows, columns = own.shape
    return call(
        functools.partial(place_kernel, row_halves),
        [((2 * rows, columns) if row_halves else (rows, 2 * columns), F32)],
        [SMEM] + [VMEM] * 2,
        rows * columns,
        14 * MIB,
    )(core.reshape(1), own, other)[0]


def place_kernel(row_halves, core, own, other, out):
    rows, columns = own.shape
    for where, ref in ((core[0], own), (1 - core[0], other)):
        if row_halves:
            out[pl.ds(pl.multiple_of(where * rows, 128), rows), :] = ref[...].astype(F32)
        else:
            out[:, pl.ds(pl.multiple_of(where * columns, 128), columns)] = ref[...].astype(F32)


def call(kernel, outs, in_specs, flops, limit, scratch=(), out_specs=None, aliases=None):
    return pl.pallas_call(
        kernel,
        out_shape=[jax.ShapeDtypeStruct(s, d) for s, d in outs],
        in_specs=in_specs,
        out_specs=out_specs or [VMEM] * len(outs),
        scratch_shapes=list(scratch),
        input_output_aliases=aliases or {},
        compiler_params=pltpu.CompilerParams(vmem_limit_bytes=limit),
        cost_estimate=pl.CostEstimate(
            flops=flops, bytes_accessed=2 * flops // 1000, transcendentals=0
        ),
    )


def part_shapes(n, rows):
    return [((rows, D), BF16)] * (n - 1) + [((rows // 2, D), BF16)] * 2


class Copies:
    def __init__(self, semaphores):
        self.semaphores, self.count, self.out = semaphores, 0, []

    def start(self, source, target):
        copy = pltpu.make_async_copy(source, target, self.semaphores.at[self.count])
        self.count += 1
        copy.start()
        return copy

    def write(self, source, target):
        self.out.append(self.start(source, target))

    def drain(self):
        for copy in self.out:
            copy.wait()


def other_half(core):
    return pl.ds(pl.multiple_of((1 - core[0]) * (D // 2), D // 2), D // 2)


def fetch_pieces(copies, pieces, target, start_of, halved=True):
    rows = pieces[0].shape[0]
    out = []
    for r, piece in enumerate(pieces):
        if halved and r == len(pieces) - 1:
            at = start_of(r - 1) + rows // 2
        else:
            at = start_of(r)
        out.append(copies.start(piece, target.at[pl.ds(at, piece.shape[0]), :]))
    return out


def write_part(copies, buffer, parts, r, halved=True):
    n = len(parts) - halved
    rows = parts[0].shape[0]
    start = r * rows
    if halved and r == n - 1:
        half = rows // 2
        copies.write(buffer.at[pl.ds(start, half), :], parts[n - 1])
        copies.write(buffer.at[pl.ds(start + half, half), :], parts[n])
    else:
        copies.write(buffer.at[pl.ds(start, rows), :], parts[r])


def store_part(parts, r, values):
    n = len(parts) - 1
    if r < n - 1:
        parts[r][...] = values
    else:
        half = values.shape[0] // 2
        parts[n - 1][...] = values[:half]
        parts[n][...] = values[half:]


def assemble(pieces, target, start_of):
    n = len(pieces) - 1
    rows = pieces[0].shape[0]
    half = rows // 2
    for r in range(n - 1):
        target[pl.ds(start_of(r), rows), :] = pieces[r][...]
    start = start_of(n - 1)
    target[pl.ds(start, half), :] = pieces[n - 1][...]
    target[pl.ds(start + half, half), :] = pieces[n][...]


def segment_of(positions, ends):
    return sum((positions >= e).astype(jnp.int32) for e in ends)


def row_ends(lengths):
    first = lengths[0, 0]
    second = first + lengths[0, 1]
    return (first, second, second + lengths[0, 2])


class Block:
    def __init__(self, b, ends):
        start = b * BLOCK
        rows = lax.broadcasted_iota(jnp.int32, (BLOCK, BLOCK), 0)
        columns = lax.broadcasted_iota(jnp.int32, (BLOCK, BLOCK), 1)
        seg_rows = segment_of(rows + start, ends)
        seg_columns = segment_of(columns + start, ends)
        self.mask = jnp.logical_and(seg_rows == seg_columns, rows >= columns)
        self.last = segment_of(start + BLOCK - 1, ends)
        self.earlier = segment_of(start - 1, ends) if b > 0 else -1
        wide_rows = lax.broadcasted_iota(jnp.int32, (BLOCK, HEAD_DIM), 0)
        segments = segment_of(wide_rows + start, ends)
        self.from_state = segments == self.earlier
        self.to_state = segments == self.last

    def decay(self, full):
        return jnp.where(self.mask, full, 0.0)

    def keeping(self, rate):
        factor = jnp.exp(jnp.full((HEAD_DIM, HEAD_DIM), -rate * BLOCK, F32))
        return jnp.where(self.last == self.earlier, factor, 0.0)


def full_decay(rate):
    rows = lax.broadcasted_iota(jnp.int32, (BLOCK, BLOCK), 0)
    columns = lax.broadcasted_iota(jnp.int32, (BLOCK, BLOCK), 1)
    return jnp.exp(-rate * jnp.maximum(rows - columns, 0).astype(F32))


def edge_factors(rate):
    rows = lax.broadcasted_iota(jnp.int32, (BLOCK, HEAD_DIM), 0).astype(F32)
    return jnp.exp(-rate * (rows + 1.0)), jnp.exp(-rate * (BLOCK - 1.0 - rows))


def silu16(values):
    return (values * jax.nn.sigmoid(values)).astype(BF16)


def silu_grad(before):
    sigmoid = jax.nn.sigmoid(before)
    return sigmoid * (1.0 + before * (1.0 - sigmoid))


def entry_kernel(n, heads, order, core, lengths, rates, *refs):
    pieces, refs = refs[: n + 1], refs[n + 1 :]
    weights, mixer, refs = refs[:4], refs[4], refs[5:]
    normed_out, normed_send, proj_out, mixed_out, squares, states_out, refs = *refs[:6], refs[6:]
    parts, refs = refs[: n + 1], refs[n + 1 :]
    normed, weight_in, mixer_in, proj, mixed, pre, states, buffer, semaphores = refs
    copies = Copies(semaphores)
    rows = pieces[0].shape[0]
    total = n * rows
    width = heads * HEAD_DIM
    coming = fetch_pieces(
        copies, pieces, normed, lambda r: pl.multiple_of(order[0, r] * rows, rows)
    )
    for copy in coming:
        copy.wait()
    fetched = [copies.start(w, weight_in.at[i]) for i, w in enumerate(weights)]
    mixer_copy = copies.start(mixer, mixer_in)
    copies.write(normed, normed_out)
    copies.write(normed.at[:, other_half(core)], normed_send)
    for i in range(4):
        fetched[i].wait()
        for b in range(total // BLOCK):
            here = pl.ds(b * BLOCK, BLOCK)
            proj[here, i * width : (i + 1) * width] = dot(normed[here, :], weight_in[i])
    copies.write(proj, proj_out)
    ends = row_ends(lengths)
    fulls = [full_decay(rates[h]) for h in range(heads)]
    edges = [edge_factors(rates[h]) for h in range(heads)]
    state = [jnp.zeros((HEAD_DIM, HEAD_DIM), F32) for _ in range(heads)]
    ones = jnp.ones((8, HEAD_DIM), BF16)
    for b in range(total // BLOCK):
        here = pl.ds(b * BLOCK, BLOCK)
        block = Block(b, ends)
        square = jnp.zeros((8, BLOCK), F32)
        for h in range(heads):
            at = [slice(i * width + h * HEAD_DIM, i * width + (h + 1) * HEAD_DIM) for i in range(4)]
            query, key = silu16(proj[here, at[0]]), silu16(proj[here, at[1]])
            value = proj[here, at[2]].astype(BF16)
            inner, carried = edges[h]
            inner = jnp.where(block.from_state, inner, 0.0)
            carried = jnp.where(block.to_state, carried, 0.0)
            states[b, h] = state[h]
            weight = (dot(query, key, NT) * block.decay(fulls[h])).astype(BF16)
            high, low = split(state[h])
            out = dot(weight, value) + inner * (dot(query, high) + dot(query, low))
            high, low = split(key.astype(F32) * carried)
            state[h] = block.keeping(rates[h]) * state[h] + (
                dot(high, value, TN) + dot(low, value, TN)
            )
            mixed[here, at[0]] = out
            pre[here, at[0]] = (out * proj[here, at[3]]).astype(BF16)
            high, low = split(out * out)
            square += dot(ones, high, NT) + dot(ones, low, NT)
        squares[:, here] = square[0:1]
    copies.write(mixed, mixed_out)
    copies.write(states, states_out)
    mixer_copy.wait()
    for r in reversed(range(0, n, 2)):
        both = jnp.concatenate(
            [pre[pl.ds(pl.multiple_of(order[0, q] * rows, rows), rows), :] for q in (r, r + 1)], 0
        )
        buffer[r * rows : (r + 2) * rows, :] = dot(both, mixer_in[...]).astype(BF16)
        write_part(copies, buffer, parts, r + 1)
        write_part(copies, buffer, parts, r)
    copies.drain()


def column(row):
    return jnp.transpose(jnp.broadcast_to(row, (HEAD_DIM, row.shape[1])))


def exit_kernel(n, heads, order, core, lengths, rates, *refs):
    pieces, refs = refs[: n + 1], refs[n + 1 :]
    weights, mixer_hbm, refs = refs[:4], refs[4], refs[5:]
    proj_hbm, mixed_hbm, states_hbm, inverses, inners, refs = *refs[:5], refs[5:]
    resid_out, bundle, refs = *refs[:2], refs[2:]
    parts, refs = refs[: n + 1], refs[n + 1 :]
    resid, weight_in, mixer, proj, mixed, states, scaled, entry_g, scaled_g, buffer, sems = refs
    copies = Copies(sems)
    rows = pieces[0].shape[0]
    total = n * rows
    width = heads * HEAD_DIM
    mixer_copy = copies.start(mixer_hbm, mixer)
    coming = fetch_pieces(
        copies, pieces, resid, lambda r: pl.multiple_of(order[0, r] * rows, rows)
    )
    mixer_copy.wait()
    for copy in coming:
        copy.wait()
    saved = [
        copies.start(a, b)
        for a, b in ((proj_hbm, proj), (mixed_hbm, mixed), (states_hbm, states))
    ]
    fetched = [copies.start(w, weight_in.at[i]) for i, w in enumerate(weights)]
    copies.write(resid, resid_out)
    copies.write(resid.at[:, other_half(core)], bundle.at[:, pl.ds(5 * width, D // 2)])
    for b in range(total // BLOCK):
        here = pl.ds(b * BLOCK, BLOCK)
        scaled_g[here, :] = dot(resid[here, :], mixer[...], NT)
    for copy in saved:
        copy.wait()
    ends = row_ends(lengths)
    fulls = [full_decay(rates[h]) for h in range(heads)]
    edges = [edge_factors(rates[h]) for h in range(heads)]
    later = [jnp.zeros((HEAD_DIM, HEAD_DIM), F32) for _ in range(heads)]
    for b in reversed(range(total // BLOCK)):
        here = pl.ds(b * BLOCK, BLOCK)
        block = Block(b, ends)
        inverse = column(inverses[:, here])
        mean = column(inners[:, here]) * (1.0 / D)
        for h in range(heads):
            at = [slice(i * width + h * HEAD_DIM, i * width + (h + 1) * HEAD_DIM) for i in range(4)]
            query_pre, key_pre = proj[here, at[0]], proj[here, at[1]]
            query, key = silu16(query_pre), silu16(key_pre)
            value = proj[here, at[2]].astype(BF16)
            gate = proj[here, at[3]]
            grad_s = scaled_g[here, at[0]]
            unit = mixed[here, at[0]] * inverse
            scaled[here, at[0]] = (unit * gate).astype(BF16)
            entry_g[here, at[3]] = (grad_s * unit).astype(BF16)
            grad = (inverse * (grad_s * gate - unit * mean)).astype(BF16)
            inner, carried = edges[h]
            inner = jnp.where(block.from_state, inner, 0.0)
            carried = jnp.where(block.to_state, carried, 0.0)
            decay = block.decay(fulls[h])
            weight = (dot(query, key, NT) * decay).astype(BF16)
            score = (dot(grad, value, NT) * decay).astype(BF16)
            high, low = split(states[b, h])
            query_g = dot(score, key) + inner * (dot(grad, high, NT) + dot(grad, low, NT))
            high, low = split(later[h])
            key_g = dot(score, query, TN) + carried * (dot(value, high, NT) + dot(value, low, NT))
            value_g = dot(weight, grad, TN) + carried * (dot(key, high) + dot(key, low))
            high, low = split(query.astype(F32) * inner)
            later[h] = (
                dot(high, grad, TN) + dot(low, grad, TN) + block.keeping(rates[h]) * later[h]
            )
            entry_g[here, at[0]] = (query_g * silu_grad(query_pre)).astype(BF16)
            entry_g[here, at[1]] = (key_g * silu_grad(key_pre)).astype(BF16)
            entry_g[here, at[2]] = value_g.astype(BF16)
    copies.write(scaled, bundle.at[:, pl.ds(4 * width, width)])
    copies.write(entry_g, bundle.at[:, pl.ds(0, 4 * width)])
    for copy in fetched:
        copy.wait()
    for r in reversed(range(0, n, 2)):
        both = jnp.concatenate(
            [entry_g[pl.ds(pl.multiple_of(order[0, q] * rows, rows), rows), :] for q in (r, r + 1)],
            0,
        )
        buffer[r * rows : (r + 2) * rows, :] = sum(
            dot(both[:, i * width : (i + 1) * width], weight_in[i], NT) for i in range(4)
        ).astype(BF16)
        write_part(copies, buffer, parts, r + 1)
        write_part(copies, buffer, parts, r)
    copies.drain()


def cotangent_kernel(n, core, *refs):
    pieces, down, grad, grad_send, *products = refs[: n + 1], *refs[n + 1 :]
    rows = pieces[0].shape[0]
    assemble(pieces, grad, lambda r: r * rows)
    grad_send[...] = grad[:, other_half(core)]
    for r, out in enumerate(products):
        out[...] = dot(grad[pl.ds(2 * r * rows, 2 * rows), :], down[...], NT)


def hidden_kernel(index, halved, core, *refs):
    count = 2 + halved
    pieces, refs = refs[:count], refs[count:]
    first, second, product_g, refs = *refs[:3], refs[3:]
    refs = refs if index == 0 else refs[4:]
    (normed_out, product_out, second_out, bundle), refs = refs[:4], refs[4:]
    parts, refs = refs[:count], refs[count:]
    normed, product, first_g, second_g, sems = refs
    copies = Copies(sems)
    low = 0
    for piece in pieces:
        normed[low : low + piece.shape[0], :] = piece[...]
        low += piece.shape[0]
    units, padded = first.shape[0], product.shape[1]
    if padded > units:
        for ref in (product, first_g, second_g):
            ref[:, units:] = jnp.zeros((low, padded - units), BF16)
    here = pl.ds(index * low, low)
    copies.write(normed, normed_out.at[here, :])
    copies.write(normed.at[:, other_half(core)], bundle.at[here, pl.ds(padded, D // 2)])
    tokens = normed[...]
    first_act, second_act = dot(tokens, first[...], NT), dot(tokens, second[...], NT)
    product[:, :units] = (first_act * second_act).astype(BF16)
    copies.write(product, product_out.at[here, :])
    grad = product_g[...]
    one, two = (grad * second_act).astype(BF16), (grad * first_act).astype(BF16)
    first_g[:, :units] = one
    copies.write(first_g, bundle.at[here, pl.ds(0, padded)])
    second_g[:, :units] = two
    copies.write(second_g, second_out.at[here, :])
    result = (dot(one, first[...]) + dot(two, second[...])).astype(BF16)
    low = 0
    for part in parts:
        part[...] = result[low : low + part.shape[0]]
        low += part.shape[0]
    copies.drain()


def down_kernel(n, product, down, *parts):
    rows, units = parts[0].shape[0], down.shape[0]
    for r in range(0, n, 2):
        result = dot(product[pl.ds(r * rows, 2 * rows), :units], down[...]).astype(BF16)
        store_part(parts, r, result[:rows])
        store_part(parts, r + 1, result[rows:])


def output_kernel(tokens, attn, ffn, valid_rows, output, sums):
    rows = tokens.shape[0]
    valid = lax.broadcasted_iota(jnp.int32, (rows, 1), 0) < valid_rows[0]
    tokens_wide = tokens[...].astype(F32)
    output[...] = (tokens_wide + attn[...] + ffn[...]).astype(BF16)
    lane = lax.broadcasted_iota(jnp.int32, (1, 128), 1)
    out = jnp.zeros((1, 128), F32)
    for i, values in enumerate((tokens_wide, attn[...], ffn[...])):
        per_row = jnp.sum(values * values, axis=1, keepdims=True)
        whole = jnp.sum(jnp.where(valid, per_row, 0.0), axis=0, keepdims=True)
        out += jnp.where(lane == i, whole, 0.0)
    counted = jnp.clip(valid_rows[0], 0, rows).astype(F32)
    sums[...] = out + jnp.where(lane == 3, counted, 0.0)


def local(
    tokens_in,
    query_weight,
    key_weight,
    value_weight,
    gate_weight,
    mixer_weight,
    first_weight,
    second_weight,
    down_weight,
    doc_lengths,
    head_decay,
    out_grad,
):
    n = lax.axis_size("narrow")
    rows = tokens_in.shape[0]
    total = rows * n
    heads = head_decay.shape[0]
    width = heads * HEAD_DIM
    units = first_weight.shape[1]
    me = lax.axis_index("narrow")
    core = lax.axis_index("wide") % 2
    start_row = me * rows
    order = lax.dynamic_slice(jnp.asarray(order_table(n)), (me, 0), (1, n))
    where = core.reshape(1)
    entry_weights = (query_weight, key_weight, value_weight, gate_weight)
    tokens_wide = tokens_in.astype(F32)
    rates = head_decay

    half_rows = total // 2
    blocks = total // BLOCK
    first_t, second_t = first_weight.T, second_weight.T
    valid_rows = (jnp.sum(doc_lengths[0, : NDOC - 1]) - start_row).reshape(1)

    pieces = Gather(normalize(tokens_wide).astype(BF16), n).finish()
    shapes = [
        ((total, D), BF16),
        ((total, D // 2), BF16),
        ((total, 4 * width), F32),
        ((total, width), F32),
        ((1, total), F32),
        ((blocks, heads, HEAD_DIM, HEAD_DIM), F32),
    ] + part_shapes(n, rows)
    *pieces, grad_own = barrier(*pieces, out_grad)
    cotangent = Gather(grad_own, n).step()
    normed, normed_send, proj, mixed, squares, states, *parts = call(
        functools.partial(entry_kernel, n, heads),
        shapes,
        [SMEM] * 4 + [ANY] * (n + 6),
        12 * total * D * width,
        48 * MIB,
        [
            pltpu.VMEM((total, D), BF16),
            pltpu.VMEM((4, D, width), BF16),
            pltpu.VMEM((width, D), BF16),
            pltpu.VMEM((total, 4 * width), F32),
            pltpu.VMEM((total, width), F32),
            pltpu.VMEM((total, width), BF16),
            pltpu.VMEM((blocks, heads, HEAD_DIM, HEAD_DIM), F32),
            pltpu.VMEM((total, D), BF16),
            pltpu.SemaphoreType.DMA((2 * n + 13,)),
        ],
        [VMEM if i == 4 else ANY for i in range(len(shapes))],
    )(order, where, doc_lengths, rates, *pieces, *entry_weights, mixer_weight)
    squares, cotangent.left, cotangent.right, *parts = barrier(
        squares, cotangent.left, cotangent.right, *parts
    )
    scatter = Scatter(parts, n)
    hop = Butterfly(squares, "narrow")
    while cotangent.left_steps:
        scatter.step()
        cotangent.step()
        hop.step()
        meet(scatter, cotangent, hop)
    squares = hop.finish()
    grad_pieces = cotangent.pieces
    attn_raw, normed_other = barrier(scatter.finish(), swap(normed_send, "wide", 1))
    inverses = lax.rsqrt(squares / D + EPS)
    inverse_own = lax.dynamic_slice(inverses, (0, start_row), (1, rows)).reshape(rows, 1)
    attn_own = attn_raw * inverse_own
    hidden_own = tokens_wide + attn_own

    padded = -(-units // 128) * 128

    def hidden(index, pieces):
        halved = len(pieces) == 3
        count = len(pieces)
        outs = call(
            functools.partial(hidden_kernel, index, halved),
            [((total, D), BF16)]
            + [((total, padded), BF16)] * 2
            + [((total, padded + D // 2), BF16)]
            + [(p.shape, BF16) for p in pieces],
            [SMEM] + [VMEM] * (count + 3) + [ANY] * len(whole),
            16 * rows * D * units,
            40 * MIB,
            [pltpu.VMEM((2 * rows, D), BF16)]
            + [pltpu.VMEM((2 * rows, padded), BF16)] * 3
            + [pltpu.SemaphoreType.DMA((5,))],
            [ANY] * 4 + [VMEM] * count,
            {count + 4 + i: i for i in range(len(whole))},
        )(where, *pieces, first_t, second_t, product_g[index], *whole)
        return outs[:4], list(outs[4:])

    gather = Gather(normalize(hidden_own).astype(BF16), n)
    *grad_pieces, gather.left = barrier(*grad_pieces, gather.left)
    gather.right = gather.left
    gather.step()
    grad_all, grad_send, *product_g = call(
        functools.partial(cotangent_kernel, n),
        [((total, D), BF16), ((total, D // 2), BF16)] + [((2 * rows, units), F32)] * (n // 2),
        [SMEM] + [VMEM] * (n + 2),
        2 * total * D * units,
        22 * MIB,
    )(where, *grad_pieces, down_weight)
    gather.left, gather.right, grad_send, *product_g = barrier(
        gather.left, gather.right, grad_send, *product_g
    )
    whole, parts = [], []
    for i in range(n // 2 - 1):
        pieces = gather.pieces[2 * i : 2 * i + 2]
        gather.step()
        whole, new_parts = hidden(i, pieces)
        if gather.left_steps:
            gather.left, gather.right, *new_parts = barrier(
                gather.left, gather.right, *new_parts
            )
        parts += new_parts
    grad_other = swap(grad_send, "wide", 1)
    pieces = barrier(*gather.pieces[n - 2 :], grad_other)
    grad_other = pieces[-1]
    whole, new_parts = hidden(n // 2 - 1, pieces[:-1])
    parts += new_parts
    normed2, product, second_g, bundle = whole

    scatter = Scatter(parts, n)
    stream = Together(scatter)
    half = D // 2
    step = 3 * half // 8
    cuts = tuple((low, min(half, low + step)) for low in range(0, half, step))

    def first_work(product, grad_all, grad_other):
        other = swap(product, "wide", 1)
        return own_columns(core, cuts, units, product, other, grad_all, grad_other)

    (bundle_other,), down_own = region(
        [stream], [(bundle, "wide", 1)], first_work, [product, grad_all, grad_other]
    )
    (received, second_other_g), first_own = region(
        [stream],
        [(down_own[0], "wide", 2), (second_g, "wide", 1)],
        lambda *v: own_columns(core, cuts, units, *v),
        [bundle, bundle_other, normed2, bundle_other],
    )
    down_in = [received]
    (received,), second_own = region(
        [stream],
        [(down_own[1], "wide", 2)],
        lambda *v: own_columns(core, cuts, units, *v),
        [second_g, second_other_g, normed2, bundle_other],
    )
    down_in.append(received)
    (received,), _ = region([stream], [(down_own[2], "wide", 2)])
    down_in.append(received)
    while scatter.left_steps:
        region([stream])
    normed2_g = scatter.result
    hidden_g = out_grad.astype(F32) + norm_grad(hidden_own, normed2_g)
    resid_own = hidden_g.astype(BF16)
    inner_own = jnp.sum(resid_own.astype(F32) * attn_own, axis=1).reshape(1, rows)
    inners = lax.dynamic_update_slice(jnp.zeros((1, total), F32), inner_own, (0, start_row))

    gather = Gather(resid_own, n)

    def mixed_pairs(owns, ins):
        return [v for pair in zip(owns, ins) for v in pair]

    def output_parts(product, *pairs):
        parts = call(
            functools.partial(down_kernel, n),
            part_shapes(n, rows),
            [VMEM] * 2,
            2 * total * D * units,
            40 * MIB,
        )(product, down_weight)
        return parts, summed(*pairs)

    (received, hop), (parts, down_total) = region(
        [gather],
        [(first_own[0], "wide", 2), (inners, "narrow", 1)],
        output_parts,
        [product, *mixed_pairs(down_own, down_in)],
    )
    first_in, inners = [received], inners + hop
    (received, hop, down_other), _ = region(
        [gather],
        [(first_own[1], "wide", 2), (inners, "narrow", 2), (down_total, "wide", 1)],
    )
    first_in.append(received)
    inners = inners + hop
    (received, hop), down_w = region(
        [gather],
        [(first_own[2], "wide", 2), (inners, "narrow", 4)],
        lambda own, other: place(core, own, other, False),
        [down_total, down_other],
    )
    first_in.append(received)
    inners = inners + hop
    bit = 8
    while gather.left_steps > 1:
        if bit < n:
            (hop,), _ = region([gather], [(inners, "narrow", bit)])
            inners = inners + hop
            bit *= 2
        else:
            region([gather])
    scatter2 = Scatter(parts, n)
    stream2 = Together(scatter2)
    (received,), first_total = region(
        [gather, stream2],
        [(second_own[0], "wide", 2)],
        summed,
        mixed_pairs(first_own, first_in),
    )
    second_in = [received]

    shapes = [
        ((total, D), BF16),
        ((total, 5 * width + D // 2), BF16),
    ] + part_shapes(n, rows)
    leave = call(
        functools.partial(exit_kernel, n, heads),
        shapes,
        [SMEM] * 4 + [ANY] * (n + 9) + [VMEM] * 2,
        12 * total * D * width,
        48 * MIB,
        [
            pltpu.VMEM((total, D), BF16),
            pltpu.VMEM((4, D, width), BF16),
            pltpu.VMEM((width, D), BF16),
            pltpu.VMEM((total, 4 * width), F32),
            pltpu.VMEM((total, width), F32),
            pltpu.VMEM((blocks, heads, HEAD_DIM, HEAD_DIM), F32),
            pltpu.VMEM((total, width), BF16),
            pltpu.VMEM((total, 4 * width), BF16),
            pltpu.VMEM((total, width), F32),
            pltpu.VMEM((total, D), BF16),
            pltpu.SemaphoreType.DMA((2 * n + 15,)),
        ],
        [ANY] * len(shapes),
    )
    (received, first_other), (resid, bundle, *parts) = region(
        [stream2],
        [(second_own[1], "wide", 2), (first_total, "wide", 1)],
        lambda inverses, inners, *pieces: leave(
            order,
            where,
            doc_lengths,
            rates,
            *pieces,
            *entry_weights,
            mixer_weight,
            proj,
            mixed,
            states,
            inverses,
            inners,
        ),
        [inverses, inners, *gather.pieces],
    )
    second_in.append(received)

    scatter = Scatter(parts, n)

    stream = Together(scatter2, scatter)

    def entry_work(bundle, resid, normed, normed_other, *first):
        owns = call(
            entry_sums_kernel,
            [((width, D // 2), BF16)] + [((D // 2, width), BF16)] * 4,
            [SMEM, VMEM, VMEM, ANY, ANY, VMEM],
            10 * total * D * width,
            40 * MIB,
            [pltpu.VMEM((total, D // 2), BF16)] * 2 + [pltpu.SemaphoreType.DMA((2,))],
        )(where, bundle, swap(bundle, "wide", 1), resid, normed, normed_other)
        return owns, place(core, *first, False)

    (received,), ((mixer_own, *owns), first_w) = region(
        [stream],
        [(second_own[2], "wide", 2)],
        entry_work,
        [bundle, resid, normed, normed_other, first_total, first_other],
    )
    second_in.append(received)
    query_own, key_own, value_own, gate_own = owns
    (mixer_in, gate_in), second_total = region(
        [stream],
        [(mixer_own, "wide", 2), (gate_own, "wide", 2)],
        summed,
        mixed_pairs(second_own, second_in),
    )
    while scatter2.left_steps:
        region([stream])
    ffn_own = scatter2.result
    stream = Together(scatter)

    def output_work(tokens_in, attn_own, ffn_own, a, b, c, d):
        output, stats = call(
            output_kernel,
            [((rows, D), BF16), ((1, 128), F32)],
            [VMEM] * 3 + [SMEM],
            6 * rows * D,
            8 * MIB,
        )(tokens_in, attn_own, ffn_own, valid_rows)
        return output, stats, summed(a, b), summed(c, d)

    (value_in, second_other), (output, stats, mixer_total, gate_total) = region(
        [stream],
        [(value_own, "wide", 2), (second_total, "wide", 1)],
        output_work,
        [tokens_in, attn_own, ffn_own, mixer_own, mixer_in, gate_own, gate_in],
    )
    (key_in, mixer_other, gate_other), (second_w, value_total) = region(
        [stream],
        [(key_own, "wide", 2), (mixer_total, "wide", 1), (gate_total, "wide", 1)],
        lambda own, other, *v: (place(core, own, other, False), summed(*v)),
        [second_total, second_other, value_own, value_in],
    )
    while scatter.left_steps:
        region([stream])
    normed_g = scatter.result

    def end_work(stats, normed_g, a, b, *v):
        key_total = summed(a, b)
        key_other = swap(key_total, "wide", 1)
        return (
            Butterfly(stats, "narrow").finish(),
            hidden_g + norm_grad(tokens_wide, normed_g),
            place(core, key_total, key_other, True),
            place(core, *v[:2], False),
            place(core, *v[2:], True),
        )

    (query_in, value_other), (stats, input_grad, key_w, mixer_w, gate_w) = region(
        [],
        [(query_own, "wide", 2), (value_total, "wide", 1)],
        end_work,
        [stats, normed_g, key_own, key_in, mixer_total, mixer_other, gate_total, gate_other],
    )
    query_total = summed(query_own, query_in)
    query_w = place(core, query_total, swap(query_total, "wide", 1), True)
    value_w = place(core, value_total, value_other, True)
    stats = Butterfly(stats, "wide").finish()
    stream_rms = jnp.sqrt(stats[0, :3] / (stats[0, 3] * D))
    return (
        output,
        input_grad,
        query_w,
        key_w,
        value_w,
        gate_w,
        mixer_w,
        first_w.T,
        second_w.T,
        down_w,
        stream_rms,
    )


def solution(mesh):
    split_tokens = P(("wide", "narrow"), None)
    columns, rows = P(None, "narrow"), P("narrow", None)
    return jax.shard_map(
        local,
        mesh=mesh,
        in_specs=(split_tokens,)
        + (columns,) * 4
        + (rows, columns, columns, rows, P("wide", None), P("narrow"), split_tokens),
        out_specs=(split_tokens,) * 2 + (columns,) * 4 + (rows, columns, columns, rows, P()),
        check_vma=False,
    )
```

time: 543 us -> 475 us (0.87)
  Pallas kernels: 57.9 us -> 115 us
  waiting for transfers between devices: 266 us -> 210 us
  other arithmetic: 56.8 us -> 13 us
  matrix products: 24.3 us -> 0 us
    pallas_call x4 -> x38, Pallas kernels: 53.5 us -> 111 us  [the longest x4 17.9 us: hidden(): call(functools.partial(hidden_kernel, index, halved), [((total, D), BF16)...]
    ppermute x32 -> x30, waiting for transfers between devices: 67.2 us -> 22.3 us  [backward(): lax.ppermute(values, 'narrow', [(ring[(i + 1) % n], ring[i]) for i in ran...]
    dot_general x10 -> x0, matrix products: 24.3 us -> none  [dot(): return lax.dot_general(a, b, dims, preferred_element_type=F32)]
    convert_element_type x12 -> x2, other arithmetic: 24.7 us -> 1.37 us  [the longest x1 1.2 us: local(): pieces = Gather(normalize(tokens_wide).astype(BF16), n).finish()]
    ppermute x32 -> x30, starting transfers between devices: 45.4 us -> 35.3 us  [onward(): lax.ppermute(values, 'narrow', [(ring[i], ring[(i + 1) % n]) for i in ran...]
    slice x17 -> x9, local copies, waits for them, and re-layouts: 9.04 us -> 0.73 us  [the longest x1 0.58 us: local(): stream_rms = jnp.sqrt(stats[0, :3] / (stats[0, 3] * D))]
    unnamed x104 -> x202, local copies, waits for them, and re-layouts: 17.8 us -> 25.7 us
    ppermute x32 -> x30, waiting for transfers between devices: 103 us -> 95.6 us  [onward(): lax.ppermute(values, 'narrow', [(ring[i], ring[(i + 1) % n]) for i in ran...]
  transfers between devices with their start and end apart: 90 -> 99, of which waited for: 43 -> 53; matrix products, arithmetic and copies ran while one was open for 18% -> 2% of each run, Pallas kernels for 4% -> 22%
where the time goes in v2:
time: 475 us; the launch traced here: 466 us
  waiting for transfers between devices  210 us (44%)
  Pallas kernels  115 us (24%)
  starting transfers between devices  97.2 us (20%)
  local copies, waits for them, and re-layouts  27.2 us (6%)
  other arithmetic  13 us (3%)
    ppermute x30, waiting for transfers between devices, onward(): lax.ppermute(values, 'narrow', [(ring[i], ring[(i + 1) % n]) for i in ran...  95.6 us
    ppermute x39, waiting for transfers between devices, swap(): return lax.ppermute(values, axis, [(i, i ^ bit) for i in range(size)])  92.1 us
    ppermute x30, starting transfers between devices, onward(): lax.ppermute(values, 'narrow', [(ring[i], ring[(i + 1) % n]) for i in ran...  35.3 us
    ppermute x39, starting transfers between devices, swap(): return lax.ppermute(values, axis, [(i, i ^ bit) for i in range(size)])  31.5 us
    ppermute x30, starting transfers between devices, backward(): lax.ppermute(values, 'narrow', [(ring[(i + 1) % n], ring[i]) for i in ran...  30.4 us
    unnamed x202, local copies, waits for them, and re-layouts  25.7 us
    ppermute x30, waiting for transfers between devices, backward(): lax.ppermute(values, 'narrow', [(ring[(i + 1) % n], ring[i]) for i in ran...  22.3 us
    pallas_call x4, Pallas kernels, hidden(): call(functools.partial(hidden_kernel, index, halved), [((total, D), BF16)...  17.9 us
  transfers between devices with their start and end apart: 99, of which 53 were waited for; matrix products, arithmetic and copies ran while one was open for 2% of the time, Pallas kernels for 22%

profile of v2, /device:TPU:0, one launch (start us, length us, event | category | flops | bytes accessed | tf_op | source)
XLA Modules:
  0.0 465.8 jit_solution(6763423950845090148)
XLA Ops:
  3.2 3.1 collective-permute-start
  6.3 11.8 %collective-permute-done.refs_1_ = bf16[128,2048]{1,0:T(8,128)(2,1)S(1)} collective-permute-done((bf16[128,2048]{1,0:T(8,128)(2,1)S(1)}, bf16[128,2048]{1,0:T(8,128)(2,1)S(1)}, u32[]{:S(2)}, u32[]{:S(2)}) %collective-permute-start) | collective-permute-done | bytes 524320 | tf_op jit(solution)/shard_map/ppermute | solution.py:70
  20.1 11.1 %collective-permute-done.2.refs_3_ = bf16[128,2048]{1,0:T(8,128)(2,1)S(1)} collective-permute-done((bf16[128,2048]{1,0:T(8,128)(2,1)S(1)}, bf16[128,2048]{1,0:T(8,128)(2,1)S(1)}, u32[]{:S(2)}, u32[]{:S(2)}) %collective-permute-start.2) | collective-permute-done | bytes 524320 | tf_op jit(solution)/shard_map/ppermute | solution.py:70
  33.3 10.1 %collective-permute-done.4.refs_5_ = bf16[128,2048]{1,0:T(8,128)(2,1)S(1)} collective-permute-done((bf16[128,2048]{1,0:T(8,128)(2,1)S(1)}, bf16[128,2048]{1,0:T(8,128)(2,1)S(1)}, u32[]{:S(2)}, u32[]{:S(2)}) %collective-permute-start.4) | collective-permute-done | bytes 524320 | tf_op jit(solution)/shard_map/ppermute | solution.py:70
  47.1 2.8 collective-permute-done.6.refs_7_
  49.8 2.4 collective-permute-done.7.refs_8_
  54.3 14.2 %shard_map.212 = (bf16[1024,2048]{1,0:T(8,128)(2,1)}, bf16[1024,1024]{1,0:T(8,128)(2,1)}, f32[1024,1024]{1,0:T(8,128)}, f32[1024,256]{1,0:T(8,128)}, f32[1,1024]...) custom-call(s32[1,8]{1,0:T(1,128)S(1)} %constant_dynamic-slice_fusio, ...), custom_call_target="tpu_custom_call" | custom-call | flops 6442450944 | bytes 12884901 | tf_op jit(solution)/shard_map/pallas_call | solution.py:764
  74.4 12.0 %collective-permute-done.14 = f32[1,1024]{1,0:T(1,128)S(1)} collective-permute-done((f32[1,1024]{1,0:T(1,128)S(1)}, f32[1,1024]{1,0:T(1,128)S(1)}, u32[]{:S(2)}, u32[]{:S(2)}) %collective-permute-start.14) | collective-permute-done | bytes 4128 | tf_op jit(solution)/shard_map/ppermute | solution.py:238
  95.1 7.0 %collective-permute-done.19 = f32[1,1024]{1,0:T(1,128)S(1)} collective-permute-done((f32[1,1024]{1,0:T(1,128)S(1)}, f32[1,1024]{1,0:T(1,128)S(1)}, u32[]{:S(2)}, u32[]{:S(2)}) %collective-permute-start.19) | collective-permute-done | bytes 4128 | tf_op jit(solution)/shard_map/ppermute | solution.py:238
  102.4 4.0 collective-permute-done.17.refs_5_
  106.4 6.0 %collective-permute-done.18.refs_6_ = bf16[128,2048]{1,0:T(8,128)(2,1)S(1)} collective-permute-done((bf16[128,2048]{1,0:T(8,128)(2,1)S(1)}, bf16[128,2048]{1,0:T(8,128)(2,1)S(1)}, u32[]{:S(2)}, u32[]{:S(2)}) %collective-permute-start.18) | collective-permute-done | bytes 524320 | tf_op jit(solution)/shard_map/ppermute | solution.py:75
  114.4 3.5 collective-permute-start.24
  118.3 8.4 %collective-permute-done.24 = f32[1,1024]{1,0:T(1,128)S(1)} collective-permute-done((f32[1,1024]{1,0:T(1,128)S(1)}, f32[1,1024]{1,0:T(1,128)S(1)}, u32[]{:S(2)}, u32[]{:S(2)}) %collective-permute-start.24) | collective-permute-done | bytes 4128 | tf_op jit(solution)/shard_map/ppermute | solution.py:238
  126.7 2.5 collective-permute-start.23
  137.9 10.7 %collective-permute-done.25 = bf16[128,2048]{1,0:T(8,128)(2,1)} collective-permute-done((bf16[128,2048]{1,0:T(8,128)(2,1)}, bf16[128,2048]{1,0:T(8,128)(2,1)}, u32[]{:S(2)}, u32[]{:S(2)}) %collective-permute-start.25) | collective-permute-done | bytes 524320 | tf_op jit(solution)/shard_map/ppermute | solution.py:70
  155.2 3.6 shard_map.215
  160.9 3.4 collective-permute-done.28.refs_1_
  167.6 4.3 shard_map.216
  172.7 7.2 %collective-permute-done.30.refs_1_ = bf16[128,2048]{1,0:T(8,128)(2,1)S(1)} collective-permute-done((bf16[128,2048]{1,0:T(8,128)(2,1)S(1)}, bf16[128,2048]{1,0:T(8,128)(2,1)S(1)}, u32[]{:S(2)}, u32[]{:S(2)}) %collective-permute-start.30) | collective-permute-done | bytes 524320 | tf_op jit(solution)/shard_map/ppermute | solution.py:70
  183.4 4.3 shard_map.217
  187.7 6.9 %collective-permute-done.32.refs_1_ = bf16[128,2048]{1,0:T(8,128)(2,1)S(1)} collective-permute-done((bf16[128,2048]{1,0:T(8,128)(2,1)S(1)}, bf16[128,2048]{1,0:T(8,128)(2,1)S(1)}, u32[]{:S(2)}, u32[]{:S(2)}) %collective-permute-start.32) | collective-permute-done | bytes 524320 | tf_op jit(solution)/shard_map/ppermute | solution.py:70
  197.6 4.3 shard_map.218
  203.5 5.1 %shard_map.219 = (bf16[1024,2048]{1,0:T(8,128)(2,1)}, bf16[1024,768]{1,0:T(8,128)(2,1)S(1)}, bf16[1024,768]{1,0:T(8,128)(2,1)S(1)}, bf16[1024,1792]{1,0:T(8,128)...) custom-call(s32[1]{0:T(128)} %bitcast.core, ...), custom_call_target="tpu_custom_call", output_to_operand_aliasing={{0}: (7, {}), {1}: (8, {}), {2}: (9, {}), {3}: (10, {})} | custom-call | flops 2952790016 | bytes 5905580 | tf_op jit(solution)/shard_map/pallas_call | solution.py:806
  213.1 4.6 collective-permute-done.40.left_other
  225.4 3.8 shard_map.220
  233.6 6.9 %shard_map.222 = (bf16[704,384]{1,0:T(8,128)(2,1)S(1)}, bf16[704,384]{1,0:T(8,128)(2,1)S(1)}, bf16[704,256]{1,0:T(8,128)(2,1)S(1)}) custom-call(s32[1]{0:T(128)} %bitcast.core, bf16[1024,1792]{1,0:T(8,128)(2,1)S(1)} %copy-done.1, bf16[1024,1792]{1,0:T(8,128)(2,1)} %collective-permute-done.39.left_other.right_other, bf16[1024,2048]{1,0:T(8,128)(2,1)S(1)} %copy-done, ...), custom_call_target="tpu_custom_call" | custom-call | flops 2952790016 | bytes 5905580 | tf_op jit(solution)/shard_map/pallas_call | solution.py:282
  240.5 4.5 collective-permute-done.41.refs_2_
  248.7 6.5 %shard_map.224 = (bf16[704,384]{1,0:T(8,128)(2,1)S(1)}, bf16[704,384]{1,0:T(8,128)(2,1)S(1)}, bf16[704,256]{1,0:T(8,128)(2,1)}) custom-call(s32[1]{0:T(128)} %bitcast.core, bf16[1024,768]{1,0:T(8,128)(2,1)S(1)} %get-tuple-element.541.left, bf16[1024,768]{1,0:T(8,128)(2,1)S(1)} %collective-permute-done.44.left_other, bf16[1024,2048]{1,0:T(8,128)(2,1)S(1)} %copy-done, ...), custom_call_target="tpu_custom_call" | custom-call | flops 2952790016 | bytes 5905580 | tf_op jit(solution)/shard_map/pallas_call | solution.py:282
  255.2 4.0 collective-permute-done.45.refs_2_
  263.4 6.1 %collective-permute-done.50.refs_5_ = bf16[704,256]{1,0:T(8,128)(2,1)S(1)} collective-permute-done((bf16[704,256]{1,0:T(8,128)(2,1)S(1)}, bf16[704,256]{1,0:T(8,128)(2,1)S(1)}, u32[]{:S(2)}, u32[]{:S(2)}) %collective-permute-start.50) | collective-permute-done | bytes 360480 | tf_op jit(solution)/shard_map/ppermute | solution.py:238
  278.3 3.4 shard_map.226
  289.0 11.8 %collective-permute-done.58 = f32[1,1024]{1,0:T(1,128)S(1)} collective-permute-done((f32[1,1024]{1,0:T(1,128)S(1)}, f32[1,1024]{1,0:T(1,128)S(1)}, u32[]{:S(2)}, u32[]{:S(2)}) %collective-permute-start.58) | collective-permute-done | bytes 4128 | tf_op jit(solution)/shard_map/ppermute | solution.py:238
  304.2 2.7 collective-permute-start.63
  306.9 2.9 shard_map.228
  309.8 6.5 %collective-permute-done.63 = f32[1,1024]{1,0:T(1,128)S(1)} collective-permute-done((f32[1,1024]{1,0:T(1,128)S(1)}, f32[1,1024]{1,0:T(1,128)S(1)}, u32[]{:S(2)}, u32[]{:S(2)}) %collective-permute-start.63) | collective-permute-done | bytes 4128 | tf_op jit(solution)/shard_map/ppermute | solution.py:238
  323.3 3.5 collective-permute-done.64.refs_7_
  327.2 2.4 collective-permute-done.66.refs_2_
  335.8 16.8 %shard_map.231 = (bf16[1024,2048]{1,0:T(8,128)(2,1)}, bf16[1024,2304]{1,0:T(8,128)(2,1)}, bf16[128,2048]{1,0:T(8,128)(2,1)S(1)}, bf16[128,2048]{1,0:T(8,128)(2,1...) custom-call(s32[1,8]{1,0:T(1,128)S(1)} %constant_dynamic-slice_fusio, ...), custom_call_target="tpu_custom_call" | custom-call | flops 6442450944 | bytes 12884901 | tf_op jit(solution)/shard_map/pallas_call | solution.py:973
  354.3 2.9 shard_map.232
  360.0 2.9 shard_map.234
  362.9 2.6 collective-permute-done.76.bundle_other
  365.5 10.5 %shard_map.233 = (bf16[256,1024]{1,0:T(8,128)(2,1)S(1)}, bf16[1024,256]{1,0:T(8,128)(2,1)S(1)}, bf16[1024,256]{1,0:T(8,128)(2,1)S(1)}, bf16[1024,256]{1,0:T(8,128)(2,1)}, bf16[1024,256]{1,0:T(8,128)(2,1)S(1)}) custom-call(s32[1]{0:T(128)} %bitcast.core, bf16[1024,2304]{1,0:T(8,128)(2,1)} %get-tuple-element.683.bundle, ...), custom_call_target="tpu_custom_call" | custom-call | flops 5368709120 | bytes 10737418 | tf_op jit(solution)/shard_map/pallas_call | solution.py:996
  383.9 11.5 %collective-permute-done.79.refs_1_ = bf16[256,1024]{1,0:T(8,128)(2,1)S(1)} collective-permute-done((bf16[256,1024]{1,0:T(8,128)(2,1)S(1)}, bf16[256,1024]{1,0:T(8,128)(2,1)S(1)}, u32[]{:S(2)}, u32[]{:S(2)}) %collective-permute-start.79) | collective-permute-done | bytes 524320 | tf_op jit(solution)/shard_map/ppermute | solution.py:238
  395.4 9.0 %collective-permute-done.80.refs_1_ = bf16[1024,256]{1,0:T(8,128)(2,1)S(1)} collective-permute-done((bf16[1024,256]{1,0:T(8,128)(2,1)S(1)}, bf16[1024,256]{1,0:T(8,128)(2,1)S(1)}, u32[]{:S(2)}, u32[]{:S(2)}) %collective-permute-start.80) | collective-permute-done | bytes 524320 | tf_op jit(solution)/shard_map/ppermute | solution.py:238
  416.2 5.2 %collective-permute-done.81.refs_2_ = bf16[128,2048]{1,0:T(8,128)(2,1)} collective-permute-done((bf16[128,2048]{1,0:T(8,128)(2,1)}, bf16[128,2048]{1,0:T(8,128)(2,1)}, u32[]{:S(2)}, u32[]{:S(2)}) %collective-permute-start.81) | collective-permute-done | bytes 524320 | tf_op jit(solution)/shard_map/ppermute | solution.py:70
  429.1 4.3 shard_map.242
  433.4 3.7 collective-permute-done.85
  453.4 3.4 collective-permute-done.90.refs_1_
  (437 shorter events, 171.3 us)
Async XLA Ops:
  3.2 14.9 %collective-permute-start = (bf16[128,2048]{1,0:T(8,128)(2,1)S(1)}, bf16[128,2048]{1,0:T(8,128)(2,1)S(1)}, u32[]{:S(2)}, u32[]{:S(2)}) collective-permute-start(bf16[128,2048]{1,0:T(8,128)(2,1)S(1)} %fusion.2.refs_0_), channel_id=1, source_target_pairs={{0,2},{2,4},{4,6},{6,7},{7,5},{5,3},{3,1},{1,0},{8,10},{10,12},{12... | collective-permute-start | bytes 1572872 | tf_op jit(solution)/shard_map/ppermute | solution.py:70
  6.2 13.7 %collective-permute-start.1 = (bf16[128,2048]{1,0:T(8,128)(2,1)S(1)}, bf16[128,2048]{1,0:T(8,128)(2,1)S(1)}, u32[]{:S(2)}, u32[]{:S(2)}) collective-permute-start(bf16[128,2048]{1,0:T(8,128)(2,1)S(1)} %fusion.2.refs_0_), channel_id=1, source_target_pairs={{2,0},{4,2},{6,4},{7,6},{5,7},{3,5},{1,3},{0,1},{10,8},{12,10},{14... | collective-permute-start | bytes 1572872 | tf_op jit(solution)/shard_map/ppermute | solution.py:75
  52.2 17.0 %collective-permute-start.8 = (bf16[128,2048]{1,0:T(8,128)(2,1)S(1)}, bf16[128,2048]{1,0:T(8,128)(2,1)S(1)}, u32[]{:S(2)}, u32[]{:S(2)}) collective-permute-start(bf16[128,2048]{1,0:T(8,128)(2,1)S(1)} %copy-done.19), channel_id=1, source_target_pairs={{0,2},{2,4},{4,6},{6,7},{7,5},{5,3},{3,1},{1,0},{8,10},{10,12},{12... | collective-permute-start | bytes 1572872 | tf_op jit(solution)/shard_map/ppermute | solution.py:70
  53.8 15.4 %collective-permute-start.9 = (bf16[128,2048]{1,0:T(8,128)(2,1)S(1)}, bf16[128,2048]{1,0:T(8,128)(2,1)S(1)}, u32[]{:S(2)}, u32[]{:S(2)}) collective-permute-start(bf16[128,2048]{1,0:T(8,128)(2,1)S(1)} %copy-done.19), channel_id=1, source_target_pairs={{2,0},{4,2},{6,4},{7,6},{5,7},{3,5},{1,3},{0,1},{10,8},{12,10},{14... | collective-permute-start | bytes 1572872 | tf_op jit(solution)/shard_map/ppermute | solution.py:75
  69.3 19.6 %collective-permute-start.12 = (bf16[128,2048]{1,0:T(8,128)(2,1)S(1)}, bf16[128,2048]{1,0:T(8,128)(2,1)S(1)}, u32[]{:S(2)}, u32[]{:S(2)}) collective-permute-start(bf16[128,2048]{1,0:T(8,128)(2,1)S(1)} %collective-permute-done.8.refs_1_), channel_id=1, source_target_pairs={{0,2},{2,4},{4,6},{6,7},{7,5},{5,3},{3,1},{1,0},{8,10},{10,12},{12... | collective-permute-start | bytes 1572872 | tf_op jit(solution)/shard_map/ppermute | solution.py:70
  70.9 18.0 %collective-permute-start.13 = (bf16[128,2048]{1,0:T(8,128)(2,1)S(1)}, bf16[128,2048]{1,0:T(8,128)(2,1)S(1)}, u32[]{:S(2)}, u32[]{:S(2)}) collective-permute-start(bf16[128,2048]{1,0:T(8,128)(2,1)S(1)} %collective-permute-done.9.refs_2_), channel_id=1, source_target_pairs={{2,0},{4,2},{6,4},{7,6},{5,7},{3,5},{1,3},{0,1},{10,8},{12,10},{14... | collective-permute-start | bytes 1572872 | tf_op jit(solution)/shard_map/ppermute | solution.py:75
  71.3 17.3 %collective-permute-start.11 = (bf16[64,2048]{1,0:T(8,128)(2,1)S(1)}, bf16[64,2048]{1,0:T(8,128)(2,1)S(1)}, u32[]{:S(2)}, u32[]{:S(2)}) collective-permute-start(bf16[64,2048]{1,0:T(8,128)(2,1)S(1)} %get-tuple-element.425), channel_id=1, source_target_pairs={{2,0},{4,2},{6,4},{7,6},{5,7},{3,5},{1,3},{0,1},{10,8},{12,10},{14... | collective-permute-start | bytes 786440 | tf_op jit(solution)/shard_map/ppermute | solution.py:75
  72.3 16.4 %collective-permute-start.10 = (bf16[64,2048]{1,0:T(8,128)(2,1)S(1)}, bf16[64,2048]{1,0:T(8,128)(2,1)S(1)}, u32[]{:S(2)}, u32[]{:S(2)}) collective-permute-start(bf16[64,2048]{1,0:T(8,128)(2,1)S(1)} %get-tuple-element.423), channel_id=1, source_target_pairs={{0,2},{2,4},{4,6},{6,7},{7,5},{5,3},{3,1},{1,0},{8,10},{10,12},{12... | collective-permute-start | bytes 786440 | tf_op jit(solution)/shard_map/ppermute | solution.py:70
  93.0 13.3 %collective-permute-start.17 = (bf16[128,2048]{1,0:T(8,128)(2,1)S(1)}, bf16[128,2048]{1,0:T(8,128)(2,1)S(1)}, u32[]{:S(2)}, u32[]{:S(2)}) collective-permute-start(bf16[128,2048]{1,0:T(8,128)(2,1)S(1)} %collective-permute-done.12.refs_3_), channel_id=1, source_target_pairs={{0,2},{2,4},{4,6},{6,7},{7,5},{5,3},{3,1},{1,0},{8,10},{10,12},{12... | collective-permute-start | bytes 1572872 | tf_op jit(solution)/shard_map/ppermute | solution.py:70
  93.1 19.3 %collective-permute-start.18 = (bf16[128,2048]{1,0:T(8,128)(2,1)S(1)}, bf16[128,2048]{1,0:T(8,128)(2,1)S(1)}, u32[]{:S(2)}, u32[]{:S(2)}) collective-permute-start(bf16[128,2048]{1,0:T(8,128)(2,1)S(1)} %collective-permute-done.13.refs_4_), channel_id=1, source_target_pairs={{2,0},{4,2},{6,4},{7,6},{5,7},{3,5},{1,3},{0,1},{10,8},{12,10},{14... | collective-permute-start | bytes 1572872 | tf_op jit(solution)/shard_map/ppermute | solution.py:75
  112.4 16.9 %collective-permute-start.21 = (bf16[128,2048]{1,0:T(8,128)(2,1)S(1)}, bf16[128,2048]{1,0:T(8,128)(2,1)S(1)}, u32[]{:S(2)}, u32[]{:S(2)}) collective-permute-start(bf16[128,2048]{1,0:T(8,128)(2,1)S(1)} %add_convert_fusion.2), channel_id=1, source_target_pairs={{2,0},{4,2},{6,4},{7,6},{5,7},{3,5},{1,3},{0,1},{10,8},{12,10},{14... | collective-permute-start | bytes 1572872 | tf_op jit(solution)/shard_map/ppermute | solution.py:75
  112.5 38.8 %collective-permute-start.27 = (bf16[1024,1024]{1,0:T(8,128)(2,1)}, bf16[1024,1024]{1,0:T(8,128)(2,1)S(1)}, u32[]{:S(2)}, u32[]{:S(2)}) collective-permute-start(bf16[1024,1024]{1,0:T(8,128)(2,1)} %get-tuple-element.443), channel_id=1, source_target_pairs={{0,8},{8,0},{16,24},{24,16},{1,9},{9,1},{17,25},{25,17},{2,10},{10... | collective-permute-start | bytes 6291464 | tf_op jit(solution)/shard_map/ppermute | solution.py:238
  112.5 17.8 %collective-permute-start.20 = (bf16[128,2048]{1,0:T(8,128)(2,1)S(1)}, bf16[128,2048]{1,0:T(8,128)(2,1)S(1)}, u32[]{:S(2)}, u32[]{:S(2)}) collective-permute-start(bf16[128,2048]{1,0:T(8,128)(2,1)S(1)} %add_convert_fusion.3), channel_id=1, source_target_pairs={{0,2},{2,4},{4,6},{6,7},{7,5},{5,3},{3,1},{1,0},{8,10},{10,12},{12... | collective-permute-start | bytes 1572872 | tf_op jit(solution)/shard_map/ppermute | solution.py:70
  117.9 14.5 %collective-permute-start.22 = (bf16[64,2048]{1,0:T(8,128)(2,1)S(1)}, bf16[64,2048]{1,0:T(8,128)(2,1)S(1)}, u32[]{:S(2)}, u32[]{:S(2)}) collective-permute-start(bf16[64,2048]{1,0:T(8,128)(2,1)S(1)} %slice.41), channel_id=1, source_target_pairs={{0,2},{2,4},{4,6},{6,7},{7,5},{5,3},{3,1},{1,0},{8,10},{10,12},{12... | collective-permute-start | bytes 786440 | tf_op jit(solution)/shard_map/ppermute | solution.py:70
  135.2 13.4 %collective-permute-start.25 = (bf16[128,2048]{1,0:T(8,128)(2,1)}, bf16[128,2048]{1,0:T(8,128)(2,1)}, u32[]{:S(2)}, u32[]{:S(2)}) collective-permute-start(bf16[128,2048]{1,0:T(8,128)(2,1)} %add_convert_fusion.1), channel_id=1, source_target_pairs={{0,2},{2,4},{4,6},{6,7},{7,5},{5,3},{3,1},{1,0},{8,10},{10,12},{12... | collective-permute-start | bytes 1572872 | tf_op jit(solution)/shard_map/ppermute | solution.py:70
  165.6 37.9 %collective-permute-start.36 = (bf16[1024,1024]{1,0:T(8,128)(2,1)S(1)}, bf16[1024,1024]{1,0:T(8,128)(2,1)S(1)}, u32[]{:S(2)}, u32[]{:S(2)}) collective-permute-start(bf16[1024,1024]{1,0:T(8,128)(2,1)S(1)} %get-tuple-element.487), channel_id=1, source_target_pairs={{0,8},{8,0},{16,24},{24,16},{1,9},{9,1},{17,25},{25,17},{2,10},{10... | collective-permute-start | bytes 6291464 | tf_op jit(solution)/shard_map/ppermute | solution.py:238
  165.6 14.3 %collective-permute-start.30 = (bf16[128,2048]{1,0:T(8,128)(2,1)S(1)}, bf16[128,2048]{1,0:T(8,128)(2,1)S(1)}, u32[]{:S(2)}, u32[]{:S(2)}) collective-permute-start(bf16[128,2048]{1,0:T(8,128)(2,1)S(1)} %collective-permute-done.28.refs_1_), channel_id=1, source_target_pairs={{0,2},{2,4},{4,6},{6,7},{7,5},{5,3},{3,1},{1,0},{8,10},{10,12},{12... | collective-permute-start | bytes 1572872 | tf_op jit(solution)/shard_map/ppermute | solution.py:70
  167.3 14.1 %collective-permute-start.31 = (bf16[128,2048]{1,0:T(8,128)(2,1)S(1)}, bf16[128,2048]{1,0:T(8,128)(2,1)S(1)}, u32[]{:S(2)}, u32[]{:S(2)}) collective-permute-start(bf16[128,2048]{1,0:T(8,128)(2,1)S(1)} %collective-permute-done.29.refs_0_), channel_id=1, source_target_pairs={{2,0},{4,2},{6,4},{7,6},{5,7},{3,5},{1,3},{0,1},{10,8},{12,10},{14... | collective-permute-start | bytes 1572872 | tf_op jit(solution)/shard_map/ppermute | solution.py:75
  209.4 19.8 %collective-permute-start.39 = (bf16[1024,1792]{1,0:T(8,128)(2,1)}, bf16[1024,1792]{1,0:T(8,128)(2,1)}, u32[]{:S(2)}, u32[]{:S(2)}) collective-permute-start(bf16[1024,1792]{1,0:T(8,128)(2,1)} %get-tuple-element.525.left), channel_id=1, source_target_pairs={{0,8},{8,0},{16,24},{24,16},{1,9},{9,1},{17,25},{25,17},{2,10},{10... | collective-permute-start | bytes 11010056 | tf_op jit(solution)/shard_map/ppermute | solution.py:238
  211.1 18.2 %collective-permute-start.37 = (bf16[64,2048]{1,0:T(8,128)(2,1)}, bf16[64,2048]{1,0:T(8,128)(2,1)S(1)}, u32[]{:S(2)}, u32[]{:S(2)}) collective-permute-start(bf16[64,2048]{1,0:T(8,128)(2,1)} %get-tuple-element.504), channel_id=1, source_target_pairs={{0,2},{2,4},{4,6},{6,7},{7,5},{5,3},{3,1},{1,0},{8,10},{10,12},{12... | collective-permute-start | bytes 786440 | tf_op jit(solution)/shard_map/ppermute | solution.py:70
  211.8 17.4 %collective-permute-start.38 = (bf16[64,2048]{1,0:T(8,128)(2,1)}, bf16[64,2048]{1,0:T(8,128)(2,1)S(1)}, u32[]{:S(2)}, u32[]{:S(2)}) collective-permute-start(bf16[64,2048]{1,0:T(8,128)(2,1)} %get-tuple-element.505), channel_id=1, source_target_pairs={{2,0},{4,2},{6,4},{7,6},{5,7},{3,5},{1,3},{0,1},{10,8},{12,10},{14... | collective-permute-start | bytes 786440 | tf_op jit(solution)/shard_map/ppermute | solution.py:75
  229.4 16.1 %collective-permute-start.44 = (bf16[1024,768]{1,0:T(8,128)(2,1)S(1)}, bf16[1024,768]{1,0:T(8,128)(2,1)S(1)}, u32[]{:S(2)}, u32[]{:S(2)}) collective-permute-start(bf16[1024,768]{1,0:T(8,128)(2,1)S(1)} %get-tuple-element.541.left), channel_id=1, source_target_pairs={{0,8},{8,0},{16,24},{24,16},{1,9},{9,1},{17,25},{25,17},{2,10},{10... | collective-permute-start | bytes 4718600 | tf_op jit(solution)/shard_map/ppermute | solution.py:238
  229.9 15.7 %collective-permute-start.43 = (bf16[704,384]{1,0:T(8,128)(2,1)}, bf16[704,384]{1,0:T(8,128)(2,1)S(1)}, u32[]{:S(2)}, u32[]{:S(2)}) collective-permute-start(bf16[704,384]{1,0:T(8,128)(2,1)} %get-tuple-element.576.refs_0_), channel_id=1, source_target_pairs={{0,16},{8,24},{16,0},{24,8},{1,17},{9,25},{17,1},{25,9},{2,18},{10... | collective-permute-start | bytes 1622024 | tf_op jit(solution)/shard_map/ppermute | solution.py:238
  231.4 13.7 %collective-permute-start.41 = (bf16[128,2048]{1,0:T(8,128)(2,1)S(1)}, bf16[128,2048]{1,0:T(8,128)(2,1)S(1)}, u32[]{:S(2)}, u32[]{:S(2)}) collective-permute-start(bf16[128,2048]{1,0:T(8,128)(2,1)S(1)} %get-tuple-element.521), channel_id=1, source_target_pairs={{0,2},{2,4},{4,6},{6,7},{7,5},{5,3},{3,1},{1,0},{8,10},{10,12},{12... | collective-permute-start | bytes 1572872 | tf_op jit(solution)/shard_map/ppermute | solution.py:70
  232.0 13.6 %collective-permute-start.42 = (bf16[128,2048]{1,0:T(8,128)(2,1)S(1)}, bf16[128,2048]{1,0:T(8,128)(2,1)S(1)}, u32[]{:S(2)}, u32[]{:S(2)}) collective-permute-start(bf16[128,2048]{1,0:T(8,128)(2,1)S(1)} %get-tuple-element.522), channel_id=1, source_target_pairs={{2,0},{4,2},{6,4},{7,6},{5,7},{3,5},{1,3},{0,1},{10,8},{12,10},{14... | collective-permute-start | bytes 1572872 | tf_op jit(solution)/shard_map/ppermute | solution.py:75
  245.9 13.9 %collective-permute-start.47 = (bf16[704,384]{1,0:T(8,128)(2,1)S(1)}, bf16[704,384]{1,0:T(8,128)(2,1)S(1)}, u32[]{:S(2)}, u32[]{:S(2)}) collective-permute-start(bf16[704,384]{1,0:T(8,128)(2,1)S(1)} %copy-done.16), channel_id=1, source_target_pairs={{0,16},{8,24},{16,0},{24,8},{1,17},{9,25},{17,1},{25,9},{2,18},{10... | collective-permute-start | bytes 1622024 | tf_op jit(solution)/shard_map/ppermute | solution.py:238
  285.5 15.3 %collective-permute-start.59 = (bf16[704,1024]{1,0:T(8,128)(2,1)S(1)}, bf16[704,1024]{1,0:T(8,128)(2,1)S(1)}, u32[]{:S(2)}, u32[]{:S(2)}) collective-permute-start(bf16[704,1024]{1,0:T(8,128)(2,1)S(1)} %shard_map.227.own), channel_id=1, source_target_pairs={{0,8},{8,0},{16,24},{24,16},{1,9},{9,1},{17,25},{25,17},{2,10},{10... | collective-permute-start | bytes 4325384 | tf_op jit(solution)/shard_map/ppermute | solution.py:238
  285.6 15.2 %collective-permute-start.57 = (bf16[704,384]{1,0:T(8,128)(2,1)S(1)}, bf16[704,384]{1,0:T(8,128)(2,1)S(1)}, u32[]{:S(2)}, u32[]{:S(2)}) collective-permute-start(bf16[704,384]{1,0:T(8,128)(2,1)S(1)} %copy-done.14), channel_id=1, source_target_pairs={{0,16},{8,24},{16,0},{24,8},{1,17},{9,25},{17,1},{25,9},{2,18},{10... | collective-permute-start | bytes 1622024 | tf_op jit(solution)/shard_map/ppermute | solution.py:238
  286.0 14.8 %collective-permute-start.55 = (bf16[128,2048]{1,0:T(8,128)(2,1)S(1)}, bf16[128,2048]{1,0:T(8,128)(2,1)S(1)}, u32[]{:S(2)}, u32[]{:S(2)}) collective-permute-start(bf16[128,2048]{1,0:T(8,128)(2,1)S(1)} %collective-permute-done.51.refs_1_), channel_id=1, source_target_pairs={{0,2},{2,4},{4,6},{6,7},{7,5},{5,3},{3,1},{1,0},{8,10},{10,12},{12... | collective-permute-start | bytes 1572872 | tf_op jit(solution)/shard_map/ppermute | solution.py:70
  287.0 13.8 %collective-permute-start.56 = (bf16[128,2048]{1,0:T(8,128)(2,1)S(1)}, bf16[128,2048]{1,0:T(8,128)(2,1)S(1)}, u32[]{:S(2)}, u32[]{:S(2)}) collective-permute-start(bf16[128,2048]{1,0:T(8,128)(2,1)S(1)} %collective-permute-done.52.refs_2_), channel_id=1, source_target_pairs={{2,0},{4,2},{6,4},{7,6},{5,7},{3,5},{1,3},{0,1},{10,8},{12,10},{14... | collective-permute-start | bytes 1572872 | tf_op jit(solution)/shard_map/ppermute | solution.py:75
  300.9 15.5 %collective-permute-start.60 = (bf16[128,2048]{1,0:T(8,128)(2,1)S(1)}, bf16[128,2048]{1,0:T(8,128)(2,1)S(1)}, u32[]{:S(2)}, u32[]{:S(2)}) collective-permute-start(bf16[128,2048]{1,0:T(8,128)(2,1)S(1)} %collective-permute-done.55.refs_3_), channel_id=1, source_target_pairs={{0,2},{2,4},{4,6},{6,7},{7,5},{5,3},{3,1},{1,0},{8,10},{10,12},{12... | collective-permute-start | bytes 1572872 | tf_op jit(solution)/shard_map/ppermute | solution.py:70
  302.4 14.0 %collective-permute-start.61 = (bf16[128,2048]{1,0:T(8,128)(2,1)S(1)}, bf16[128,2048]{1,0:T(8,128)(2,1)S(1)}, u32[]{:S(2)}, u32[]{:S(2)}) collective-permute-start(bf16[128,2048]{1,0:T(8,128)(2,1)S(1)} %collective-permute-done.56.refs_4_), channel_id=1, source_target_pairs={{2,0},{4,2},{6,4},{7,6},{5,7},{3,5},{1,3},{0,1},{10,8},{12,10},{14... | collective-permute-start | bytes 1572872 | tf_op jit(solution)/shard_map/ppermute | solution.py:75
  302.9 13.4 %collective-permute-start.62 = (bf16[704,256]{1,0:T(8,128)(2,1)S(1)}, bf16[704,256]{1,0:T(8,128)(2,1)S(1)}, u32[]{:S(2)}, u32[]{:S(2)}) collective-permute-start(bf16[704,256]{1,0:T(8,128)(2,1)S(1)} %get-tuple-element.622.refs_4_), channel_id=1, source_target_pairs={{0,16},{8,24},{16,0},{24,8},{1,17},{9,25},{17,1},{25,9},{2,18},{10... | collective-permute-start | bytes 1081352 | tf_op jit(solution)/shard_map/ppermute | solution.py:238
  331.1 23.2 %collective-permute-start.72 = (bf16[704,1024]{1,0:T(8,128)(2,1)S(1)}, bf16[704,1024]{1,0:T(8,128)(2,1)S(1)}, u32[]{:S(2)}, u32[]{:S(2)}) collective-permute-start(bf16[704,1024]{1,0:T(8,128)(2,1)S(1)} %shard_map.229.own), channel_id=1, source_target_pairs={{0,8},{8,0},{16,24},{24,16},{1,9},{9,1},{17,25},{25,17},{2,10},{10... | collective-permute-start | bytes 4325384 | tf_op jit(solution)/shard_map/ppermute | solution.py:238
  331.1 23.1 %collective-permute-start.71 = (bf16[704,384]{1,0:T(8,128)(2,1)S(1)}, bf16[704,384]{1,0:T(8,128)(2,1)S(1)}, u32[]{:S(2)}, u32[]{:S(2)}) collective-permute-start(bf16[704,384]{1,0:T(8,128)(2,1)S(1)} %get-tuple-element.711.refs_2_), channel_id=1, source_target_pairs={{0,16},{8,24},{16,0},{24,8},{1,17},{9,25},{17,1},{25,9},{2,18},{10... | collective-permute-start | bytes 1622024 | tf_op jit(solution)/shard_map/ppermute | solution.py:238
  332.8 21.4 %collective-permute-start.69 = (bf16[128,2048]{1,0:T(8,128)(2,1)}, bf16[128,2048]{1,0:T(8,128)(2,1)S(1)}, u32[]{:S(2)}, u32[]{:S(2)}) collective-permute-start(bf16[128,2048]{1,0:T(8,128)(2,1)} %get-tuple-element.633), channel_id=1, source_target_pairs={{0,2},{2,4},{4,6},{6,7},{7,5},{5,3},{3,1},{1,0},{8,10},{10,12},{12... | collective-permute-start | bytes 1572872 | tf_op jit(solution)/shard_map/ppermute | solution.py:70
  333.4 20.8 %collective-permute-start.70 = (bf16[128,2048]{1,0:T(8,128)(2,1)}, bf16[128,2048]{1,0:T(8,128)(2,1)}, u32[]{:S(2)}, u32[]{:S(2)}) collective-permute-start(bf16[128,2048]{1,0:T(8,128)(2,1)} %get-tuple-element.634), channel_id=1, source_target_pairs={{2,0},{4,2},{6,4},{7,6},{5,7},{3,5},{1,3},{0,1},{10,8},{12,10},{14... | collective-permute-start | bytes 1572872 | tf_op jit(solution)/shard_map/ppermute | solution.py:75
  357.3 20.2 %collective-permute-start.73 = (bf16[192,2048]{1,0:T(8,128)(2,1)}, bf16[192,2048]{1,0:T(8,128)(2,1)S(1)}, u32[]{:S(2)}, u32[]{:S(2)}) collective-permute-start(bf16[192,2048]{1,0:T(8,128)(2,1)} %get-tuple-element.680), channel_id=1, source_target_pairs={{0,2},{2,4},{4,6},{6,7},{7,5},{5,3},{3,1},{1,0},{8,10},{10,12},{12... | collective-permute-start | bytes 2359304 | tf_op jit(solution)/shard_map/ppermute | solution.py:70
  358.0 20.1 %collective-permute-start.74 = (bf16[192,2048]{1,0:T(8,128)(2,1)}, bf16[192,2048]{1,0:T(8,128)(2,1)S(1)}, u32[]{:S(2)}, u32[]{:S(2)}) collective-permute-start(bf16[192,2048]{1,0:T(8,128)(2,1)} %get-tuple-element.681), channel_id=1, source_target_pairs={{2,0},{4,2},{6,4},{7,6},{5,7},{3,5},{1,3},{0,1},{10,8},{12,10},{14... | collective-permute-start | bytes 2359304 | tf_op jit(solution)/shard_map/ppermute | solution.py:75
  359.6 16.5 %collective-permute-start.75 = (bf16[704,256]{1,0:T(8,128)(2,1)}, bf16[704,256]{1,0:T(8,128)(2,1)S(1)}, u32[]{:S(2)}, u32[]{:S(2)}) collective-permute-start(bf16[704,256]{1,0:T(8,128)(2,1)} %get-tuple-element.713.refs_4_), channel_id=1, source_target_pairs={{0,16},{8,24},{16,0},{24,8},{1,17},{9,25},{17,1},{25,9},{2,18},{10... | collective-permute-start | bytes 1081352 | tf_op jit(solution)/shard_map/ppermute | solution.py:238
  378.4 25.9 %collective-permute-start.77 = (bf16[256,2048]{1,0:T(8,128)(2,1)S(1)}, bf16[256,2048]{1,0:T(8,128)(2,1)S(1)}, u32[]{:S(2)}, u32[]{:S(2)}) collective-permute-start(bf16[256,2048]{1,0:T(8,128)(2,1)S(1)} %get-tuple-element.705), channel_id=1, source_target_pairs={{0,2},{2,4},{4,6},{6,7},{7,5},{5,3},{3,1},{1,0},{8,10},{10,12},{12... | collective-permute-start | bytes 3145736 | tf_op jit(solution)/shard_map/ppermute | solution.py:70
  379.2 25.1 %collective-permute-start.78 = (bf16[256,2048]{1,0:T(8,128)(2,1)S(1)}, bf16[256,2048]{1,0:T(8,128)(2,1)S(1)}, u32[]{:S(2)}, u32[]{:S(2)}) collective-permute-start(bf16[256,2048]{1,0:T(8,128)(2,1)S(1)} %get-tuple-element.706), channel_id=1, source_target_pairs={{2,0},{4,2},{6,4},{7,6},{5,7},{3,5},{1,3},{0,1},{10,8},{12,10},{14... | collective-permute-start | bytes 3145736 | tf_op jit(solution)/shard_map/ppermute | solution.py:75
  380.5 14.9 %collective-permute-start.79 = (bf16[256,1024]{1,0:T(8,128)(2,1)S(1)}, bf16[256,1024]{1,0:T(8,128)(2,1)S(1)}, u32[]{:S(2)}, u32[]{:S(2)}) collective-permute-start(bf16[256,1024]{1,0:T(8,128)(2,1)S(1)} %get-tuple-element.733.refs_0_), channel_id=1, source_target_pairs={{0,16},{8,24},{16,0},{24,8},{1,17},{9,25},{17,1},{25,9},{2,18},{10... | collective-permute-start | bytes 1572872 | tf_op jit(solution)/shard_map/ppermute | solution.py:238
  381.0 23.4 %collective-permute-start.80 = (bf16[1024,256]{1,0:T(8,128)(2,1)S(1)}, bf16[1024,256]{1,0:T(8,128)(2,1)S(1)}, u32[]{:S(2)}, u32[]{:S(2)}) collective-permute-start(bf16[1024,256]{1,0:T(8,128)(2,1)S(1)} %get-tuple-element.735.refs_0_), channel_id=1, source_target_pairs={{0,16},{8,24},{16,0},{24,8},{1,17},{9,25},{17,1},{25,9},{2,18},{10... | collective-permute-start | bytes 1572872 | tf_op jit(solution)/shard_map/ppermute | solution.py:238
  406.7 16.1 %collective-permute-start.84 = (bf16[704,1024]{1,0:T(8,128)(2,1)S(1)}, bf16[704,1024]{1,0:T(8,128)(2,1)}, u32[]{:S(2)}, u32[]{:S(2)}) collective-permute-start(bf16[704,1024]{1,0:T(8,128)(2,1)S(1)} %shard_map.236.own), channel_id=1, source_target_pairs={{0,8},{8,0},{16,24},{24,16},{1,9},{9,1},{17,25},{25,17},{2,10},{10... | collective-permute-start | bytes 4325384 | tf_op jit(solution)/shard_map/ppermute | solution.py:238
  406.7 14.7 %collective-permute-start.81 = (bf16[128,2048]{1,0:T(8,128)(2,1)}, bf16[128,2048]{1,0:T(8,128)(2,1)}, u32[]{:S(2)}, u32[]{:S(2)}) collective-permute-start(bf16[128,2048]{1,0:T(8,128)(2,1)} %get-tuple-element.724), channel_id=1, source_target_pairs={{0,2},{2,4},{4,6},{6,7},{7,5},{5,3},{3,1},{1,0},{8,10},{10,12},{12... | collective-permute-start | bytes 1572872 | tf_op jit(solution)/shard_map/ppermute | solution.py:70
  407.5 14.3 %collective-permute-start.82 = (bf16[128,2048]{1,0:T(8,128)(2,1)}, bf16[128,2048]{1,0:T(8,128)(2,1)}, u32[]{:S(2)}, u32[]{:S(2)}) collective-permute-start(bf16[128,2048]{1,0:T(8,128)(2,1)} %get-tuple-element.725), channel_id=1, source_target_pairs={{2,0},{4,2},{6,4},{7,6},{5,7},{3,5},{1,3},{0,1},{10,8},{12,10},{14... | collective-permute-start | bytes 1572872 | tf_op jit(solution)/shard_map/ppermute | solution.py:75
  408.8 14.0 %collective-permute-start.83 = (bf16[1024,256]{1,0:T(8,128)(2,1)}, bf16[1024,256]{1,0:T(8,128)(2,1)}, u32[]{:S(2)}, u32[]{:S(2)}) collective-permute-start(bf16[1024,256]{1,0:T(8,128)(2,1)} %get-tuple-element.757.refs_0_), channel_id=1, source_target_pairs={{0,16},{8,24},{16,0},{24,8},{1,17},{9,25},{17,1},{25,9},{2,18},{10... | collective-permute-start | bytes 1572872 | tf_op jit(solution)/shard_map/ppermute | solution.py:238
  (152 other events, 1565.5 us)

commit v3 on v2

--- a/solution.py
+++ b/solution.py
@@ -173,7 +173,7 @@
                         [(shape, BF16)],
                         [VMEM] * 2,
                         shape[0] * shape[1],
-                        4 * MIB,
+                        14 * MIB,
                     )(near, part)[0]
                     for low, near, part in ((0, self.near[k], left), (half, self.near[-k], right))
                 ]
@@ -201,7 +201,7 @@
             [((rows, D), BF16)] * 2,
             [VMEM] * len(operands),
             2 * rows * D,
-            10 * MIB,
+            14 * MIB,
         )(*operands)
 
     def incoming(self, left, right):
@@ -265,48 +265,84 @@
     return pl.ds(pl.multiple_of(core[0] * (D // 2), D // 2), D // 2)
 
 
-def columns_kernel(cuts, width, right_low, core, left, left_other, right_hbm, right_other, *refs):
-    outs, right, semaphores = refs[:-2], refs[-2], refs[-1]
+def columns_kernel(cuts, lefts, rights, core, *refs):
+    sources, outs, refs = refs[:4], refs[4 : 4 + len(cuts)], refs[4 + len(cuts) :]
+    left, left_other, right, right_other, semaphores = refs
+    width = outs[0].shape[0]
+    columns = right.shape[1]
     copies = Copies(semaphores)
-    coming = copies.start(right_hbm.at[:, own_half(core)], right)
-    other = right_other[:, right_low : right_low + D // 2]
-    part = dot(left_other[:, :width], other, TN)
-    coming.wait()
+    coming = [
+        copies.start(sources[1].at[:, pl.ds(lefts[1], left.shape[1])], left_other),
+        copies.start(sources[3].at[:, pl.ds(rights[1], columns)], right_other),
+        copies.start(sources[0].at[:, pl.ds(lefts[0], left.shape[1])], left),
+    ]
+    if rights[0] is None:
+        coming.append(copies.start(sources[2].at[:, own_half(core)], right))
+    else:
+        coming.append(copies.start(sources[2].at[:, pl.ds(rights[0], columns)], right))
+    coming[0].wait()
+    coming[1].wait()
+    part = dot(left_other[:, :width], right_other[...], TN)
+    coming[2].wait()
+    coming[3].wait()
     part += dot(left[:, :width], right[...], TN)
     for out, (low, high) in zip(outs, cuts):
         out[...] = part[:, low:high].astype(BF16)
 
 
-def own_columns(core, cuts, width, left, left_other, right, right_other):
+def own_columns(core, cuts, width, left, left_other, right, right_other, lefts=(0, 0), low=0):
     total = left.shape[0]
+    padded = -(-width // 128) * 128
     return call(
-        functools.partial(columns_kernel, cuts, width, right_other.shape[1] - D // 2),
+        functools.partial(columns_kernel, cuts, lefts, (None, low)),
         [((width, high - low), BF16) for low, high in cuts],
-        [SMEM, VMEM, VMEM, ANY, VMEM],
+        [SMEM] + [ANY] * 4,
         2 * total * D * width,
-        40 * MIB,
-        [pltpu.VMEM((total, D // 2), BF16), pltpu.SemaphoreType.DMA((1,))],
+        54 * MIB,
+        [pltpu.VMEM((total, padded), BF16)] * 2
+        + [pltpu.VMEM((total, D // 2), BF16)] * 2
+        + [pltpu.SemaphoreType.DMA((4,))],
     )(core.reshape(1), left, left_other, right, right_other)
 
 
-def entry_sums_kernel(
-    core, bundle, bundle_other, resid_hbm, normed_hbm, normed_other, mixer_out, *refs
-):
-    outs, (resid, normed, semaphores) = refs[:4], refs[4:]
-    width = mixer_out.shape[0]
+def rows_kernel(first, core, *refs):
+    sources, refs = refs[:4], refs[4:]
+    outs, (normed, normed_other, grads, grads_other, semaphores) = refs[:-5], refs[-5:]
+    width = outs[0].shape[1]
+    columns = pl.ds(first * width, len(outs) * width)
     copies = Copies(semaphores)
-    first = copies.start(normed_hbm.at[:, own_half(core)], normed)
-    second = copies.start(resid_hbm.at[:, own_half(core)], resid)
-    for i in (3, 2, 1, 0):
-        at = slice(i * width, (i + 1) * width)
-        part = dot(normed_other[...], bundle_other[:, at], TN)
-        if i == 3:
-            first.wait()
-        outs[i][...] = (part + dot(normed[...], bundle[:, at], TN)).astype(BF16)
-    at, half = slice(4 * width, 5 * width), slice(5 * width, 5 * width + D // 2)
-    part = dot(bundle_other[:, at], bundle_other[:, half], TN)
-    second.wait()
-    mixer_out[...] = (part + dot(bundle[:, at], resid[...], TN)).astype(BF16)
+    coming = [
+        copies.start(sources[1], normed_other),
+        copies.start(sources[3].at[:, columns], grads_other),
+        copies.start(sources[0].at[:, own_half(core)], normed),
+        copies.start(sources[2].at[:, columns], grads),
+    ]
+    coming[0].wait()
+    coming[1].wait()
+    part = dot(normed_other[...], grads_other[...], TN)
+    coming[2].wait()
+    coming[3].wait()
+    part += dot(normed[...], grads[...], TN)
+    for i, out in enumerate(outs):
+        out[...] = part[:, i * width : (i + 1) * width].astype(BF16)
+
+
+def own_rows(core, first, count, width, normed, normed_other, bundle, bundle_other):
+    total = normed.shape[0]
+    return call(
+        functools.partial(rows_kernel, first),
+        [((D // 2, width), BF16)] * count,
+        [SMEM] + [ANY] * 4,
+        2 * total * D * width * count,
+        54 * MIB,
+        [pltpu.VMEM((total, D // 2), BF16)] * 2
+        + [pltpu.VMEM((total, count * width), BF16)] * 2
+        + [pltpu.SemaphoreType.DMA((4,))],
+    )(core.reshape(1), normed, normed_other, bundle, bundle_other)
+
+
+def add_kernel(keep, crossed, out):
+    out[...] = (keep[...] + crossed[...].astype(F32)).astype(BF16)
 
 
 def sum_kernel(*refs):
@@ -326,7 +362,7 @@
             [((rows, columns), BF16)],
             [VMEM] * len(values),
             rows * columns,
-            12 * MIB,
+            14 * MIB,
         )(*values)[0]
     )
 
@@ -454,7 +490,9 @@
         columns = lax.broadcasted_iota(jnp.int32, (BLOCK, BLOCK), 1)
         seg_rows = segment_of(rows + start, ends)
         seg_columns = segment_of(columns + start, ends)
-        self.mask = jnp.logical_and(seg_rows == seg_columns, rows >= columns)
+        same = seg_rows == seg_columns
+        self.mask = jnp.logical_and(same, rows >= columns)
+        self.mask_t = jnp.logical_and(same, columns >= rows)
         self.last = segment_of(start + BLOCK - 1, ends)
         self.earlier = segment_of(start - 1, ends) if b > 0 else -1
         wide_rows = lax.broadcasted_iota(jnp.int32, (BLOCK, HEAD_DIM), 0)
@@ -470,9 +508,9 @@
         return jnp.where(self.last == self.earlier, factor, 0.0)
 
 
-def full_decay(rate):
-    rows = lax.broadcasted_iota(jnp.int32, (BLOCK, BLOCK), 0)
-    columns = lax.broadcasted_iota(jnp.int32, (BLOCK, BLOCK), 1)
+def full_decay(rate, turned=False):
+    rows = lax.broadcasted_iota(jnp.int32, (BLOCK, BLOCK), int(turned))
+    columns = lax.broadcasted_iota(jnp.int32, (BLOCK, BLOCK), 1 - int(turned))
     return jnp.exp(-rate * jnp.maximum(rows - columns, 0).astype(F32))
 
 
@@ -535,9 +573,8 @@
             weight = (dot(query, key, NT) * block.decay(fulls[h])).astype(BF16)
             high, low = split(state[h])
             out = dot(weight, value) + inner * (dot(query, high) + dot(query, low))
-            high, low = split(key.astype(F32) * carried)
-            state[h] = block.keeping(rates[h]) * state[h] + (
-                dot(high, value, TN) + dot(low, value, TN)
+            state[h] = block.keeping(rates[h]) * state[h] + dot(
+                (key.astype(F32) * carried).astype(BF16), value, TN
             )
             mixed[here, at[0]] = out
             pre[here, at[0]] = (out * proj[here, at[3]]).astype(BF16)
@@ -564,10 +601,10 @@
 def exit_kernel(n, heads, order, core, lengths, rates, *refs):
     pieces, refs = refs[: n + 1], refs[n + 1 :]
     weights, mixer_hbm, refs = refs[:4], refs[4], refs[5:]
-    proj_hbm, mixed_hbm, states_hbm, inverses, inners, refs = *refs[:5], refs[5:]
-    resid_out, bundle, refs = *refs[:2], refs[2:]
+    proj_hbm, mixed_hbm, states_hbm, inverses, refs = *refs[:4], refs[4:]
+    entry_out, send_out, keep_out, refs = *refs[:3], refs[3:]
     parts, refs = refs[: n + 1], refs[n + 1 :]
-    resid, weight_in, mixer, proj, mixed, states, scaled, entry_g, scaled_g, buffer, sems = refs
+    resid, weight_in, mixer, proj, mixed, states, scaled, entry_g, scaled_g, buffer, send, keep, sems = refs
     copies = Copies(sems)
     rows = pieces[0].shape[0]
     total = n * rows
@@ -583,23 +620,25 @@
         copies.start(a, b)
         for a, b in ((proj_hbm, proj), (mixed_hbm, mixed), (states_hbm, states))
     ]
-    fetched = [copies.start(w, weight_in.at[i]) for i, w in enumerate(weights)]
-    copies.write(resid, resid_out)
-    copies.write(resid.at[:, other_half(core)], bundle.at[:, pl.ds(5 * width, D // 2)])
+    fetched = [
+        copies.start(w, weight_in.at[:, i * width : (i + 1) * width]) for i, w in enumerate(weights)
+    ]
     for b in range(total // BLOCK):
         here = pl.ds(b * BLOCK, BLOCK)
-        scaled_g[here, :] = dot(resid[here, :], mixer[...], NT)
+        scaled_g[here, :] = dot(resid[here, :D], mixer[...], NT)
     for copy in saved:
         copy.wait()
     ends = row_ends(lengths)
     fulls = [full_decay(rates[h]) for h in range(heads)]
+    turned = [full_decay(rates[h], True) for h in range(heads)]
     edges = [edge_factors(rates[h]) for h in range(heads)]
     later = [jnp.zeros((HEAD_DIM, HEAD_DIM), F32) for _ in range(heads)]
     for b in reversed(range(total // BLOCK)):
         here = pl.ds(b * BLOCK, BLOCK)
         block = Block(b, ends)
         inverse = column(inverses[:, here])
-        mean = column(inners[:, here]) * (1.0 / D)
+        coded = resid[here, D : D + 128].astype(F32)
+        mean = (coded[:, 0:1] + coded[:, 1:2] + coded[:, 2:3]) * (1.0 / D)
         for h in range(heads):
             at = [slice(i * width + h * HEAD_DIM, i * width + (h + 1) * HEAD_DIM) for i in range(4)]
             query_pre, key_pre = proj[here, at[0]], proj[here, at[1]]
@@ -615,22 +654,27 @@
             inner = jnp.where(block.from_state, inner, 0.0)
             carried = jnp.where(block.to_state, carried, 0.0)
             decay = block.decay(fulls[h])
-            weight = (dot(query, key, NT) * decay).astype(BF16)
+            decay_t = jnp.where(block.mask_t, turned[h], 0.0)
+            weight_t = (dot(key, query, NT) * decay_t).astype(BF16)
             score = (dot(grad, value, NT) * decay).astype(BF16)
+            score_t = (dot(value, grad, NT) * decay_t).astype(BF16)
             high, low = split(states[b, h])
             query_g = dot(score, key) + inner * (dot(grad, high, NT) + dot(grad, low, NT))
             high, low = split(later[h])
-            key_g = dot(score, query, TN) + carried * (dot(value, high, NT) + dot(value, low, NT))
-            value_g = dot(weight, grad, TN) + carried * (dot(key, high) + dot(key, low))
-            high, low = split(query.astype(F32) * inner)
+            key_g = dot(score_t, query) + carried * (dot(value, high, NT) + dot(value, low, NT))
+            value_g = dot(weight_t, grad) + carried * (dot(key, high) + dot(key, low))
             later[h] = (
-                dot(high, grad, TN) + dot(low, grad, TN) + block.keeping(rates[h]) * later[h]
+                dot((query.astype(F32) * inner).astype(BF16), grad, TN)
+                + block.keeping(rates[h]) * later[h]
             )
             entry_g[here, at[0]] = (query_g * silu_grad(query_pre)).astype(BF16)
             entry_g[here, at[1]] = (key_g * silu_grad(key_pre)).astype(BF16)
             entry_g[here, at[2]] = value_g.astype(BF16)
-    copies.write(scaled, bundle.at[:, pl.ds(4 * width, width)])
-    copies.write(entry_g, bundle.at[:, pl.ds(0, 4 * width)])
+    copies.write(entry_g, entry_out)
+    send[...] = dot(scaled[...], resid[:, other_half(core)], TN).astype(BF16)
+    copies.write(send, send_out)
+    keep[...] = dot(scaled[...], resid[:, own_half(core)], TN)
+    copies.write(keep, keep_out)
     for copy in fetched:
         copy.wait()
     for r in reversed(range(0, n, 2)):
@@ -638,9 +682,7 @@
             [entry_g[pl.ds(pl.multiple_of(order[0, q] * rows, rows), rows), :] for q in (r, r + 1)],
             0,
         )
-        buffer[r * rows : (r + 2) * rows, :] = sum(
-            dot(both[:, i * width : (i + 1) * width], weight_in[i], NT) for i in range(4)
-        ).astype(BF16)
+        buffer[r * rows : (r + 2) * rows, :] = dot(both, weight_in[...], NT).astype(BF16)
         write_part(copies, buffer, parts, r + 1)
         write_part(copies, buffer, parts, r)
     copies.drain()
@@ -701,6 +743,24 @@
         store_part(parts, r + 1, result[rows:])
 
 
+def resid_kernel(low, grad, hidden, near, left, right, attn, hidden_g, coded):
+    rows = grad.shape[0]
+    here = slice(low, low + rows)
+    normed_g = near[...].astype(F32) + left[here, :].astype(F32) + right[here, :].astype(F32)
+    whole = grad[...].astype(F32) + norm_grad(hidden[...], normed_g)
+    hidden_g[...] = whole
+    resid = whole.astype(BF16)
+    coded[:, :D] = resid
+    inner = jnp.sum(resid.astype(F32) * attn[...], axis=1, keepdims=True)
+    lane = lax.broadcasted_iota(jnp.int32, (1, 128), 1)
+    out = jnp.zeros((rows, 128), F32)
+    for i in range(3):
+        high = inner.astype(BF16).astype(F32)
+        out += jnp.where(lane == i, high, 0.0)
+        inner -= high
+    coded[:, D:] = out.astype(BF16)
+
+
 def output_kernel(tokens, attn, ffn, valid_rows, output, sums):
     rows = tokens.shape[0]
     valid = lax.broadcasted_iota(jnp.int32, (rows, 1), 0) < valid_rows[0]
@@ -792,7 +852,7 @@
         meet(scatter, cotangent, hop)
     squares = hop.finish()
     grad_pieces = cotangent.pieces
-    attn_raw, normed_other = barrier(scatter.finish(), swap(normed_send, "wide", 1))
+    attn_raw = scatter.finish()
     inverses = lax.rsqrt(squares / D + EPS)
     inverse_own = lax.dynamic_slice(inverses, (0, start_row), (1, rows)).reshape(rows, 1)
     attn_own = attn_raw * inverse_own
@@ -831,17 +891,18 @@
         2 * total * D * units,
         22 * MIB,
     )(where, *grad_pieces, down_weight)
-    gather.left, gather.right, grad_send, *product_g = barrier(
-        gather.left, gather.right, grad_send, *product_g
-    )
+    gather.left, gather.right, grad_send, normed_send, *product_g = barrier(
+        gather.left, gather.right, grad_send, normed_send, *product_g
+    )
+    normed_other = swap(normed_send, "wide", 1)
     whole, parts = [], []
     for i in range(n // 2 - 1):
         pieces = gather.pieces[2 * i : 2 * i + 2]
         gather.step()
         whole, new_parts = hidden(i, pieces)
         if gather.left_steps:
-            gather.left, gather.right, *new_parts = barrier(
-                gather.left, gather.right, *new_parts
+            gather.left, gather.right, normed_other, *new_parts = barrier(
+                gather.left, gather.right, normed_other, *new_parts
             )
         parts += new_parts
     grad_other = swap(grad_send, "wide", 1)
@@ -854,84 +915,76 @@
     scatter = Scatter(parts, n)
     stream = Together(scatter)
     half = D // 2
-    step = 3 * half // 8
-    cuts = tuple((low, min(half, low + step)) for low in range(0, half, step))
-
-    def first_work(product, grad_all, grad_other):
-        other = swap(product, "wide", 1)
-        return own_columns(core, cuts, units, product, other, grad_all, grad_other)
-
-    (bundle_other,), down_own = region(
-        [stream], [(bundle, "wide", 1)], first_work, [product, grad_all, grad_other]
-    )
-    (received, second_other_g), first_own = region(
+    cut_at = [(0, 384, 768, half), (0, 256, 640, half), (0, 384, 896, half)]
+    cuts = [tuple(zip(at[:-1], at[1:])) for at in cut_at]
+
+    (product_other, bundle_other), _ = region(
+        [stream], [(product, "wide", 1), (bundle, "wide", 1)]
+    )
+    (second_other_g,), down_own = region(
         [stream],
-        [(down_own[0], "wide", 2), (second_g, "wide", 1)],
-        lambda *v: own_columns(core, cuts, units, *v),
-        [bundle, bundle_other, normed2, bundle_other],
-    )
-    down_in = [received]
+        [(second_g, "wide", 1)],
+        lambda *v: own_columns(core, cuts[0], units, *v),
+        [product, product_other, grad_all, grad_other],
+    )
+    down_in, first_in, second_in = [], [], []
+    (received,), first_own = region(
+        [stream],
+        [(down_own[0], "wide", 2)],
+        lambda *v: own_columns(core, cuts[1], units, *v, v[1], low=padded),
+        [bundle, bundle_other, normed2],
+    )
+    down_in.append(received)
     (received,), second_own = region(
         [stream],
         [(down_own[1], "wide", 2)],
-        lambda *v: own_columns(core, cuts, units, *v),
+        lambda *v: own_columns(core, cuts[2], units, *v, low=padded),
         [second_g, second_other_g, normed2, bundle_other],
     )
-    down_in.append(received)
-    (received,), _ = region([stream], [(down_own[2], "wide", 2)])
     down_in.append(received)
     while scatter.left_steps:
         region([stream])
-    normed2_g = scatter.result
-    hidden_g = out_grad.astype(F32) + norm_grad(hidden_own, normed2_g)
-    resid_own = hidden_g.astype(BF16)
-    inner_own = jnp.sum(resid_own.astype(F32) * attn_own, axis=1).reshape(1, rows)
-    inners = lax.dynamic_update_slice(jnp.zeros((1, total), F32), inner_own, (0, start_row))
+    left, right, low, _ = scatter.received
+    hidden_g, resid_own = call(
+        functools.partial(resid_kernel, low),
+        [((rows, D), F32), ((rows, D + 128), BF16)],
+        [VMEM] * 6,
+        20 * rows * D,
+        14 * MIB,
+    )(out_grad, hidden_own, scatter.near[0], left, right, attn_own)
 
     gather = Gather(resid_own, n)
 
     def mixed_pairs(owns, ins):
         return [v for pair in zip(owns, ins) for v in pair]
 
-    def output_parts(product, *pairs):
-        parts = call(
+    def output_parts(product):
+        return call(
             functools.partial(down_kernel, n),
             part_shapes(n, rows),
             [VMEM] * 2,
             2 * total * D * units,
-            40 * MIB,
+            14 * MIB,
         )(product, down_weight)
-        return parts, summed(*pairs)
-
-    (received, hop), (parts, down_total) = region(
+
+    (received, received2), parts = region(
         [gather],
-        [(first_own[0], "wide", 2), (inners, "narrow", 1)],
+        [(down_own[2], "wide", 2), (first_own[0], "wide", 2)],
         output_parts,
-        [product, *mixed_pairs(down_own, down_in)],
-    )
-    first_in, inners = [received], inners + hop
-    (received, hop, down_other), _ = region(
-        [gather],
-        [(first_own[1], "wide", 2), (inners, "narrow", 2), (down_total, "wide", 1)],
+        [product],
+    )
+    down_in.append(received)
+    first_in.append(received2)
+    (received,), down_total = region(
+        [gather], [(first_own[1], "wide", 2)], summed, mixed_pairs(down_own, down_in)
     )
     first_in.append(received)
-    inners = inners + hop
-    (received, hop), down_w = region(
-        [gather],
-        [(first_own[2], "wide", 2), (inners, "narrow", 4)],
-        lambda own, other: place(core, own, other, False),
-        [down_total, down_other],
+    (received, down_other), _ = region(
+        [gather], [(first_own[2], "wide", 2), (down_total, "wide", 1)]
     )
     first_in.append(received)
-    inners = inners + hop
-    bit = 8
     while gather.left_steps > 1:
-        if bit < n:
-            (hop,), _ = region([gather], [(inners, "narrow", bit)])
-            inners = inners + hop
-            bit *= 2
-        else:
-            region([gather])
+        region([gather])
     scatter2 = Scatter(parts, n)
     stream2 = Together(scatter2)
     (received,), first_total = region(
@@ -940,21 +993,22 @@
         summed,
         mixed_pairs(first_own, first_in),
     )
-    second_in = [received]
+    second_in.append(received)
 
     shapes = [
-        ((total, D), BF16),
-        ((total, 5 * width + D // 2), BF16),
+        ((total, 4 * width), BF16),
+        ((width, D // 2), BF16),
+        ((width, D // 2), F32),
     ] + part_shapes(n, rows)
     leave = call(
         functools.partial(exit_kernel, n, heads),
         shapes,
-        [SMEM] * 4 + [ANY] * (n + 9) + [VMEM] * 2,
+        [SMEM] * 4 + [ANY] * (n + 9) + [VMEM],
         12 * total * D * width,
-        48 * MIB,
+        56 * MIB,
         [
-            pltpu.VMEM((total, D), BF16),
-            pltpu.VMEM((4, D, width), BF16),
+            pltpu.VMEM((total, D + 128), BF16),
+            pltpu.VMEM((D, 4 * width), BF16),
             pltpu.VMEM((width, D), BF16),
             pltpu.VMEM((total, 4 * width), F32),
             pltpu.VMEM((total, width), F32),
@@ -963,14 +1017,16 @@
             pltpu.VMEM((total, 4 * width), BF16),
             pltpu.VMEM((total, width), F32),
             pltpu.VMEM((total, D), BF16),
+            pltpu.VMEM((width, D // 2), BF16),
+            pltpu.VMEM((width, D // 2), F32),
             pltpu.SemaphoreType.DMA((2 * n + 15,)),
         ],
         [ANY] * len(shapes),
     )
-    (received, first_other), (resid, bundle, *parts) = region(
+    (received, first_other), (entry_g, mixer_send, mixer_keep, *parts) = region(
         [stream2],
         [(second_own[1], "wide", 2), (first_total, "wide", 1)],
-        lambda inverses, inners, *pieces: leave(
+        lambda inverses, *pieces: leave(
             order,
             where,
             doc_lengths,
@@ -982,40 +1038,45 @@
             mixed,
             states,
             inverses,
-            inners,
         ),
-        [inverses, inners, *gather.pieces],
+        [inverses, *gather.pieces],
     )
     second_in.append(received)
 
     scatter = Scatter(parts, n)
-
     stream = Together(scatter2, scatter)
 
-    def entry_work(bundle, resid, normed, normed_other, *first):
-        owns = call(
-            entry_sums_kernel,
-            [((width, D // 2), BF16)] + [((D // 2, width), BF16)] * 4,
-            [SMEM, VMEM, VMEM, ANY, ANY, VMEM],
-            10 * total * D * width,
-            40 * MIB,
-            [pltpu.VMEM((total, D // 2), BF16)] * 2 + [pltpu.SemaphoreType.DMA((2,))],
-        )(where, bundle, swap(bundle, "wide", 1), resid, normed, normed_other)
-        return owns, place(core, *first, False)
-
-    (received,), ((mixer_own, *owns), first_w) = region(
+    def mixer_work(keep, crossed_send, entry_g, normed, normed_other, *placed):
+        (mixer_own,) = call(
+            add_kernel, [(keep.shape, BF16)], [VMEM] * 2, keep.size, 14 * MIB
+        )(keep, swap(crossed_send, "wide", 1))
+        mixer_in = swap(mixer_own, "wide", 2)
+        entry_other = swap(entry_g, "wide", 1)
+        owns = own_rows(core, 2, 2, width, normed, normed_other, entry_g, entry_other)
+        down_w = place(core, *placed[:2], False)
+        first_w = place(core, *placed[2:], False)
+        return mixer_own, mixer_in, owns, entry_other, down_w, first_w
+
+    (received,), work_out = region(
         [stream],
         [(second_own[2], "wide", 2)],
+        mixer_work,
+        [mixer_keep, mixer_send, entry_g, normed, normed_other]
+        + [down_total, down_other, first_total, first_other],
+    )
+    second_in.append(received)
+    mixer_own, mixer_in, (value_own, gate_own), entry_other, down_w, first_w = work_out
+
+    def entry_work(normed, normed_other, entry_g, entry_other, *pairs):
+        owns = own_rows(core, 0, 2, width, normed, normed_other, entry_g, entry_other)
+        return owns, summed(*pairs[:2]), summed(*pairs[2:])
+
+    (gate_in, value_in), ((query_own, key_own), mixer_total, second_total) = region(
+        [stream],
+        [(gate_own, "wide", 2), (value_own, "wide", 2)],
         entry_work,
-        [bundle, resid, normed, normed_other, first_total, first_other],
-    )
-    second_in.append(received)
-    query_own, key_own, value_own, gate_own = owns
-    (mixer_in, gate_in), second_total = region(
-        [stream],
-        [(mixer_own, "wide", 2), (gate_own, "wide", 2)],
-        summed,
-        mixed_pairs(second_own, second_in),
+        [normed, normed_other, entry_g, entry_other, mixer_own, mixer_in]
+        + mixed_pairs(second_own, second_in),
     )
     while scatter2.left_steps:
         region([stream])
@@ -1028,47 +1089,44 @@
             [((rows, D), BF16), ((1, 128), F32)],
             [VMEM] * 3 + [SMEM],
             6 * rows * D,
-            8 * MIB,
+            14 * MIB,
         )(tokens_in, attn_own, ffn_own, valid_rows)
-        return output, stats, summed(a, b), summed(c, d)
-
-    (value_in, second_other), (output, stats, mixer_total, gate_total) = region(
+        return output, stats + swap(stats, "narrow", 1), summed(a, b), summed(c, d)
+
+    (key_in, second_other), (output, stats, gate_total, value_total) = region(
         [stream],
-        [(value_own, "wide", 2), (second_total, "wide", 1)],
+        [(key_own, "wide", 2), (second_total, "wide", 1)],
         output_work,
-        [tokens_in, attn_own, ffn_own, mixer_own, mixer_in, gate_own, gate_in],
-    )
-    (key_in, mixer_other, gate_other), (second_w, value_total) = region(
+        [tokens_in, attn_own, ffn_own, gate_own, gate_in, value_own, value_in],
+    )
+    (query_in, mixer_other, hop), (second_w, key_total) = region(
         [stream],
-        [(key_own, "wide", 2), (mixer_total, "wide", 1), (gate_total, "wide", 1)],
+        [(query_own, "wide", 2), (mixer_total, "wide", 1), (stats, "narrow", 2)],
         lambda own, other, *v: (place(core, own, other, False), summed(*v)),
-        [second_total, second_other, value_own, value_in],
-    )
+        [second_total, second_other, key_own, key_in],
+    )
+    stats = stats + hop
     while scatter.left_steps:
         region([stream])
     normed_g = scatter.result
 
-    def end_work(stats, normed_g, a, b, *v):
-        key_total = summed(a, b)
-        key_other = swap(key_total, "wide", 1)
-        return (
-            Butterfly(stats, "narrow").finish(),
-            hidden_g + norm_grad(tokens_wide, normed_g),
-            place(core, key_total, key_other, True),
-            place(core, *v[:2], False),
-            place(core, *v[2:], True),
-        )
-
-    (query_in, value_other), (stats, input_grad, key_w, mixer_w, gate_w) = region(
+    (gate_other, value_other, key_other, hop), (query_total, mixer_w) = region(
         [],
-        [(query_own, "wide", 2), (value_total, "wide", 1)],
-        end_work,
-        [stats, normed_g, key_own, key_in, mixer_total, mixer_other, gate_total, gate_other],
-    )
-    query_total = summed(query_own, query_in)
-    query_w = place(core, query_total, swap(query_total, "wide", 1), True)
+        [(v, "wide", 1) for v in (gate_total, value_total, key_total)] + [(stats, "narrow", 4)],
+        lambda a, b, *v: (summed(a, b), place(core, *v, False)),
+        [query_own, query_in, mixer_total, mixer_other],
+    )
+    stats = stats + hop
+    query_other = swap(query_total, "wide", 1)
+    for axis, bit in (("narrow", 8), ("wide", 1)):
+        while bit < lax.axis_size(axis):
+            stats = stats + swap(stats, axis, bit)
+            bit *= 2
+    gate_w = place(core, gate_total, gate_other, True)
+    input_grad = hidden_g + norm_grad(tokens_wide, normed_g)
     value_w = place(core, value_total, value_other, True)
-    stats = Butterfly(stats, "wide").finish()
+    key_w = place(core, key_total, key_other, True)
+    query_w = place(core, query_total, query_other, True)
     stream_rms = jnp.sqrt(stats[0, :3] / (stats[0, 3] * D))
     return (
         output,

time: 475 us -> 458 us (0.964)
  waiting for transfers between devices: 210 us -> 196 us
  Pallas kernels: 115 us -> 123 us
  local copies, waits for them, and re-layouts: 27.2 us -> 22 us
    ppermute x39 -> x37, waiting for transfers between devices: 92.1 us -> 80.3 us  [swap(): return lax.ppermute(values, axis, [(i, i ^ bit) for i in range(size)])]
    pallas_call x4 -> x7, Pallas kernels: 27.7 us -> 35.5 us  [the longest x3 22 us: own_columns(): call(functools.partial(columns_kernel, cuts, lefts, (None, low)), [((widt...]
    unnamed x202 -> x204, local copies, waits for them, and re-layouts: 25.7 us -> 20.6 us
    ppermute x39 -> x37, starting transfers between devices: 31.5 us -> 30.2 us  [swap(): return lax.ppermute(values, axis, [(i, i ^ bit) for i in range(size)])]
  transfers between devices with their start and end apart: 99 -> 97, of which waited for: 53 -> 46; matrix products, arithmetic and copies ran while one was open for 2% -> 1% of each run, Pallas kernels for 22% -> 24%
where the time goes in v3:
time: 458 us; the launch traced here: 449 us
  waiting for transfers between devices  196 us (43%)
  Pallas kernels  123 us (27%)
  starting transfers between devices  95 us (21%)
  local copies, waits for them, and re-layouts  22 us (5%)
  other arithmetic  9.01 us (2%)
    ppermute x30, waiting for transfers between devices, onward(): lax.ppermute(values, 'narrow', [(ring[i], ring[(i + 1) % n]) for i in ran...  96.9 us
    ppermute x37, waiting for transfers between devices, swap(): return lax.ppermute(values, axis, [(i, i ^ bit) for i in range(size)])  80.3 us
    ppermute x30, starting transfers between devices, onward(): lax.ppermute(values, 'narrow', [(ring[i], ring[(i + 1) % n]) for i in ran...  38.5 us
    ppermute x37, starting transfers between devices, swap(): return lax.ppermute(values, axis, [(i, i ^ bit) for i in range(size)])  30.2 us
    ppermute x30, starting transfers between devices, backward(): lax.ppermute(values, 'narrow', [(ring[(i + 1) % n], ring[i]) for i in ran...  26.3 us
    pallas_call x3, Pallas kernels, own_columns(): call(functools.partial(columns_kernel, cuts, lefts, (None, low)), [((widt...  22 us
    unnamed x204, local copies, waits for them, and re-layouts  20.6 us
    ppermute x30, waiting for transfers between devices, backward(): lax.ppermute(values, 'narrow', [(ring[(i + 1) % n], ring[i]) for i in ran...  18.9 us
  transfers between devices with their start and end apart: 97, of which 46 were waited for; matrix products, arithmetic and copies ran while one was open for 1% of the time, Pallas kernels for 24%

profile of v3, /device:TPU:0, one launch (start us, length us, event | category | flops | bytes accessed | tf_op | source)
XLA Modules:
  0.0 448.8 jit_solution(8310049531379574098)
XLA Ops:
  3.2 3.1 collective-permute-start
  6.3 11.8 %collective-permute-done.refs_1_ = bf16[128,2048]{1,0:T(8,128)(2,1)S(1)} collective-permute-done((bf16[128,2048]{1,0:T(8,128)(2,1)S(1)}, bf16[128,2048]{1,0:T(8,128)(2,1)S(1)}, u32[]{:S(2)}, u32[]{:S(2)}) %collective-permute-start) | collective-permute-done | bytes 524320 | tf_op jit(solution)/shard_map/ppermute | solution.py:70
  20.1 11.1 %collective-permute-done.2.refs_3_ = bf16[128,2048]{1,0:T(8,128)(2,1)S(1)} collective-permute-done((bf16[128,2048]{1,0:T(8,128)(2,1)S(1)}, bf16[128,2048]{1,0:T(8,128)(2,1)S(1)}, u32[]{:S(2)}, u32[]{:S(2)}) %collective-permute-start.2) | collective-permute-done | bytes 524320 | tf_op jit(solution)/shard_map/ppermute | solution.py:70
  33.3 10.1 %collective-permute-done.4.refs_5_ = bf16[128,2048]{1,0:T(8,128)(2,1)S(1)} collective-permute-done((bf16[128,2048]{1,0:T(8,128)(2,1)S(1)}, bf16[128,2048]{1,0:T(8,128)(2,1)S(1)}, u32[]{:S(2)}, u32[]{:S(2)}) %collective-permute-start.4) | collective-permute-done | bytes 524320 | tf_op jit(solution)/shard_map/ppermute | solution.py:70
  47.9 2.8 collective-permute-done.6.refs_7_
  54.8 14.1 %shard_map.212 = (bf16[1024,2048]{1,0:T(8,128)(2,1)}, bf16[1024,1024]{1,0:T(8,128)(2,1)}, f32[1024,1024]{1,0:T(8,128)}, f32[1024,256]{1,0:T(8,128)}, f32[1,1024]...) custom-call(s32[1,8]{1,0:T(1,128)S(1)} %constant_dynamic-slice_fusio, ...), custom_call_target="tpu_custom_call" | custom-call | flops 6442450944 | bytes 12884901 | tf_op jit(solution)/shard_map/pallas_call | solution.py:824
  75.1 11.7 %collective-permute-done.14 = f32[1,1024]{1,0:T(1,128)S(1)} collective-permute-done((f32[1,1024]{1,0:T(1,128)S(1)}, f32[1,1024]{1,0:T(1,128)S(1)}, u32[]{:S(2)}, u32[]{:S(2)}) %collective-permute-start.14) | collective-permute-done | bytes 4128 | tf_op jit(solution)/shard_map/ppermute | solution.py:238
  86.8 2.3 collective-permute-done.11.part
  95.6 7.3 %collective-permute-done.19 = f32[1,1024]{1,0:T(1,128)S(1)} collective-permute-done((f32[1,1024]{1,0:T(1,128)S(1)}, f32[1,1024]{1,0:T(1,128)S(1)}, u32[]{:S(2)}, u32[]{:S(2)}) %collective-permute-start.19) | collective-permute-done | bytes 4128 | tf_op jit(solution)/shard_map/ppermute | solution.py:238
  103.2 6.5 %collective-permute-done.17.refs_5_ = bf16[128,2048]{1,0:T(8,128)(2,1)S(1)} collective-permute-done((bf16[128,2048]{1,0:T(8,128)(2,1)S(1)}, bf16[128,2048]{1,0:T(8,128)(2,1)S(1)}, u32[]{:S(2)}, u32[]{:S(2)}) %collective-permute-start.17) | collective-permute-done | bytes 524320 | tf_op jit(solution)/shard_map/ppermute | solution.py:70
  109.7 3.1 collective-permute-done.18.refs_6_
  114.9 3.5 collective-permute-start.24
  120.5 4.1 collective-permute-done.24
  124.9 4.4 collective-permute-done.22.refs_7_
  130.1 2.8 collective-permute-start.25
  133.2 11.4 %collective-permute-done.25 = bf16[128,2048]{1,0:T(8,128)(2,1)} collective-permute-done((bf16[128,2048]{1,0:T(8,128)(2,1)S(1)}, bf16[128,2048]{1,0:T(8,128)(2,1)}, u32[]{:S(2)}, u32[]{:S(2)}) %collective-permute-start.25) | collective-permute-done | bytes 524320 | tf_op jit(solution)/shard_map/ppermute | solution.py:70
  144.6 3.7 collective-permute-done.26
  154.4 3.6 shard_map.215
  163.8 4.3 shard_map.216
  168.8 6.7 %collective-permute-done.29.refs_1_ = bf16[128,2048]{1,0:T(8,128)(2,1)S(1)} collective-permute-done((bf16[128,2048]{1,0:T(8,128)(2,1)S(1)}, bf16[128,2048]{1,0:T(8,128)(2,1)S(1)}, u32[]{:S(2)}, u32[]{:S(2)}) %collective-permute-start.29) | collective-permute-done | bytes 524320 | tf_op jit(solution)/shard_map/ppermute | solution.py:70
  178.0 4.3 shard_map.217
  182.3 6.4 %collective-permute-done.32.refs_1_ = bf16[128,2048]{1,0:T(8,128)(2,1)S(1)} collective-permute-done((bf16[128,2048]{1,0:T(8,128)(2,1)S(1)}, bf16[128,2048]{1,0:T(8,128)(2,1)S(1)}, u32[]{:S(2)}, u32[]{:S(2)}) %collective-permute-start.32) | collective-permute-done | bytes 524320 | tf_op jit(solution)/shard_map/ppermute | solution.py:70
  189.5 2.1 collective-permute-start.35
  191.7 4.3 shard_map.218
  196.4 4.3 shard_map.219
  203.3 6.3 %collective-permute-done.37.refs_2_ = bf16[64,2048]{1,0:T(8,128)(2,1)S(1)} collective-permute-done((bf16[64,2048]{1,0:T(8,128)(2,1)S(1)}, bf16[64,2048]{1,0:T(8,128)(2,1)S(1)}, u32[]{:S(2)}, u32[]{:S(2)}) %collective-permute-start.37) | collective-permute-done | bytes 262176 | tf_op jit(solution)/shard_map/ppermute | solution.py:70
  214.5 7.3 %shard_map.221 = (bf16[704,384]{1,0:T(8,128)(2,1)}, bf16[704,384]{1,0:T(8,128)(2,1)}, bf16[704,256]{1,0:T(8,128)(2,1)}) custom-call(s32[1]{0:T(128)} %bitcast.core, bf16[1024,768]{1,0:T(8,128)(2,1)} %copy-done.4, bf16[1024,768]{1,0:T(8,128)(2,1)} %copy-done.90, bf16[1024,2048]{1,0:T(8,128)(2,1)} %copy-done.80, bf16[1024,1024]{1,0:T(8,128)(2,1)} %collective-permute-done.36.refs_3_), custom_call_target="tpu_custom_call" | custom-call | flops 2952790016 | bytes 5905580 | tf_op jit(solution)/shard_map/pallas_call | solution.py:296
  221.8 5.0 %collective-permute-done.41.refs_2_ = bf16[128,2048]{1,0:T(8,128)(2,1)S(1)} collective-permute-done((bf16[128,2048]{1,0:T(8,128)(2,1)S(1)}, bf16[128,2048]{1,0:T(8,128)(2,1)S(1)}, u32[]{:S(2)}, u32[]{:S(2)}) %collective-permute-start.41) | collective-permute-done | bytes 524320 | tf_op jit(solution)/shard_map/ppermute | solution.py:70
  231.4 7.4 %shard_map.223 = (bf16[704,256]{1,0:T(8,128)(2,1)}, bf16[704,384]{1,0:T(8,128)(2,1)}, bf16[704,384]{1,0:T(8,128)(2,1)}) custom-call(s32[1]{0:T(128)} %bitcast.core, bf16[1024,1792]{1,0:T(8,128)(2,1)} %get-tuple-element.541.refs_0_, bf16[1024,1792]{1,0:T(8,128)(2,1)} %copy-done.82, bf16[1024,2048]{1,0:T(8,128)(2,1)} %get-tuple-element.558.refs_2_, ...), custom_call_target="tpu_custom_call" | custom-call | flops 2952790016 | bytes 5905580 | tf_op jit(solution)/shard_map/pallas_call | solution.py:296
  238.7 3.4 collective-permute-done.44.refs_2_
  246.4 7.3 %shard_map.225 = (bf16[704,384]{1,0:T(8,128)(2,1)}, bf16[704,512]{1,0:T(8,128)(2,1)}, bf16[704,128]{1,0:T(8,128)(2,1)}) custom-call(s32[1]{0:T(128)} %bitcast.core, bf16[1024,768]{1,0:T(8,128)(2,1)} %copy-done.2, bf16[1024,768]{1,0:T(8,128)(2,1)} %collective-permute-done.43.refs_1_, bf16[1024,2048]{1,0:T(8,128)(2,1)} %get-tuple-element.558.refs_2_, ...), custom_call_target="tpu_custom_call" | custom-call | flops 2952790016 | bytes 5905580 | tf_op jit(solution)/shard_map/pallas_call | solution.py:296
  264.9 3.4 shard_map.227
  271.1 4.7 %collective-permute-done.53.refs_1_ = bf16[704,256]{1,0:T(8,128)(2,1)S(1)} collective-permute-done((bf16[704,256]{1,0:T(8,128)(2,1)S(1)}, bf16[704,256]{1,0:T(8,128)(2,1)S(1)}, u32[]{:S(2)}, u32[]{:S(2)}) %collective-permute-start.53) | collective-permute-done | bytes 360480 | tf_op jit(solution)/shard_map/ppermute | solution.py:238
  279.8 7.5 %collective-permute-done.56.refs_3_ = bf16[704,384]{1,0:T(8,128)(2,1)S(1)} collective-permute-done((bf16[704,384]{1,0:T(8,128)(2,1)S(1)}, bf16[704,384]{1,0:T(8,128)(2,1)S(1)}, u32[]{:S(2)}, u32[]{:S(2)}) %collective-permute-start.56) | collective-permute-done | bytes 540704 | tf_op jit(solution)/shard_map/ppermute | solution.py:238
  291.0 12.6 %collective-permute-done.59.refs_5_ = bf16[704,384]{1,0:T(8,128)(2,1)S(1)} collective-permute-done((bf16[704,384]{1,0:T(8,128)(2,1)S(1)}, bf16[704,384]{1,0:T(8,128)(2,1)S(1)}, u32[]{:S(2)}, u32[]{:S(2)}) %collective-permute-start.59) | collective-permute-done | bytes 540704 | tf_op jit(solution)/shard_map/ppermute | solution.py:238
  309.9 8.8 %collective-permute-done.63.refs_2_ = bf16[64,2048]{1,0:T(8,128)(2,1)S(1)} collective-permute-done((bf16[64,2048]{1,0:T(8,128)(2,1)S(1)}, bf16[64,2048]{1,0:T(8,128)(2,1)S(1)}, u32[]{:S(2)}, u32[]{:S(2)}) %collective-permute-start.63) | collective-permute-done | bytes 262176 | tf_op jit(solution)/shard_map/ppermute | solution.py:70
  323.6 16.5 %shard_map.231 = (bf16[1024,1024]{1,0:T(8,128)(2,1)}, bf16[256,1024]{1,0:T(8,128)(2,1)}, f32[256,1024]{1,0:T(8,128)}, bf16[128,2048]{1,0:T(8,128)(2,1)}, bf16[12...) custom-call(s32[1,8]{1,0:T(1,128)} %copy-done.79, ...), custom_call_target="tpu_custom_call" | custom-call | flops 6442450944 | bytes 12884901 | tf_op jit(solution)/shard_map/pallas_call | solution.py:1029
  343.6 2.6 shard_map.232
  353.0 2.9 shard_map.236
  355.9 2.9 shard_map.235
  358.8 6.3 %shard_map.234 = (bf16[1024,256]{1,0:T(8,128)(2,1)}, bf16[1024,256]{1,0:T(8,128)(2,1)}) custom-call(s32[1]{0:T(128)} %bitcast.core, bf16[1024,2048]{1,0:T(8,128)(2,1)} %get-tuple-element.715.refs_0_, bf16[1024,1024]{1,0:T(8,128)(2,1)} %copy-done.83, bf16[1024,1024]{1,0:T(8,128)(2,1)} %get-tuple-element.717.refs_2_, ...), custom_call_target="tpu_custom_call" | custom-call | flops 2147483648 | bytes 4294967 | tf_op jit(solution)/shard_map/pallas_call | solution.py:332
  365.2 3.9 collective-permute-done.72.refs_5_
  377.8 6.2 %shard_map.238 = (bf16[1024,256]{1,0:T(8,128)(2,1)}, bf16[1024,256]{1,0:T(8,128)(2,1)}) custom-call(s32[1]{0:T(128)} %bitcast.core, bf16[1024,2048]{1,0:T(8,128)(2,1)} %get-tuple-element.715.refs_0_, bf16[1024,1024]{1,0:T(8,128)(2,1)} %copy-done.83, bf16[1024,1024]{1,0:T(8,128)(2,1)} %get-tuple-element.717.refs_2_, ...), custom_call_target="tpu_custom_call" | custom-call | flops 2147483648 | bytes 4294967 | tf_op jit(solution)/shard_map/pallas_call | solution.py:332
  384.0 3.7 collective-permute-done.78.refs_1_
  387.7 9.2 %collective-permute-done.79.refs_1_ = bf16[1024,256]{1,0:T(8,128)(2,1)S(1)} collective-permute-done((bf16[1024,256]{1,0:T(8,128)(2,1)S(1)}, bf16[1024,256]{1,0:T(8,128)(2,1)S(1)}, u32[]{:S(2)}, u32[]{:S(2)}) %collective-permute-start.79) | collective-permute-done | bytes 524320 | tf_op jit(solution)/shard_map/ppermute | solution.py:238
  407.7 6.2 %collective-permute-done.84 = f32[1,128]{1,0:T(1,128)S(1)} collective-permute-done((f32[1,128]{1,0:T(1,128)S(1)}, f32[1,128]{1,0:T(1,128)S(1)}, u32[]{:S(2)}, u32[]{:S(2)}) %collective-permute-start.84) | collective-permute-done | bytes 544 | tf_op jit(solution)/shard_map/ppermute | solution.py:238
  422.8 4.3 shard_map.246
  427.1 3.5 collective-permute-done.89
  (428 shorter events, 153.3 us)
Async XLA Ops:
  3.2 14.9 %collective-permute-start = (bf16[128,2048]{1,0:T(8,128)(2,1)S(1)}, bf16[128,2048]{1,0:T(8,128)(2,1)S(1)}, u32[]{:S(2)}, u32[]{:S(2)}) collective-permute-start(bf16[128,2048]{1,0:T(8,128)(2,1)S(1)} %fusion.2.refs_0_), channel_id=1, source_target_pairs={{0,2},{2,4},{4,6},{6,7},{7,5},{5,3},{3,1},{1,0},{8,10},{10,12},{12... | collective-permute-start | bytes 1572872 | tf_op jit(solution)/shard_map/ppermute | solution.py:70
  6.2 13.7 %collective-permute-start.1 = (bf16[128,2048]{1,0:T(8,128)(2,1)S(1)}, bf16[128,2048]{1,0:T(8,128)(2,1)S(1)}, u32[]{:S(2)}, u32[]{:S(2)}) collective-permute-start(bf16[128,2048]{1,0:T(8,128)(2,1)S(1)} %fusion.2.refs_0_), channel_id=1, source_target_pairs={{2,0},{4,2},{6,4},{7,6},{5,7},{3,5},{1,3},{0,1},{10,8},{12,10},{14... | collective-permute-start | bytes 1572872 | tf_op jit(solution)/shard_map/ppermute | solution.py:75
  52.7 17.0 %collective-permute-start.8 = (bf16[128,2048]{1,0:T(8,128)(2,1)S(1)}, bf16[128,2048]{1,0:T(8,128)(2,1)S(1)}, u32[]{:S(2)}, u32[]{:S(2)}) collective-permute-start(bf16[128,2048]{1,0:T(8,128)(2,1)S(1)} %copy-done.49), channel_id=1, source_target_pairs={{0,2},{2,4},{4,6},{6,7},{7,5},{5,3},{3,1},{1,0},{8,10},{10,12},{12... | collective-permute-start | bytes 1572872 | tf_op jit(solution)/shard_map/ppermute | solution.py:70
  54.3 15.4 %collective-permute-start.9 = (bf16[128,2048]{1,0:T(8,128)(2,1)S(1)}, bf16[128,2048]{1,0:T(8,128)(2,1)S(1)}, u32[]{:S(2)}, u32[]{:S(2)}) collective-permute-start(bf16[128,2048]{1,0:T(8,128)(2,1)S(1)} %copy-done.49), channel_id=1, source_target_pairs={{2,0},{4,2},{6,4},{7,6},{5,7},{3,5},{1,3},{0,1},{10,8},{12,10},{14... | collective-permute-start | bytes 1572872 | tf_op jit(solution)/shard_map/ppermute | solution.py:75
  69.7 19.6 %collective-permute-start.12 = (bf16[128,2048]{1,0:T(8,128)(2,1)S(1)}, bf16[128,2048]{1,0:T(8,128)(2,1)S(1)}, u32[]{:S(2)}, u32[]{:S(2)}) collective-permute-start(bf16[128,2048]{1,0:T(8,128)(2,1)S(1)} %collective-permute-done.8.refs_1_), channel_id=1, source_target_pairs={{0,2},{2,4},{4,6},{6,7},{7,5},{5,3},{3,1},{1,0},{8,10},{10,12},{12... | collective-permute-start | bytes 1572872 | tf_op jit(solution)/shard_map/ppermute | solution.py:70
  71.4 18.0 %collective-permute-start.13 = (bf16[128,2048]{1,0:T(8,128)(2,1)S(1)}, bf16[128,2048]{1,0:T(8,128)(2,1)S(1)}, u32[]{:S(2)}, u32[]{:S(2)}) collective-permute-start(bf16[128,2048]{1,0:T(8,128)(2,1)S(1)} %collective-permute-done.9.refs_2_), channel_id=1, source_target_pairs={{2,0},{4,2},{6,4},{7,6},{5,7},{3,5},{1,3},{0,1},{10,8},{12,10},{14... | collective-permute-start | bytes 1572872 | tf_op jit(solution)/shard_map/ppermute | solution.py:75
  71.8 17.3 %collective-permute-start.11 = (bf16[64,2048]{1,0:T(8,128)(2,1)S(1)}, bf16[64,2048]{1,0:T(8,128)(2,1)S(1)}, u32[]{:S(2)}, u32[]{:S(2)}) collective-permute-start(bf16[64,2048]{1,0:T(8,128)(2,1)S(1)} %get-tuple-element.431), channel_id=1, source_target_pairs={{2,0},{4,2},{6,4},{7,6},{5,7},{3,5},{1,3},{0,1},{10,8},{12,10},{14... | collective-permute-start | bytes 786440 | tf_op jit(solution)/shard_map/ppermute | solution.py:75
  73.1 16.2 %collective-permute-start.10 = (bf16[64,2048]{1,0:T(8,128)(2,1)S(1)}, bf16[64,2048]{1,0:T(8,128)(2,1)S(1)}, u32[]{:S(2)}, u32[]{:S(2)}) collective-permute-start(bf16[64,2048]{1,0:T(8,128)(2,1)S(1)} %get-tuple-element.429), channel_id=1, source_target_pairs={{0,2},{2,4},{4,6},{6,7},{7,5},{5,3},{3,1},{1,0},{8,10},{10,12},{12... | collective-permute-start | bytes 786440 | tf_op jit(solution)/shard_map/ppermute | solution.py:70
  89.4 13.5 %collective-permute-start.16 = (bf16[128,2048]{1,0:T(8,128)(2,1)S(1)}, bf16[128,2048]{1,0:T(8,128)(2,1)S(1)}, u32[]{:S(2)}, u32[]{:S(2)}) collective-permute-start(bf16[128,2048]{1,0:T(8,128)(2,1)S(1)} %shard_map.214), channel_id=1, source_target_pairs={{2,0},{4,2},{6,4},{7,6},{5,7},{3,5},{1,3},{0,1},{10,8},{12,10},{14... | collective-permute-start | bytes 1572872 | tf_op jit(solution)/shard_map/ppermute | solution.py:75
  89.6 13.4 %collective-permute-start.15 = (bf16[128,2048]{1,0:T(8,128)(2,1)S(1)}, bf16[128,2048]{1,0:T(8,128)(2,1)S(1)}, u32[]{:S(2)}, u32[]{:S(2)}) collective-permute-start(bf16[128,2048]{1,0:T(8,128)(2,1)S(1)} %shard_map.213), channel_id=1, source_target_pairs={{0,2},{2,4},{4,6},{6,7},{7,5},{5,3},{3,1},{1,0},{8,10},{10,12},{12... | collective-permute-start | bytes 1572872 | tf_op jit(solution)/shard_map/ppermute | solution.py:70
  93.5 16.2 %collective-permute-start.17 = (bf16[128,2048]{1,0:T(8,128)(2,1)S(1)}, bf16[128,2048]{1,0:T(8,128)(2,1)S(1)}, u32[]{:S(2)}, u32[]{:S(2)}) collective-permute-start(bf16[128,2048]{1,0:T(8,128)(2,1)S(1)} %collective-permute-done.12.refs_3_), channel_id=1, source_target_pairs={{0,2},{2,4},{4,6},{6,7},{7,5},{5,3},{3,1},{1,0},{8,10},{10,12},{12... | collective-permute-start | bytes 1572872 | tf_op jit(solution)/shard_map/ppermute | solution.py:70
  93.6 19.3 %collective-permute-start.18 = (bf16[128,2048]{1,0:T(8,128)(2,1)S(1)}, bf16[128,2048]{1,0:T(8,128)(2,1)S(1)}, u32[]{:S(2)}, u32[]{:S(2)}) collective-permute-start(bf16[128,2048]{1,0:T(8,128)(2,1)S(1)} %collective-permute-done.13.refs_4_), channel_id=1, source_target_pairs={{2,0},{4,2},{6,4},{7,6},{5,7},{3,5},{1,3},{0,1},{10,8},{12,10},{14... | collective-permute-start | bytes 1572872 | tf_op jit(solution)/shard_map/ppermute | solution.py:75
  130.1 14.5 %collective-permute-start.25 = (bf16[128,2048]{1,0:T(8,128)(2,1)S(1)}, bf16[128,2048]{1,0:T(8,128)(2,1)}, u32[]{:S(2)}, u32[]{:S(2)}) collective-permute-start(bf16[128,2048]{1,0:T(8,128)(2,1)S(1)} %add_convert_fusion.1), channel_id=1, source_target_pairs={{0,2},{2,4},{4,6},{6,7},{7,5},{5,3},{3,1},{1,0},{8,10},{10,12},{12... | collective-permute-start | bytes 1572872 | tf_op jit(solution)/shard_map/ppermute | solution.py:70
  132.8 15.5 %collective-permute-start.26 = (bf16[128,2048]{1,0:T(8,128)(2,1)S(1)}, bf16[128,2048]{1,0:T(8,128)(2,1)}, u32[]{:S(2)}, u32[]{:S(2)}) collective-permute-start(bf16[128,2048]{1,0:T(8,128)(2,1)S(1)} %add_convert_fusion), channel_id=1, source_target_pairs={{2,0},{4,2},{6,4},{7,6},{5,7},{3,5},{1,3},{0,1},{10,8},{12,10},{14... | collective-permute-start | bytes 1572872 | tf_op jit(solution)/shard_map/ppermute | solution.py:75
  161.2 14.7 %collective-permute-start.31 = (bf16[1024,1024]{1,0:T(8,128)(2,1)}, bf16[1024,1024]{1,0:T(8,128)(2,1)S(1)}, u32[]{:S(2)}, u32[]{:S(2)}) collective-permute-start(bf16[1024,1024]{1,0:T(8,128)(2,1)} %get-tuple-element.468), channel_id=1, source_target_pairs={{0,8},{8,0},{16,24},{24,16},{1,9},{9,1},{17,25},{25,17},{2,10},{10... | collective-permute-start | bytes 6291464 | tf_op jit(solution)/shard_map/ppermute | solution.py:238
  161.2 34.7 %collective-permute-start.36 = (bf16[1024,1024]{1,0:T(8,128)(2,1)S(1)}, bf16[1024,1024]{1,0:T(8,128)(2,1)}, u32[]{:S(2)}, u32[]{:S(2)}) collective-permute-start(bf16[1024,1024]{1,0:T(8,128)(2,1)S(1)} %get-tuple-element.494), channel_id=1, source_target_pairs={{0,8},{8,0},{16,24},{24,16},{1,9},{9,1},{17,25},{25,17},{2,10},{10... | collective-permute-start | bytes 6291464 | tf_op jit(solution)/shard_map/ppermute | solution.py:238
  161.7 13.8 %collective-permute-start.29 = (bf16[128,2048]{1,0:T(8,128)(2,1)S(1)}, bf16[128,2048]{1,0:T(8,128)(2,1)S(1)}, u32[]{:S(2)}, u32[]{:S(2)}) collective-permute-start(bf16[128,2048]{1,0:T(8,128)(2,1)S(1)} %collective-permute-done.27.refs_1_), channel_id=1, source_target_pairs={{0,2},{2,4},{4,6},{6,7},{7,5},{5,3},{3,1},{1,0},{8,10},{10,12},{12... | collective-permute-start | bytes 1572872 | tf_op jit(solution)/shard_map/ppermute | solution.py:70
  162.3 13.6 %collective-permute-start.30 = (bf16[128,2048]{1,0:T(8,128)(2,1)S(1)}, bf16[128,2048]{1,0:T(8,128)(2,1)S(1)}, u32[]{:S(2)}, u32[]{:S(2)}) collective-permute-start(bf16[128,2048]{1,0:T(8,128)(2,1)S(1)} %collective-permute-done.28.refs_0_), channel_id=1, source_target_pairs={{2,0},{4,2},{6,4},{7,6},{5,7},{3,5},{1,3},{0,1},{10,8},{12,10},{14... | collective-permute-start | bytes 1572872 | tf_op jit(solution)/shard_map/ppermute | solution.py:75
  212.4 14.8 %collective-permute-start.43 = (bf16[1024,768]{1,0:T(8,128)(2,1)S(1)}, bf16[1024,768]{1,0:T(8,128)(2,1)}, u32[]{:S(2)}, u32[]{:S(2)}) collective-permute-start(bf16[1024,768]{1,0:T(8,128)(2,1)S(1)} %get-tuple-element.556.refs_0_), channel_id=1, source_target_pairs={{0,8},{8,0},{16,24},{24,16},{1,9},{9,1},{17,25},{25,17},{2,10},{10... | collective-permute-start | bytes 4718600 | tf_op jit(solution)/shard_map/ppermute | solution.py:238
  212.4 14.3 %collective-permute-start.41 = (bf16[128,2048]{1,0:T(8,128)(2,1)S(1)}, bf16[128,2048]{1,0:T(8,128)(2,1)S(1)}, u32[]{:S(2)}, u32[]{:S(2)}) collective-permute-start(bf16[128,2048]{1,0:T(8,128)(2,1)S(1)} %get-tuple-element.521), channel_id=1, source_target_pairs={{0,2},{2,4},{4,6},{6,7},{7,5},{5,3},{3,1},{1,0},{8,10},{10,12},{12... | collective-permute-start | bytes 1572872 | tf_op jit(solution)/shard_map/ppermute | solution.py:70
  213.2 14.1 %collective-permute-start.42 = (bf16[128,2048]{1,0:T(8,128)(2,1)S(1)}, bf16[128,2048]{1,0:T(8,128)(2,1)S(1)}, u32[]{:S(2)}, u32[]{:S(2)}) collective-permute-start(bf16[128,2048]{1,0:T(8,128)(2,1)S(1)} %get-tuple-element.522), channel_id=1, source_target_pairs={{2,0},{4,2},{6,4},{7,6},{5,7},{3,5},{1,3},{0,1},{10,8},{12,10},{14... | collective-permute-start | bytes 1572872 | tf_op jit(solution)/shard_map/ppermute | solution.py:75
  227.5 16.0 %collective-permute-start.46 = (bf16[704,384]{1,0:T(8,128)(2,1)S(1)}, bf16[704,384]{1,0:T(8,128)(2,1)S(1)}, u32[]{:S(2)}, u32[]{:S(2)}) collective-permute-start(bf16[704,384]{1,0:T(8,128)(2,1)S(1)} %copy-done.18), channel_id=1, source_target_pairs={{0,16},{8,24},{16,0},{24,8},{1,17},{9,25},{17,1},{25,9},{2,18},{10... | collective-permute-start | bytes 1622024 | tf_op jit(solution)/shard_map/ppermute | solution.py:238
  243.8 13.4 %collective-permute-start.49 = (bf16[704,384]{1,0:T(8,128)(2,1)S(1)}, bf16[704,384]{1,0:T(8,128)(2,1)S(1)}, u32[]{:S(2)}, u32[]{:S(2)}) collective-permute-start(bf16[704,384]{1,0:T(8,128)(2,1)S(1)} %copy-done.19), channel_id=1, source_target_pairs={{0,16},{8,24},{16,0},{24,8},{1,17},{9,25},{17,1},{25,9},{2,18},{10... | collective-permute-start | bytes 1622024 | tf_op jit(solution)/shard_map/ppermute | solution.py:238
  259.1 16.8 %collective-permute-start.50 = (bf16[128,2176]{1,0:T(8,128)(2,1)S(1)}, bf16[128,2176]{1,0:T(8,128)(2,1)S(1)}, u32[]{:S(2)}, u32[]{:S(2)}) collective-permute-start(bf16[128,2176]{1,0:T(8,128)(2,1)S(1)} %get-tuple-element.638.refs_0_), channel_id=1, source_target_pairs={{0,2},{2,4},{4,6},{6,7},{7,5},{5,3},{3,1},{1,0},{8,10},{10,12},{12... | collective-permute-start | bytes 1671176 | tf_op jit(solution)/shard_map/ppermute | solution.py:70
  260.7 15.1 %collective-permute-start.51 = (bf16[128,2176]{1,0:T(8,128)(2,1)S(1)}, bf16[128,2176]{1,0:T(8,128)(2,1)S(1)}, u32[]{:S(2)}, u32[]{:S(2)}) collective-permute-start(bf16[128,2176]{1,0:T(8,128)(2,1)S(1)} %get-tuple-element.638.refs_0_), channel_id=1, source_target_pairs={{2,0},{4,2},{6,4},{7,6},{5,7},{3,5},{1,3},{0,1},{10,8},{12,10},{14... | collective-permute-start | bytes 1671176 | tf_op jit(solution)/shard_map/ppermute | solution.py:75
  287.3 16.5 %collective-permute-start.60 = (bf16[704,1024]{1,0:T(8,128)(2,1)S(1)}, bf16[704,1024]{1,0:T(8,128)(2,1)S(1)}, u32[]{:S(2)}, u32[]{:S(2)}) collective-permute-start(bf16[704,1024]{1,0:T(8,128)(2,1)S(1)} %shard_map.228.own), channel_id=1, source_target_pairs={{0,8},{8,0},{16,24},{24,16},{1,9},{9,1},{17,25},{25,17},{2,10},{10... | collective-permute-start | bytes 4325384 | tf_op jit(solution)/shard_map/ppermute | solution.py:238
  287.4 16.1 %collective-permute-start.57 = (bf16[128,2176]{1,0:T(8,128)(2,1)S(1)}, bf16[128,2176]{1,0:T(8,128)(2,1)S(1)}, u32[]{:S(2)}, u32[]{:S(2)}) collective-permute-start(bf16[128,2176]{1,0:T(8,128)(2,1)S(1)} %collective-permute-done.54.refs_3_), channel_id=1, source_target_pairs={{0,2},{2,4},{4,6},{6,7},{7,5},{5,3},{3,1},{1,0},{8,10},{10,12},{12... | collective-permute-start | bytes 1671176 | tf_op jit(solution)/shard_map/ppermute | solution.py:70
  289.1 14.7 %collective-permute-start.58 = (bf16[128,2176]{1,0:T(8,128)(2,1)S(1)}, bf16[128,2176]{1,0:T(8,128)(2,1)S(1)}, u32[]{:S(2)}, u32[]{:S(2)}) collective-permute-start(bf16[128,2176]{1,0:T(8,128)(2,1)S(1)} %collective-permute-done.55.refs_4_), channel_id=1, source_target_pairs={{2,0},{4,2},{6,4},{7,6},{5,7},{3,5},{1,3},{0,1},{10,8},{12,10},{14... | collective-permute-start | bytes 1671176 | tf_op jit(solution)/shard_map/ppermute | solution.py:75
  289.5 14.1 %collective-permute-start.59 = (bf16[704,384]{1,0:T(8,128)(2,1)S(1)}, bf16[704,384]{1,0:T(8,128)(2,1)S(1)}, u32[]{:S(2)}, u32[]{:S(2)}) collective-permute-start(bf16[704,384]{1,0:T(8,128)(2,1)S(1)} %copy-done.17), channel_id=1, source_target_pairs={{0,16},{8,24},{16,0},{24,8},{1,17},{9,25},{17,1},{25,9},{2,18},{10... | collective-permute-start | bytes 1622024 | tf_op jit(solution)/shard_map/ppermute | solution.py:238
  303.9 15.7 %collective-permute-start.65 = (bf16[704,384]{1,0:T(8,128)(2,1)S(1)}, bf16[704,384]{1,0:T(8,128)(2,1)S(1)}, u32[]{:S(2)}, u32[]{:S(2)}) collective-permute-start(bf16[704,384]{1,0:T(8,128)(2,1)S(1)} %copy-done.12), channel_id=1, source_target_pairs={{0,16},{8,24},{16,0},{24,8},{1,17},{9,25},{17,1},{25,9},{2,18},{10... | collective-permute-start | bytes 1622024 | tf_op jit(solution)/shard_map/ppermute | solution.py:238
  305.4 14.1 %collective-permute-start.61 = (bf16[64,2176]{1,0:T(8,128)(2,1)S(1)}, bf16[64,2176]{1,0:T(8,128)(2,1)S(1)}, u32[]{:S(2)}, u32[]{:S(2)}) collective-permute-start(bf16[64,2176]{1,0:T(8,128)(2,1)S(1)} %slice.45), channel_id=1, source_target_pairs={{0,2},{2,4},{4,6},{6,7},{7,5},{5,3},{3,1},{1,0},{8,10},{10,12},{12... | collective-permute-start | bytes 835592 | tf_op jit(solution)/shard_map/ppermute | solution.py:70
  320.7 19.4 %collective-permute-start.69 = (bf16[704,1024]{1,0:T(8,128)(2,1)S(1)}, bf16[704,1024]{1,0:T(8,128)(2,1)S(1)}, u32[]{:S(2)}, u32[]{:S(2)}) collective-permute-start(bf16[704,1024]{1,0:T(8,128)(2,1)S(1)} %shard_map.229.own), channel_id=1, source_target_pairs={{0,8},{8,0},{16,24},{24,16},{1,9},{9,1},{17,25},{25,17},{2,10},{10... | collective-permute-start | bytes 4325384 | tf_op jit(solution)/shard_map/ppermute | solution.py:238
  320.8 19.3 %collective-permute-start.68 = (bf16[704,512]{1,0:T(8,128)(2,1)}, bf16[704,512]{1,0:T(8,128)(2,1)}, u32[]{:S(2)}, u32[]{:S(2)}) collective-permute-start(bf16[704,512]{1,0:T(8,128)(2,1)} %get-tuple-element.725.refs_2_), channel_id=1, source_target_pairs={{0,16},{8,24},{16,0},{24,8},{1,17},{9,25},{17,1},{25,9},{2,18},{10... | collective-permute-start | bytes 2162696 | tf_op jit(solution)/shard_map/ppermute | solution.py:238
  321.4 18.7 %collective-permute-start.66 = (bf16[128,2048]{1,0:T(8,128)(2,1)}, bf16[128,2048]{1,0:T(8,128)(2,1)}, u32[]{:S(2)}, u32[]{:S(2)}) collective-permute-start(bf16[128,2048]{1,0:T(8,128)(2,1)} %get-tuple-element.634), channel_id=1, source_target_pairs={{0,2},{2,4},{4,6},{6,7},{7,5},{5,3},{3,1},{1,0},{8,10},{10,12},{12... | collective-permute-start | bytes 1572872 | tf_op jit(solution)/shard_map/ppermute | solution.py:70
  322.1 18.0 %collective-permute-start.67 = (bf16[128,2048]{1,0:T(8,128)(2,1)}, bf16[128,2048]{1,0:T(8,128)(2,1)}, u32[]{:S(2)}, u32[]{:S(2)}) collective-permute-start(bf16[128,2048]{1,0:T(8,128)(2,1)} %get-tuple-element.635), channel_id=1, source_target_pairs={{2,0},{4,2},{6,4},{7,6},{5,7},{3,5},{1,3},{0,1},{10,8},{12,10},{14... | collective-permute-start | bytes 1572872 | tf_op jit(solution)/shard_map/ppermute | solution.py:75
  346.8 22.4 %collective-permute-start.70 = (bf16[192,2048]{1,0:T(8,128)(2,1)}, bf16[192,2048]{1,0:T(8,128)(2,1)S(1)}, u32[]{:S(2)}, u32[]{:S(2)}) collective-permute-start(bf16[192,2048]{1,0:T(8,128)(2,1)} %get-tuple-element.683), channel_id=1, source_target_pairs={{0,2},{2,4},{4,6},{6,7},{7,5},{5,3},{3,1},{1,0},{8,10},{10,12},{12... | collective-permute-start | bytes 2359304 | tf_op jit(solution)/shard_map/ppermute | solution.py:70
  347.6 21.6 %collective-permute-start.71 = (bf16[192,2048]{1,0:T(8,128)(2,1)}, bf16[192,2048]{1,0:T(8,128)(2,1)S(1)}, u32[]{:S(2)}, u32[]{:S(2)}) collective-permute-start(bf16[192,2048]{1,0:T(8,128)(2,1)} %get-tuple-element.684), channel_id=1, source_target_pairs={{2,0},{4,2},{6,4},{7,6},{5,7},{3,5},{1,3},{0,1},{10,8},{12,10},{14... | collective-permute-start | bytes 2359304 | tf_op jit(solution)/shard_map/ppermute | solution.py:75
  350.9 18.2 %collective-permute-start.74 = (bf16[256,1024]{1,0:T(8,128)(2,1)S(1)}, bf16[256,1024]{1,0:T(8,128)(2,1)}, u32[]{:S(2)}, u32[]{:S(2)}) collective-permute-start(bf16[256,1024]{1,0:T(8,128)(2,1)S(1)} %shard_map.233.refs_0_), channel_id=1, source_target_pairs={{0,16},{8,24},{16,0},{24,8},{1,17},{9,25},{17,1},{25,9},{2,18},{10... | collective-permute-start | bytes 1572872 | tf_op jit(solution)/shard_map/ppermute | solution.py:238
  352.5 16.7 %collective-permute-start.72 = (bf16[704,128]{1,0:T(8,128)(2,1)S(1)}, bf16[704,128]{1,0:T(8,128)(2,1)}, u32[]{:S(2)}, u32[]{:S(2)}) collective-permute-start(bf16[704,128]{1,0:T(8,128)(2,1)S(1)} %copy-done.58), channel_id=1, source_target_pairs={{0,16},{8,24},{16,0},{24,8},{1,17},{9,25},{17,1},{25,9},{2,18},{10... | collective-permute-start | bytes 540680 | tf_op jit(solution)/shard_map/ppermute | solution.py:238
  370.8 26.1 %collective-permute-start.76 = (bf16[256,2048]{1,0:T(8,128)(2,1)}, bf16[256,2048]{1,0:T(8,128)(2,1)S(1)}, u32[]{:S(2)}, u32[]{:S(2)}) collective-permute-start(bf16[256,2048]{1,0:T(8,128)(2,1)} %get-tuple-element.711), channel_id=1, source_target_pairs={{0,2},{2,4},{4,6},{6,7},{7,5},{5,3},{3,1},{1,0},{8,10},{10,12},{12... | collective-permute-start | bytes 3145736 | tf_op jit(solution)/shard_map/ppermute | solution.py:70
  371.6 25.3 %collective-permute-start.77 = (bf16[256,2048]{1,0:T(8,128)(2,1)}, bf16[256,2048]{1,0:T(8,128)(2,1)S(1)}, u32[]{:S(2)}, u32[]{:S(2)}) collective-permute-start(bf16[256,2048]{1,0:T(8,128)(2,1)} %get-tuple-element.712), channel_id=1, source_target_pairs={{2,0},{4,2},{6,4},{7,6},{5,7},{3,5},{1,3},{0,1},{10,8},{12,10},{14... | collective-permute-start | bytes 3145736 | tf_op jit(solution)/shard_map/ppermute | solution.py:75
  372.8 14.9 %collective-permute-start.78 = (bf16[1024,256]{1,0:T(8,128)(2,1)S(1)}, bf16[1024,256]{1,0:T(8,128)(2,1)S(1)}, u32[]{:S(2)}, u32[]{:S(2)}) collective-permute-start(bf16[1024,256]{1,0:T(8,128)(2,1)S(1)} %copy-done.29), channel_id=1, source_target_pairs={{0,16},{8,24},{16,0},{24,8},{1,17},{9,25},{17,1},{25,9},{2,18},{10... | collective-permute-start | bytes 1572872 | tf_op jit(solution)/shard_map/ppermute | solution.py:238
  374.4 22.6 %collective-permute-start.79 = (bf16[1024,256]{1,0:T(8,128)(2,1)S(1)}, bf16[1024,256]{1,0:T(8,128)(2,1)S(1)}, u32[]{:S(2)}, u32[]{:S(2)}) collective-permute-start(bf16[1024,256]{1,0:T(8,128)(2,1)S(1)} %copy-done.31), channel_id=1, source_target_pairs={{0,16},{8,24},{16,0},{24,8},{1,17},{9,25},{17,1},{25,9},{2,18},{10... | collective-permute-start | bytes 1572872 | tf_op jit(solution)/shard_map/ppermute | solution.py:238
  399.3 16.1 %collective-permute-start.83 = (bf16[704,1024]{1,0:T(8,128)(2,1)S(1)}, bf16[704,1024]{1,0:T(8,128)(2,1)}, u32[]{:S(2)}, u32[]{:S(2)}) collective-permute-start(bf16[704,1024]{1,0:T(8,128)(2,1)S(1)} %shard_map.240.own), channel_id=1, source_target_pairs={{0,8},{8,0},{16,24},{24,16},{1,9},{9,1},{17,25},{25,17},{2,10},{10... | collective-permute-start | bytes 4325384 | tf_op jit(solution)/shard_map/ppermute | solution.py:238
  399.3 14.7 %collective-permute-start.80 = (bf16[128,2048]{1,0:T(8,128)(2,1)}, bf16[128,2048]{1,0:T(8,128)(2,1)}, u32[]{:S(2)}, u32[]{:S(2)}) collective-permute-start(bf16[128,2048]{1,0:T(8,128)(2,1)} %get-tuple-element.738), channel_id=1, source_target_pairs={{0,2},{2,4},{4,6},{6,7},{7,5},{5,3},{3,1},{1,0},{8,10},{10,12},{12... | collective-permute-start | bytes 1572872 | tf_op jit(solution)/shard_map/ppermute | solution.py:70
  400.1 14.3 %collective-permute-start.81 = (bf16[128,2048]{1,0:T(8,128)(2,1)}, bf16[128,2048]{1,0:T(8,128)(2,1)}, u32[]{:S(2)}, u32[]{:S(2)}) collective-permute-start(bf16[128,2048]{1,0:T(8,128)(2,1)} %get-tuple-element.739), channel_id=1, source_target_pairs={{2,0},{4,2},{6,4},{7,6},{5,7},{3,5},{1,3},{0,1},{10,8},{12,10},{14... | collective-permute-start | bytes 1572872 | tf_op jit(solution)/shard_map/ppermute | solution.py:75
  401.4 14.0 %collective-permute-start.82 = (bf16[1024,256]{1,0:T(8,128)(2,1)}, bf16[1024,256]{1,0:T(8,128)(2,1)}, u32[]{:S(2)}, u32[]{:S(2)}) collective-permute-start(bf16[1024,256]{1,0:T(8,128)(2,1)} %get-tuple-element.772.refs_0_), channel_id=1, source_target_pairs={{0,16},{8,24},{16,0},{24,8},{1,17},{9,25},{17,1},{25,9},{2,18},{10... | collective-permute-start | bytes 1572872 | tf_op jit(solution)/shard_map/ppermute | solution.py:238
  416.8 13.8 %collective-permute-start.85 = (bf16[128,2048]{1,0:T(8,128)(2,1)S(1)}, bf16[128,2048]{1,0:T(8,128)(2,1)S(1)}, u32[]{:S(2)}, u32[]{:S(2)}) collective-permute-start(bf16[128,2048]{1,0:T(8,128)(2,1)S(1)} %get-tuple-element.765), channel_id=1, source_target_pairs={{0,2},{2,4},{4,6},{6,7},{7,5},{5,3},{3,1},{1,0},{8,10},{10,12},{12... | collective-permute-start | bytes 1572872 | tf_op jit(solution)/shard_map/ppermute | solution.py:70
  (151 other events, 1654.0 us)
